TPU v7x, 32 devices: a whole 2x2x4 slice. The times are simulated.
32 devices in a mesh: dp: 4 (over z), fsdp: 8 (over y, x, core).
Axes of the slice: x: 2, y: 2, z: 4, core: 2. Of those that a mesh axis runs over, the one named last changes fastest.
Arguments:
- clip_count: int32 [32], P(('dp', 'fsdp')), may hold values from 2 to 4, as said below
- frame_count: int32 [128], P(('dp', 'fsdp')), may hold values from 4 to 8, as said below
- frame_mask: int32 [128, 8], P(('dp', 'fsdp')), may hold values from 0 to 1, as said below
- features: bfloat16 [128, 8, 14, 14, 1024], P(('dp', 'fsdp')), may hold values from -6 to 6
- w_reduce1: bfloat16 [1024, 512], P(('dp', 'fsdp')), may hold values from -0.1875 to 0.1875
- w_spatial1: bfloat16 [9, 262144], P(None, ('dp', 'fsdp')), may hold values from -0.09375 to 0.09375
- w_expand1: bfloat16 [512, 2048], P(('dp', 'fsdp')), may hold values from -0.25 to 0.25
- w_project1: bfloat16 [1024, 2048], P(('dp', 'fsdp')), may hold values from -0.1875 to 0.1875
- w_reduce2: bfloat16 [2048, 512], P(('dp', 'fsdp')), may hold values from -0.125 to 0.125
- w_motion_in: bfloat16 [512, 32], P(('dp', 'fsdp')), may hold values from -0.25 to 0.25
- w_motion_out: bfloat16 [512, 32], P(('dp', 'fsdp')), may hold values from -1 to 1
- w_spatial2: bfloat16 [27, 16384], P(None, ('dp', 'fsdp')), may hold values from -0.1875 to 0.1875
- w_expand2: bfloat16 [512, 2048], P(('dp', 'fsdp')), may hold values from -0.25 to 0.25
- gains: float32 [8608], replicated, may hold values from 0.5 to 1.5
- biases: float32 [8608], replicated, may hold values from -2.5 to 2.5
- motion_taps: float32 [9, 32], replicated, may hold values from -2 to 2
- temporal_taps: float32 [3, 3, 128], replicated, may hold values from -3.5 to 3.5
- cotangent: bfloat16 [128, 8, 7, 7, 2048], P(('dp', 'fsdp')), may hold values from -6 to 6
Outputs:
- output: bfloat16 [128, 8, 7, 7, 2048], P(('dp', 'fsdp'))
- grad_features: bfloat16 [128, 8, 14, 14, 1024], P(('dp', 'fsdp'))
- grad_reduce1: float32 [1024, 512], P(('dp', 'fsdp'))
- grad_spatial1: float32 [9, 262144], P(None, ('dp', 'fsdp'))
- grad_expand1: float32 [512, 2048], P(('dp', 'fsdp'))
- grad_project1: float32 [1024, 2048], P(('dp', 'fsdp'))
- grad_reduce2: float32 [2048, 512], P(('dp', 'fsdp'))
- grad_motion_in: float32 [512, 32], P(('dp', 'fsdp'))
- grad_motion_out: float32 [512, 32], P(('dp', 'fsdp'))
- grad_spatial2: float32 [27, 16384], P(None, ('dp', 'fsdp'))
- grad_expand2: float32 [512, 2048], P(('dp', 'fsdp'))
- grad_gains: float32 [8608], replicated
- grad_biases: float32 [8608], replicated
- grad_motion_taps: float32 [9, 32], replicated
- grad_temporal_taps: float32 [3, 3, 128], replicated
Inputs may be any that keep to these rules, and one draw needn't show every extreme that they name: Each device's live clips are its first clip_count slots; some device has all 4 live and some has the fewest. A clip's frames are its first frame_count slots; some clip has all 8 and some has the fewest. `frame_mask`: the first frame of every clip slot is usable.
All inputs are finite; a program needn't handle non-finite values.
Results may differ from a plain program's by a relative error of at most 0.024.
Values may be sent and summed in bfloat16 or wider, within the bound.
No kernel may reach another device: no remote copies, remote signals or barrier semaphores. Data moves between devices by JAX's collectives and lax.ppermute only.
A program may use at most 384 MiB of HBM per device.

v0:
```python
import jax
import jax.numpy as jnp
from jax import lax
from jax.sharding import PartitionSpec as P

EPSILON = 1e-05
HIGHEST = lax.Precision.HIGHEST
AXES = ("dp", "fsdp")
BF = jnp.bfloat16
F32 = jnp.float32


def earlier(values):
    return jnp.concatenate([jnp.zeros_like(values[..., :1, :]), values[..., :-1, :]], axis=-2)


def later(values):
    return jnp.concatenate([values[..., 1:, :], jnp.zeros_like(values[..., :1, :])], axis=-2)


def taps_of(values, size):
    padded = jnp.pad(values, ((0, 0), (1, 1), (1, 1), (0, 0), (0, 0)))
    return [padded[:, r : r + size, c : c + size] for r in range(3) for c in range(3)]


def dot(left, weight):
    shape = left.shape
    flat = jnp.dot(left.reshape(-1, shape[-1]), weight, preferred_element_type=F32)
    return flat.reshape(shape[:-1] + (weight.shape[1],))


def dot_t(grad, weight):
    shape = grad.shape
    flat = lax.dot_general(
        grad.reshape(-1, shape[-1]), weight, (((1,), (1,)), ((), ())), preferred_element_type=F32
    )
    return flat.reshape(shape[:-1] + (weight.shape[0],))


def weight_grad(left, grad):
    return lax.dot_general(
        left.reshape(-1, left.shape[-1]),
        grad.reshape(-1, grad.shape[-1]),
        (((0,), (0,)), ((), ())),
        preferred_element_type=F32,
    )


def silu_slope(values):
    sig = jax.nn.sigmoid(values)
    return sig * (1.0 + values * (1.0 - sig))


def total_over(values):
    return jnp.sum(values, axis=tuple(range(values.ndim - 1)))


class Sums:
    def __init__(self, dp, fsdp):
        self.devices = dp * fsdp
        half = self.devices // 2
        self.groups = [[2 * i + c for i in range(half)] for c in range(2)]
        self.swap = [(i, i ^ 1) for i in range(self.devices)]

    def flat(self, values):
        size = values.shape[0]
        if size <= 2048:
            copies = jnp.broadcast_to(values[None], (self.devices, size))
            return jnp.sum(lax.all_to_all(copies, AXES, 0, 0), axis=0)
        core = lax.axis_index("fsdp") % 2
        halves = values.reshape(2, size // 2)
        mine = lax.dynamic_index_in_dim(halves, core, 0, False)
        other = lax.dynamic_index_in_dim(halves, 1 - core, 0, False)
        mine = mine + lax.ppermute(other, AXES, self.swap)
        copies = jnp.broadcast_to(mine[None], (self.devices // 2, size // 2))
        mine = jnp.sum(lax.all_to_all(copies, AXES, 0, 0, axis_index_groups=self.groups), axis=0)
        other = lax.ppermute(mine, AXES, self.swap)
        low = jnp.where(core == 0, mine, other)
        high = jnp.where(core == 0, other, mine)
        return jnp.concatenate([low, high])

    def __call__(self, *arrays):
        sizes = [a.size for a in arrays]
        extra = -sum(sizes) % 256
        parts = [a.reshape(-1) for a in arrays]
        if extra:
            parts.append(jnp.zeros((extra,), F32))
        merged = self.flat(jnp.concatenate(parts))
        out, begin = [], 0
        for a, size in zip(arrays, sizes):
            out.append(merged[begin : begin + size].reshape(a.shape))
            begin += size
        return out


def affine(total, square, count, gain, bias):
    mean = total / count
    inv = lax.rsqrt(square / count - mean * mean + EPSILON)
    alpha = gain * inv
    return mean, inv, alpha, bias - mean * alpha


def local(
    dp,
    fsdp,
    clip_count,
    frame_count,
    frame_mask,
    features,
    w_reduce1,
    w_spatial1,
    w_expand1,
    w_project1,
    w_reduce2,
    w_motion_in,
    w_motion_out,
    w_spatial2,
    w_expand2,
    gains,
    biases,
    motion_taps,
    temporal_taps,
    cotangent,
):
    devices = dp * fsdp
    sums = Sums(dp, fsdp)
    slots, frames, height = features.shape[:3]
    half = height // 2
    area = half * half
    c_in = features.shape[-1]
    middle = w_reduce1.shape[1]
    group = middle // 4
    wide = w_expand1.shape[1]
    narrow = w_motion_in.shape[1]
    valid = (
        (jnp.arange(slots)[:, None] < clip_count[0])
        & (jnp.arange(frames)[None, :] < frame_count[:, None])
        & (frame_mask == 1)
    ).astype(F32)
    mask = valid[:, None, None, :, None]
    fmask = valid[:, :, None]
    widths = [middle, middle, wide, wide, middle, narrow, middle, group, group, group, wide]
    starts = [sum(widths[:k]) for k in range(len(widths))]
    gain = [gains[s : s + w] for s, w in zip(starts, widths)]
    bias = [biases[s : s + w] for s, w in zip(starts, widths)]

    feats = features.transpose(0, 2, 3, 1, 4)
    cot = cotangent.transpose(0, 2, 3, 1, 4)

    def gather(value):
        return lax.all_gather(value, AXES, axis=0, tiled=False)

    own = middle // devices
    full_reduce1 = gather(w_reduce1).reshape(c_in, middle)
    full_spatial1 = (
        gather(w_spatial1.reshape(9, own, middle)).transpose(1, 0, 2, 3).reshape(9, middle, middle)
    )
    pack_wide = gather(jnp.concatenate([w_expand1, w_project1, w_expand2], axis=0))
    rows1, rowsp = w_expand1.shape[0], w_project1.shape[0]
    full_expand1 = pack_wide[:, :rows1].reshape(middle, wide)
    full_project1 = pack_wide[:, rows1 : rows1 + rowsp].reshape(c_in, wide)
    full_expand2 = pack_wide[:, rows1 + rowsp :].reshape(middle, wide)
    rows2 = w_reduce2.shape[0]
    def rows_of(value):
        return jnp.pad(value, ((0, 0), (0, -value.shape[1] % middle))).reshape(
            value.shape[0], -1, middle
        )

    smalls = jnp.concatenate(
        [w_spatial2.reshape(1, -1), w_motion_in.reshape(1, -1), w_motion_out.reshape(1, -1)], axis=1
    )
    pack_mid = gather(jnp.concatenate([w_reduce2, rows_of(smalls)[0]], axis=0))
    full_reduce2 = pack_mid[:, :rows2].reshape(wide, middle)
    flat_small = pack_mid[:, rows2:].reshape(devices, -1)
    size_s, size_m = w_spatial2.size, w_motion_in.size
    kernels = (
        flat_small[:, :size_s].reshape(devices, 27, -1).swapaxes(0, 1).reshape(3, 9, group, group)
    )
    small = flat_small[:, size_s : size_s + 2 * size_m].reshape(devices, 2, own, narrow)
    full_motion_in = small[:, 0].reshape(middle, narrow)
    full_motion_out = small[:, 1].reshape(middle, narrow).astype(F32)

    raw_a = dot(feats, full_reduce1)
    sum_a, square_a, frame_total, pairs = sums(
        total_over(raw_a * mask),
        total_over(raw_a * raw_a * mask),
        jnp.sum(valid),
        jnp.sum(valid[:, :-1] * valid[:, 1:]),
    )
    count_big = frame_total * (height * height)
    count = frame_total * area
    mean_a, inv_a, alpha_a, beta_a = affine(sum_a, square_a, count_big, gain[0], bias[0])
    act_a = (jax.nn.silu(raw_a * alpha_a + beta_a) * mask).astype(BF)
    padded_a = jnp.pad(act_a, ((0, 0), (1, 1), (1, 1), (0, 0), (0, 0)))
    split_a = padded_a.reshape(slots, half + 1, 2, half + 1, 2, frames, middle)
    cols_b = jnp.concatenate(
        [
            split_a[:, r // 2 : r // 2 + half, r % 2, c // 2 : c // 2 + half, c % 2]
            for r in range(3)
            for c in range(3)
        ],
        axis=-1,
    )
    raw_b = dot(cols_b, full_spatial1.reshape(9 * middle, middle))
    sampled = feats.reshape(slots, half, 2, half, 2, frames, c_in)[:, :, 0, :, 0]
    raw_p = dot(sampled, full_project1)

    def moments(raw):
        return total_over(raw * mask), total_over(raw * raw * mask)

    sum_b, square_b = sums(*moments(raw_b))
    mean_b, inv_b, alpha_b, beta_b = affine(sum_b, square_b, count, gain[1], bias[1])
    act_b = (jax.nn.silu(raw_b * alpha_b + beta_b) * mask).astype(BF)
    raw_c = dot(act_b, full_expand1)
    sum_c, square_c, sum_p, square_p = sums(*moments(raw_c), *moments(raw_p))
    mean_c, inv_c, alpha_c, beta_c = affine(sum_c, square_c, count, gain[2], bias[2])
    mean_p, inv_p, alpha_p, beta_p = affine(sum_p, square_p, count, gain[3], bias[3])
    sum_one = raw_c * alpha_c + beta_c + (raw_p * alpha_p + beta_p)
    block_one = (jax.nn.silu(sum_one) * mask).astype(BF)

    raw_d = dot(block_one, full_reduce2)
    sum_d, square_d = sums(*moments(raw_d))
    mean_d, inv_d, alpha_d, beta_d = affine(sum_d, square_d, count, gain[4], bias[4])
    norm_d = raw_d * alpha_d + beta_d
    act_d = (jax.nn.silu(norm_d) * mask).astype(BF)
    raw_m = dot(act_d, full_motion_in)

    spot = jnp.arange(half)
    reach = [(spot - k + 1 >= 0) & (spot - k + 1 < half) for k in range(3)]
    windows = jnp.stack(
        [(reach[r][:, None] & reach[c][None, :]) for r in range(3) for c in range(3)], axis=-1
    ).astype(F32)
    kmap = jnp.sum(windows[..., None] * motion_taps, axis=2)
    ksum = jnp.sum(kmap, axis=(0, 1))
    in_window = jnp.stack(
        [jnp.sum(raw_m * windows[None, :, :, k, None, None], axis=(1, 2)) for k in range(9)]
    )
    mapped = jnp.sum(in_window * motion_taps[:, None, None, :], axis=0)
    plain = jnp.sum(raw_m, axis=(1, 2))
    vnext = later(fmask)
    pool_raw = (vnext / area) * (later(mapped * fmask) - fmask * plain)
    pool_one = (vnext / area) * (later(fmask) * ksum - fmask * area)
    flat_raw = pool_raw.reshape(-1, narrow)
    flat_valid = valid.reshape(-1, 1)
    gram = lax.dot_general(
        flat_raw * flat_valid, flat_raw, (((0,), (0,)), ((), ())), precision=HIGHEST
    )
    sum_m, square_m, pool_a, gram_aa = sums(
        *moments(raw_m), jnp.sum(flat_raw * flat_valid, axis=0), gram
    )
    mean_m, inv_m, alpha_m, beta_m = affine(sum_m, square_m, count, gain[5], bias[5])
    step = ksum / area - 1.0
    pool_b = pairs * step
    gram_ab = pool_a[:, None] * step[None, :]
    gram_bb = pairs * step[:, None] * step[None, :]
    pooled = alpha_m * pool_raw + beta_m * pool_one
    lifted = jnp.einsum("cfr,or->cfo", pooled, full_motion_out, precision=HIGHEST)
    gram_p = (
        alpha_m[:, None] * alpha_m * gram_aa
        + alpha_m[:, None] * beta_m * gram_ab
        + beta_m[:, None] * alpha_m * gram_ab.T
        + beta_m[:, None] * beta_m * gram_bb
    )
    sum_x = jnp.dot(full_motion_out, alpha_m * pool_a + beta_m * pool_b, precision=HIGHEST)
    square_x = jnp.sum(jnp.dot(full_motion_out, gram_p, precision=HIGHEST) * full_motion_out, axis=1)
    mean_x, inv_x, alpha_x, beta_x = affine(sum_x, square_x, frame_total, gain[6], bias[6])
    sigma = jax.nn.sigmoid(lifted * alpha_x + beta_x)
    attend1 = 2.0 * sigma
    attend_px = attend1[:, None, None, :, :]
    excited = (act_d.astype(F32) * attend_px).astype(BF)

    pieces, cols_g, raws, stats = [], [], [], []
    outputs = [excited[..., :group]]
    previous = None
    for k in range(3):
        piece = excited[..., (k + 1) * group : (k + 2) * group].astype(F32)
        if previous is not None:
            piece = piece + previous.astype(F32)
        taps = temporal_taps[k]
        shifted = (taps[0] * earlier(piece) + taps[1] * piece + taps[2] * later(piece)).astype(BF)
        cols = jnp.concatenate(taps_of(shifted, half), axis=-1)
        raw = dot(cols, kernels[k].reshape(9 * group, group))
        stat = affine(*sums(*moments(raw)), count, gain[7 + k], bias[7 + k])
        previous = (jax.nn.silu(raw * stat[2] + stat[3]) * mask).astype(BF)
        pieces.append(piece)
        cols_g.append(cols)
        raws.append(raw)
        stats.append(stat)
        outputs.append(previous)
    joined = jnp.concatenate(outputs, axis=-1)
    raw_e = dot(joined, full_expand2)
    mean_e, inv_e, alpha_e, beta_e = affine(*sums(*moments(raw_e)), count, gain[10], bias[10])
    total_two = raw_e * alpha_e + beta_e + block_one.astype(F32)
    result = (jax.nn.silu(total_two) * mask).astype(BF)

    shifts = [None] * 11
    spreads = [None] * 11

    def grad_raw(index, grad, raw, mean, inv, weight, number):
        unit = (raw - mean) * inv
        return gain[index] * inv * (grad - weight * (shifts[index] + unit * spreads[index]) / number)

    grad_total = cot.astype(F32) * mask * silu_slope(total_two)
    shifts[10], spreads[10] = sums(
        total_over(grad_total), total_over(grad_total * ((raw_e - mean_e) * inv_e))
    )
    final_grad = grad_raw(10, grad_total, raw_e, mean_e, inv_e, mask, count).astype(BF)
    grad_expand2 = weight_grad(joined, final_grad)
    grad_joined = dot_t(final_grad, full_expand2)
    grad_groups = [grad_joined[..., :group], None, None, None]
    kernel_grads = [None] * 3
    temporal_grads = [None] * 3
    incoming = None
    for k in (2, 1, 0):
        grad_out = grad_joined[..., (k + 1) * group : (k + 2) * group]
        if incoming is not None:
            grad_out = grad_out + incoming
        mean, inv, alpha, beta = stats[k]
        grad_pre = grad_out * mask * silu_slope(raws[k] * alpha + beta)
        shifts[7 + k], spreads[7 + k] = sums(
            total_over(grad_pre), total_over(grad_pre * ((raws[k] - mean) * inv))
        )
        group_grad = grad_raw(7 + k, grad_pre, raws[k], mean, inv, mask, count).astype(BF)
        kernel_grads[k] = weight_grad(cols_g[k], group_grad)
        back = jnp.concatenate(taps_of(group_grad, half), axis=-1)
        flipped = kernels[k][::-1].transpose(0, 2, 1).reshape(9 * group, group)
        grad_shifted = dot(back, flipped)
        taps = temporal_taps[k]
        piece = pieces[k]
        incoming = (
            taps[0] * later(grad_shifted) + taps[1] * grad_shifted + taps[2] * earlier(grad_shifted)
        )
        temporal_grads[k] = jnp.stack(
            [
                total_over(grad_shifted * earlier(piece)),
                total_over(grad_shifted * piece),
                total_over(grad_shifted * later(piece)),
            ]
        )
        grad_groups[k + 1] = incoming
    grad_excited = jnp.concatenate(grad_groups, axis=-1)
    grad_attend = jnp.sum(grad_excited * act_d.astype(F32), axis=(1, 2))
    grad_x = grad_attend * 2.0 * sigma * (1.0 - sigma)
    unit_x = (lifted - mean_x) * inv_x
    pool_unit = (pool_raw - mean_m * pool_one) * inv_m
    grad_e = jnp.einsum("cfo,or->cfr", grad_x, full_motion_out * alpha_x[:, None], precision=HIGHEST)
    shifts[6], spreads[6], first_t, second_t = sums(
        jnp.sum(grad_x, axis=(0, 1)),
        jnp.sum(grad_x * unit_x, axis=(0, 1)),
        jnp.sum(grad_e * pool_one, axis=(0, 1)),
        jnp.sum(grad_e * pool_unit, axis=(0, 1)),
    )
    lift_b = jnp.dot(
        full_motion_out, alpha_m[:, None] * gram_ab + beta_m[:, None] * gram_bb, precision=HIGHEST
    )
    lift_a = jnp.dot(
        full_motion_out, alpha_m[:, None] * gram_aa + beta_m[:, None] * gram_ab.T, precision=HIGHEST
    )
    unit_b = inv_x[:, None] * (lift_b - mean_x[:, None] * pool_b)
    unit_a = inv_x[:, None] * (lift_a - mean_x[:, None] * pool_a)
    unit_u = (unit_a - unit_b * mean_m) * inv_m
    pool_u = (pool_a - pool_b * mean_m) * inv_m
    back_x = full_motion_out * alpha_x[:, None]
    shifts[5] = first_t - jnp.sum(
        back_x * (shifts[6][:, None] * pool_b + spreads[6][:, None] * unit_b), axis=0
    ) / frame_total
    spreads[5] = second_t - jnp.sum(
        back_x * (shifts[6][:, None] * pool_u + spreads[6][:, None] * unit_u), axis=0
    ) / frame_total
    grad_lifted = alpha_x * (grad_x - fmask * (shifts[6] + unit_x * spreads[6]) / frame_total)
    grad_motion_out = jnp.einsum("cfo,cfr->or", grad_lifted, pooled, precision=HIGHEST)
    grad_pooled = jnp.einsum("cfo,or->cfr", grad_lifted, full_motion_out, precision=HIGHEST)
    grad_change = grad_pooled * vnext / area
    reduced_windows = later(
        fmask * (alpha_m * in_window + beta_m * jnp.sum(windows, axis=(0, 1))[:, None, None, None])
    )
    motion_tap_grad = jnp.sum(grad_change * reduced_windows, axis=(1, 2))
    grad_motion = (
        kmap[None, :, :, None, :] * earlier(grad_change)[:, None, None]
        - grad_change[:, None, None]
    ) * mask
    motion_grad = grad_raw(5, grad_motion, raw_m, mean_m, inv_m, mask, count).astype(BF)
    grad_motion_in = weight_grad(act_d, motion_grad)
    grad_act = grad_excited * attend_px + dot_t(motion_grad, full_motion_in)
    grad_narrow = grad_act * mask * silu_slope(norm_d)
    shifts[4], spreads[4] = sums(
        total_over(grad_narrow), total_over(grad_narrow * ((raw_d - mean_d) * inv_d))
    )
    narrow_grad = grad_raw(4, grad_narrow, raw_d, mean_d, inv_d, mask, count).astype(BF)
    grad_reduce2 = weight_grad(block_one, narrow_grad)
    grad_block = grad_total + dot_t(narrow_grad, full_reduce2)

    def by_owner(values):
        return values.astype(BF).reshape((dp, fsdp) + values.shape[1:]).swapaxes(0, 1)

    def scatter(*arrays):
        merged = jnp.concatenate([by_owner(a) for a in arrays], axis=2)
        merged = lax.psum_scatter(merged, "fsdp", scatter_dimension=0, tiled=False)
        merged = lax.psum_scatter(merged, "dp", scatter_dimension=0, tiled=False)
        out, begin = [], 0
        for a in arrays:
            out.append(merged[begin : begin + a.shape[1]].astype(F32))
            begin += a.shape[1]
        return out

    grad_kernels = jnp.stack(kernel_grads).reshape(27, devices, -1).swapaxes(0, 1)
    small_grads = jnp.concatenate(
        [
            grad_kernels.reshape(devices, -1),
            grad_motion_in.reshape(devices, -1),
            grad_motion_out.reshape(devices, -1),
        ],
        axis=1,
    )
    own_reduce2, own_expand2, own_small = scatter(
        grad_reduce2.reshape(devices, -1, middle),
        grad_expand2.reshape(devices, -1, middle),
        rows_of(small_grads),
    )
    own_small = own_small.reshape(-1)
    own_kernels = own_small[:size_s]
    own_motion = own_small[size_s : size_s + 2 * size_m].reshape(2, own, narrow)

    grad_one = grad_block * mask * silu_slope(sum_one)
    shifts[2], spreads[2], spreads[3] = sums(
        total_over(grad_one),
        total_over(grad_one * ((raw_c - mean_c) * inv_c)),
        total_over(grad_one * ((raw_p - mean_p) * inv_p)),
    )
    shifts[3] = shifts[2]
    widen_grad = grad_raw(2, grad_one, raw_c, mean_c, inv_c, mask, count).astype(BF)
    shortcut_grad = grad_raw(3, grad_one, raw_p, mean_p, inv_p, mask, count).astype(BF)
    grad_act_b = dot_t(widen_grad, full_expand1)
    grad_expand1 = weight_grad(act_b, widen_grad)
    grad_project1 = weight_grad(sampled, shortcut_grad)
    own_expand1, own_project1 = scatter(
        grad_expand1.reshape(devices, -1, wide), grad_project1.reshape(devices, -1, wide)
    )
    grad_sampled = dot_t(shortcut_grad, full_project1)
    grad_strided = grad_act_b * mask * silu_slope(raw_b * alpha_b + beta_b)
    shifts[1], spreads[1] = sums(
        total_over(grad_strided), total_over(grad_strided * ((raw_b - mean_b) * inv_b))
    )
    strided_grad = grad_raw(1, grad_strided, raw_b, mean_b, inv_b, mask, count).astype(BF)
    grad_spatial1 = weight_grad(cols_b, strided_grad)
    (own_spatial1,) = scatter(
        grad_spatial1.reshape(9, devices, own, middle)
        .swapaxes(0, 1)
        .reshape(devices, 9 * own, middle)
    )
    beyond = jnp.pad(strided_grad, ((0, 0), (0, 1), (0, 1), (0, 0), (0, 0)))
    here = beyond[:, :half, :half]
    right = beyond[:, :half, 1:]
    below = beyond[:, 1:, :half]
    both = beyond[:, 1:, 1:]

    def back_taps(*pairs_of):
        left = jnp.concatenate([p[0] for p in pairs_of], axis=-1)
        weight = jnp.concatenate([full_spatial1[p[1]] for p in pairs_of], axis=1)
        return dot_t(left, weight)

    even_even = back_taps((here, 4))
    even_odd = back_taps((here, 5), (right, 3))
    odd_even = back_taps((here, 7), (below, 1))
    odd_odd = back_taps((here, 8), (right, 6), (below, 2), (both, 0))
    grad_act_a = jnp.stack(
        [jnp.stack([even_even, even_odd], axis=3), jnp.stack([odd_even, odd_odd], axis=3)], axis=2
    ).reshape(slots, height, height, frames, middle)
    grad_first = grad_act_a * mask * silu_slope(raw_a * alpha_a + beta_a)
    shifts[0], spreads[0], motion_total, temporal_total = sums(
        total_over(grad_first),
        total_over(grad_first * ((raw_a - mean_a) * inv_a)),
        motion_tap_grad,
        jnp.stack(temporal_grads),
    )
    first_grad = grad_raw(0, grad_first, raw_a, mean_a, inv_a, mask, count_big).astype(BF)
    grad_reduce1 = weight_grad(feats, first_grad)
    (own_reduce1,) = scatter(grad_reduce1.reshape(devices, -1, middle))
    grad_inputs = dot_t(first_grad, full_reduce1)
    spread_sampled = jnp.pad(
        grad_sampled[:, :, None, :, None], ((0, 0), (0, 0), (0, 1), (0, 0), (0, 1), (0, 0), (0, 0))
    ).reshape(grad_inputs.shape)
    grad_features = (grad_inputs + spread_sampled).astype(BF)
    return (
        result.transpose(0, 3, 1, 2, 4),
        grad_features.transpose(0, 3, 1, 2, 4),
        own_reduce1,
        own_spatial1.reshape(9, own * middle),
        own_expand1,
        own_project1,
        own_reduce2,
        own_motion[0],
        own_motion[1],
        own_kernels.reshape(27, -1),
        own_expand2.reshape(-1, wide),
        jnp.concatenate(spreads),
        jnp.concatenate(shifts),
        motion_total,
        temporal_total,
    )


def solution(mesh):
    dp, fsdp = mesh.shape["dp"], mesh.shape["fsdp"]

    def run(*arrays):
        return local(dp, fsdp, *arrays)

    rows = P(AXES, None)
    columns = P(None, AXES)
    clips = P(AXES, None, None, None, None)
    return jax.shard_map(
        run,
        mesh=mesh,
        in_specs=(
            P(AXES),
            P(AXES),
            rows,
            clips,
            rows,
            columns,
            rows,
            rows,
            rows,
            rows,
            rows,
            columns,
            rows,
            P(),
            P(),
            P(),
            P(),
            clips,
        ),
        out_specs=(
            clips,
            clips,
            rows,
            columns,
            rows,
            rows,
            rows,
            rows,
            rows,
            columns,
            rows,
            P(),
            P(),
            P(),
            P(),
        ),
        check_vma=False,
    )
```

profile of v0, /device:TPU:0, one launch (start us, length us, event | category | flops | bytes accessed | tf_op | source)
XLA Modules:
  0.0 1173.8 jit_solution(9355234129210168834)
XLA Ops:
  19.8 47.4 %all-gather.11.cloned.1.call-done = bf16[1024,512]{1,0:T(8,128)(2,1)} async-done(((bf16[32,512]{1,0:T(8,128)(2,1)}), bf16[1024,512]{1,0:T(8,128)(2,1)}) %all-gather.11.cloned.1.call-update) | async-done | bytes 1048592 | tf_op jit(solution)/shard_map/all_gather | solution.py:151
  67.3 13.9 %multiply_reduce_fusion.8 = (f32[512]{0:T(512)S(1)}, f32[512]{0:T(512)S(1)}, f32[4,14,14,8,512]{4,3,2,1,0:T(8,128)}) fusion(f32[4,8]{1,0:T(4,128)S(1)} %get-tuple-element.313, bf16[1024,512]{1,0:T(8,128)(2,1)} %all-gather.11.cloned.1.call-done, bf16[4,8,14,14,1024]{4,1,3,2,0:T(8,128)(2,1)} %param.21), kind=kOutput, calls=%fused_computation.40 | convolution fusion | flops 6592723968 | bytes 26742912 | tf_op jit(solution)/shard_map/dot_general | solution.py:28
  87.1 8.4 all-to-all-done
  98.1 6.9 multiply_convert_fusion.6
  105.0 4.3 pad.47
  127.1 6.6 all-gather.9.cloned.1.call-done
  133.7 12.4 %multiply_reduce_fusion.15 = (f32[512]{0:T(512)S(1)}, f32[512]{0:T(512)S(1)}, f32[4,7,7,8,512]{4,3,2,1,0:T(8,128)S(1)}) fusion(f32[4,8]{1,0:T(4,128)S(1)} %get-tuple-element.313, bf16[4,7,7,8,4608]{4,3,2,1,0:T(8,128)(2,1)} %bitcast_dynamic-update-slice_fusion, bf16[4608,512,1,1,1]{1,0,4,3,2:T(8,128)(2,1)} %bitcast.579), kind=kOutput, calls=%fused_computation.87 | convolution fusion | flops 7402765312 | bytes 22384768 | tf_op jit(solution)/shard_map/dot_general | solution.py:28
  154.9 4.8 all-to-all-done.1
  163.3 50.9 %all-gather.13.cloned.1.call-done = bf16[2048,2048]{1,0:T(8,128)(2,1)} async-done(((bf16[64,2048]{1,0:T(8,128)(2,1)}), bf16[2048,2048]{1,0:T(8,128)(2,1)}) %all-gather.13.cloned.1.call-update) | async-done | bytes 8388624 | tf_op jit(solution)/shard_map/all_gather | solution.py:151
  221.3 6.9 multiply_reduce_fusion.7
  228.3 11.0 fusion.1
  241.5 4.6 all-to-all-start.2
  248.0 9.8 all-to-all-done.2
  258.6 17.7 %all-gather.15.cloned.1.call-done = bf16[32,93,512]{2,1,0:T(8,128)(2,1)} async-done(((bf16[1,93,512]{2,1,0:T(8,128)(2,1)}), bf16[32,93,512]{2,1,0:T(8,128)(2,1)}) %all-gather.15.cloned.1.call-update) | async-done | bytes 3047440 | tf_op jit(solution)/shard_map/all_gather | solution.py:151
  279.7 10.3 multiply_convert_fusion.5
  298.1 10.8 fusion.216
  322.1 6.1 all-to-all-start.4
  357.4 5.9 all-to-all-start.5
  380.9 5.4 all-to-all-start.6
  403.9 5.2 all-to-all-start.7
  411.9 4.5 all-to-all-done.7
  419.2 9.0 multiply_reduce_fusion.5
  431.9 4.2 all-to-all-start.8
  438.8 5.5 all-to-all-done.8
  449.0 18.8 %fusion.203 = (f32[2048]{0:T(1024)S(1)}, f32[2048]{0:T(1024)S(1)}, f32[4,7,7,8,2048]{4,3,2,1,0:T(8,128)}, bf16[4,8,7,7,2048]{4,1,3,2,0:T(8,128)(2,1)}) fusion(f32[2048]{0:T(1024)S(1)} %get-tuple-element.148, f32[4,7,7,8,2048]{4,3,2,1,0:T(8,128)} %get-tuple-element.325, f32[2048]{0:T(1024)S(1)} %get-tuple-element.149, ...), kind=kLoop, calls=%fused_computation.601 | loop fusion | flops 70643712 | bytes 45006976 | tf_op jit(solution)/shard_map/reduce_sum | solution.py:55
  471.8 4.6 all-to-all-start.9
  479.1 19.2 %copy.304 = bf16[4608,1568]{1,0:T(8,128)(2,1)} copy(bf16[4608,1568]{0,1:T(8,128)(2,1)} %bitcast.556) | data formatting | bytes 28901376 | tf_op jit(solution)/shard_map/dot_general | solution.py:41
  516.2 9.9 multiply_convert_fusion.3
  532.5 6.1 all-to-all-start.10
  538.5 4.5 fusion.218
  543.1 9.6 copy.309
  560.7 6.0 all-to-all-start.11
  567.4 6.6 all-to-all-done.11
  587.1 5.9 all-to-all-done.12
  609.0 8.8 bitcast_convert_fusion
  617.8 4.4 convert_element_type.265
  631.2 6.3 fusion.205
  638.2 6.3 all-to-all-start.14
  644.6 4.3 fusion.26
  657.2 24.9 %fusion.202 = (f32[2048]{0:T(1024)S(1)}, f32[2048]{0:T(1024)S(1)}, f32[2048]{0:T(1024)S(1)}, f32[4,7,7,8,2048]{4,3,2,1,0:T(8,128)}) fusion(f32[2048]{0:T(1024)S(1)} %copy-done.104, f32[4,7,7,8,2048]{4,3,2,1,0:T(8,128)} %bitcast.552, f32[2048]{0:T(1024)S(1)} %copy-done.105, f32[2048]{0:T(1024)S(1)} %copy-done.102, ...), kind=kOutput, calls=%fused_computation.600 | convolution fusion | flops 3365398528 | bytes 55173248 | tf_op jit(solution)/shard_map/dot_general | solution.py:34
  694.3 5.1 all-to-all-done.15
  700.9 17.7 %multiply_convert_fusion.2 = (bf16[4,7,7,8,2048]{4,3,2,1,0:T(8,128)(2,1)S(1)}, bf16[4,7,7,8,2048]{4,3,2,1,0:T(8,128)(2,1)}) fusion(f32[4,7,7,8,2048]{4,3,2,1,0:T(8,128)} %get-tuple-element.329, f32[4,7,7,8,2048]{4,3,2,1,0:T(8,128)} %get-tuple-element.317, f32[2048]{0:T(1024)S(1)} %get-tuple-element.276, f32[2048]{0:T(1024)S(1)} %get-tuple-element.277, ...), kind=kLoop, calls=%fused_computation.18 | loop fusion | flops 57802752 | bytes 51454084 | tf_op jit(solution)/shard_map/convert_element_type | solution.py:431
  718.7 6.8 fusion.204
  731.1 6.1 all-to-all-done.16
  757.7 11.9 %pad_maximum_fusion = f32[4,7,2,7,2,8,512]{6,5,3,1,0,4,2:T(8,128)} fusion(f32[4,7,1,7,2,8,512]{6,5,3,1,0,4,2:T(8,128)} %maximum_bitcast_fusion.1, f32[4,7,1,7,2,8,512]{6,5,3,1,0,4,2:T(8,128)} %maximum_bitcast_fusion), kind=kLoop, calls=%fused_computation.2 | loop fusion | flops 3211264 | bytes 25690112 | tf_op jit(solution)/shard_map/stack | solution.py:466
  769.6 11.6 copy.300
  781.3 11.5 multiply_reduce_fusion
  801.6 5.3 all-to-all-done.17
  807.1 13.6 %convert_bitcast_fusion = bf16[32,9,16,512]{3,2,0,1:T(8,128)(2,1)} fusion(bf16[9,32,16,1568]{3,2,1,0:T(8,128)(2,1)} %bitcast.558, bf16[1568,512,1,1]{1,0,3,2:T(8,128)(2,1)S(1)} %bitcast.559), kind=kOutput, calls=%fused_computation.55 | convolution fusion | flops 7401111552 | bytes 20774912 | tf_op jit(solution)/shard_map/dot_general | solution.py:41
  820.7 5.0 copy.305
  826.6 9.9 multiply_convert_fusion.1
  836.5 12.1 %fusion.42 = bf16[1024,512]{0,1:T(8,128)(2,1)S(1)} fusion(bf16[4,14,14,8,512]{4,3,2,1,0:T(8,128)(2,1)} %multiply_convert_fusion.1, bf16[4,8,14,14,1024]{4,1,3,2,0:T(8,128)(2,1)} %param.21), kind=kOutput, calls=%fused_computation.128 | convolution fusion | flops 6577192960 | bytes 20316160 | tf_op jit(solution)/shard_map/dot_general | solution.py:41
  851.4 8.4 convolution_convert_fusion.2
  867.1 11.1 convolution_convert_fusion
  878.5 7.1 convolution_convert_fusion.1
  890.4 55.4 %all-reduce.30.cloned.1.call-done = (bf16[8,4,144,512]{3,2,0,1:T(8,128)(2,1)}, bf16[8,4,32,512]{3,2,0,1:T(8,128)(2,1)}) async-done(((bf16[8,4,144,512]{3,2,0,1:T(8,128)(2,1)}, bf16[8,4,32,512]{3,2,0,1:T(8,128)(2,1)}), (bf16[8,4,144,512]{3,2,0,1:T(8,128)(2,1)}, bf16[8,4,32,512]{3,2,0,1:T(8,128)(2,1)})) %all-reduce.30.cloned.1.call-update) | async-done | bytes 5767184
  950.8 55.3 %reduce-scatter.21.cloned.1.call-done = bf16[1,4,157,512]{3,2,1,0:T(8,128)(2,1)} async-done(((bf16[8,4,157,512]{3,2,1,0:T(8,128)(2,1)}), bf16[1,4,157,512]{3,2,1,0:T(8,128)(2,1)}) %reduce-scatter.21.cloned.1.call-update) | async-done | bytes 643088 | tf_op jit(solution)/shard_map/reduce_scatter | solution.py:398
  1006.2 10.5 convolution_bitcast_fusion
  1016.7 10.9 pad.55.clone
  1027.6 44.2 %reduce-scatter.17.cloned.1.call-done = bf16[1,4,48,2048]{3,2,1,0:T(8,128)(2,1)} async-done(((bf16[8,4,48,2048]{3,2,1,0:T(8,128)(2,1)}), bf16[1,4,48,2048]{3,2,1,0:T(8,128)(2,1)}) %reduce-scatter.17.cloned.1.call-update) | async-done | bytes 786448 | tf_op jit(solution)/shard_map/reduce_scatter | solution.py:398
  1072.1 17.1 %fusion = bf16[4,8,14,14,1024]{4,1,3,2,0:T(8,128)(2,1)} fusion(f32[4,14,14,8,1024]{4,3,2,1,0:T(8,128)} %bitcast.554, bf16[4,14,14,8,512]{4,3,2,1,0:T(8,128)(2,1)} %multiply_convert_fusion.1, bf16[1024,512]{1,0:T(8,128)(2,1)S(1)} %copy-done.254), kind=kOutput, calls=%fused_computation.1 | convolution fusion | flops 6589513728 | bytes 46006272 | tf_op jit(solution)/shard_map/dot_general | solution.py:34
  1095.4 21.2 %reduce-scatter.15.cloned.1.call-done = bf16[1,144,512]{2,1,0:T(8,128)(2,1)} async-done(((bf16[4,144,512]{2,1,0:T(8,128)(2,1)}), bf16[1,144,512]{2,1,0:T(8,128)(2,1)}) %reduce-scatter.15.cloned.1.call-update) | async-done | bytes 147472 | tf_op jit(solution)/shard_map/reduce_scatter | solution.py:399
  1118.3 20.8 %reduce-scatter.23.cloned.1.call-done = bf16[1,157,512]{2,1,0:T(8,128)(2,1)} async-done(((bf16[4,157,512]{2,1,0:T(8,128)(2,1)}), bf16[1,157,512]{2,1,0:T(8,128)(2,1)}) %reduce-scatter.23.cloned.1.call-update) | async-done | bytes 160784 | tf_op jit(solution)/shard_map/reduce_scatter | solution.py:399
  1144.2 19.5 %reduce-scatter.19.cloned.1.call-done = bf16[1,48,2048]{2,1,0:T(8,128)(2,1)} async-done(((bf16[4,48,2048]{2,1,0:T(8,128)(2,1)}), bf16[1,48,2048]{2,1,0:T(8,128)(2,1)}) %reduce-scatter.19.cloned.1.call-update) | async-done | bytes 196624 | tf_op jit(solution)/shard_map/reduce_scatter | solution.py:399
  (945 shorter events, 336.6 us)
Async XLA Ops:
  7.2 60.1 %all-gather.11.cloned.1.call-start = ((), (), s32[]{:S(2)}) async-start(), calls=%async_computation.31 | async-start | bytes 1081344 | tf_op jit(solution)/shard_map/all_gather | solution.py:151
  7.9 125.8 %all-gather.9.cloned.1.call-start = ((), (), s32[]{:S(2)}) async-start(), calls=%async_computation.24 | async-start | bytes 4866048 | tf_op jit(solution)/shard_map/all_gather | solution.py:151
  9.7 204.4 %all-gather.13.cloned.1.call-start = ((), (), s32[]{:S(2)}) async-start(), calls=%async_computation.32 | async-start | bytes 8650752 | tf_op jit(solution)/shard_map/all_gather | solution.py:151
  11.4 264.9 %all-gather.15.cloned.1.call-start = ((), (), s32[]{:S(2)}) async-start(), calls=%async_computation.33 | async-start | bytes 3244032 | tf_op jit(solution)/shard_map/all_gather | solution.py:151
  83.3 12.1 %all-to-all-start = ((f32[32,1,1280]{2,1,0:T(1,128)}), f32[32,1,1280]{2,1,0:T(1,128)S(1)}, u32[]{:S(2)}, u32[]{:S(2)}) async-start(f32[32,1,1280]{2,1,0:T(1,128)} %broadcast_in_dim.47), calls=%async_computation | async-start | bytes 327680 | tf_op jit(solution)/shard_map/all_to_all | solution.py:69
  146.9 12.8 %all-to-all-start.1 = ((f32[32,1,1024]{2,1,0:T(1,128)}), f32[32,1,1024]{2,1,0:T(1,128)S(1)}, u32[]{:S(2)}, u32[]{:S(2)}) async-start(f32[32,1,1024]{2,1,0:T(1,128)} %broadcast_in_dim.48), calls=%async_computation.1 | async-start | bytes 262144 | tf_op jit(solution)/shard_map/all_to_all | solution.py:69
  161.1 55.7 %copy-start.118 = (f32[512]{0:T(512)}, f32[512]{0:T(512)S(1)}, u32[]{:S(2)}) copy-start(f32[512]{0:T(512)S(1)} %get-tuple-element.191) | copy-start | bytes 6148
  161.1 55.7 %copy-start.138 = (f32[512]{0:T(512)}, f32[512]{0:T(512)S(1)}, u32[]{:S(2)}) copy-start(f32[512]{0:T(512)S(1)} %get-tuple-element.190) | copy-start | bytes 6148
  228.2 18.6 %copy-start.220 = (f32[3,3,128]{2,1,0:T(4,128)S(1)}, f32[3,3,128]{2,1,0:T(4,128)}, u32[]{:S(2)}) copy-start(f32[3,3,128]{2,1,0:T(4,128)} %param.34) | copy-start | bytes 13828
  239.3 1.2 collective-permute-start
  241.5 16.3 %all-to-all-start.2 = ((f32[16,1,4096]{2,1,0:T(1,128)}), f32[16,1,4096]{2,1,0:T(1,128)S(1)}, u32[]{:S(2)}, u32[]{:S(2)}) async-start(f32[16,1,4096]{2,1,0:T(1,128)} %broadcast_in_dim.49), calls=%async_computation.2 | async-start | bytes 524288 | tf_op jit(solution)/shard_map/all_to_all | solution.py:76
  258.0 20.2 %collective-permute-start.1 = (f32[4096]{0:T(1024)S(1)}, f32[4096]{0:T(1024)S(1)}, u32[]{:S(2)}, u32[]{:S(2)}) collective-permute-start(f32[4096]{0:T(1024)S(1)} %reduce_sum.822), channel_id=1, source_target_pairs={{0,1},{1,0},{2,3},{3,2},{4,5},{5,4},{6,7},{7,6},{8,9},{9,8},{10,11... | collective-permute-start | bytes 49160 | tf_op jit(solution)/shard_map/ppermute | solution.py:77
  258.6 61.5 %copy-start.165 = (f32[4,8]{1,0:T(4,128)}, f32[4,8]{1,0:T(4,128)S(1)}, u32[]{:S(2)}) copy-start(f32[4,8]{1,0:T(4,128)S(1)} %get-tuple-element.302) | copy-start | bytes 388
  294.7 18.3 %all-to-all-start.3 = ((f32[32,1,1024]{2,1,0:T(1,128)}), f32[32,1,1024]{2,1,0:T(1,128)S(1)}, u32[]{:S(2)}, u32[]{:S(2)}) async-start(f32[32,1,1024]{2,1,0:T(1,128)} %broadcast_in_dim.50), calls=%async_computation.3 | async-start | bytes 262144 | tf_op jit(solution)/shard_map/all_to_all | solution.py:69
  314.4 34.8 %copy-start.100 = (f32[512]{0:T(512)}, f32[512]{0:T(512)S(1)}, u32[]{:S(2)}) copy-start(f32[512]{0:T(512)S(1)} %get-tuple-element.178) | copy-start | bytes 6148
  322.1 18.3 %all-to-all-start.4 = ((f32[32,1,1280]{2,1,0:T(1,128)}), f32[32,1,1280]{2,1,0:T(1,128)}, u32[]{:S(2)}, u32[]{:S(2)}) async-start(f32[32,1,1280]{2,1,0:T(1,128)} %broadcast_in_dim.53), calls=%async_computation.4 | async-start | bytes 327680 | tf_op jit(solution)/shard_map/all_to_all | solution.py:69
  357.4 13.2 %all-to-all-start.5 = ((f32[32,1,256]{2,1,0:T(1,128)}), f32[32,1,256]{2,1,0:T(1,128)S(1)}, u32[]{:S(2)}, u32[]{:S(2)}) async-start(f32[32,1,256]{2,1,0:T(1,128)} %broadcast_in_dim.54), calls=%async_computation.5 | async-start | bytes 65536 | tf_op jit(solution)/shard_map/all_to_all | solution.py:69
  380.9 12.6 %all-to-all-start.6 = ((f32[32,1,256]{2,1,0:T(1,128)}), f32[32,1,256]{2,1,0:T(1,128)S(1)}, u32[]{:S(2)}, u32[]{:S(2)}) async-start(f32[32,1,256]{2,1,0:T(1,128)} %broadcast_in_dim.55), calls=%async_computation.6 | async-start | bytes 65536 | tf_op jit(solution)/shard_map/all_to_all | solution.py:69
  403.9 12.5 %all-to-all-start.7 = ((f32[32,1,256]{2,1,0:T(1,128)}), f32[32,1,256]{2,1,0:T(1,128)S(1)}, u32[]{:S(2)}, u32[]{:S(2)}) async-start(f32[32,1,256]{2,1,0:T(1,128)} %broadcast_in_dim.56), calls=%async_computation.7 | async-start | bytes 65536 | tf_op jit(solution)/shard_map/all_to_all | solution.py:69
  428.2 2.9 collective-permute-start.2
  431.9 12.4 %all-to-all-start.8 = ((f32[16,1,2048]{2,1,0:T(1,128)}), f32[16,1,2048]{2,1,0:T(1,128)}, u32[]{:S(2)}, u32[]{:S(2)}) async-start(f32[16,1,2048]{2,1,0:T(1,128)} %broadcast_in_dim.57), calls=%async_computation.8 | async-start | bytes 262144 | tf_op jit(solution)/shard_map/all_to_all | solution.py:76
  445.3 2.8 collective-permute-start.3
  467.8 3.3 collective-permute-start.4
  471.8 35.4 %all-to-all-start.9 = ((f32[16,1,2048]{2,1,0:T(1,128)}), f32[16,1,2048]{2,1,0:T(1,128)}, u32[]{:S(2)}, u32[]{:S(2)}) async-start(f32[16,1,2048]{2,1,0:T(1,128)} %broadcast_in_dim.58), calls=%async_computation.9 | async-start | bytes 262144 | tf_op jit(solution)/shard_map/all_to_all | solution.py:76
  508.2 7.3 collective-permute-start.5
  532.5 20.2 %all-to-all-start.10 = ((f32[32,1,256]{2,1,0:T(1,128)}), f32[32,1,256]{2,1,0:T(1,128)S(1)}, u32[]{:S(2)}, u32[]{:S(2)}) async-start(f32[32,1,256]{2,1,0:T(1,128)} %broadcast_in_dim.59), calls=%async_computation.10 | async-start | bytes 65536 | tf_op jit(solution)/shard_map/all_to_all | solution.py:69
  560.7 13.3 %all-to-all-start.11 = ((f32[32,1,256]{2,1,0:T(1,128)}), f32[32,1,256]{2,1,0:T(1,128)S(1)}, u32[]{:S(2)}, u32[]{:S(2)}) async-start(f32[32,1,256]{2,1,0:T(1,128)} %broadcast_in_dim.60), calls=%async_computation.11 | async-start | bytes 65536 | tf_op jit(solution)/shard_map/all_to_all | solution.py:69
  583.2 9.8 all-to-all-start.12
  605.5 19.8 %all-to-all-start.13 = ((f32[32,1,1280]{2,1,0:T(1,128)}), f32[32,1,1280]{2,1,0:T(1,128)}, u32[]{:S(2)}, u32[]{:S(2)}) async-start(f32[32,1,1280]{2,1,0:T(1,128)} %broadcast_in_dim.63), calls=%async_computation.13 | async-start | bytes 327680 | tf_op jit(solution)/shard_map/all_to_all | solution.py:69
  638.2 14.6 %all-to-all-start.14 = ((f32[32,1,1024]{2,1,0:T(1,128)}), f32[32,1,1024]{2,1,0:T(1,128)S(1)}, u32[]{:S(2)}, u32[]{:S(2)}) async-start(f32[32,1,1024]{2,1,0:T(1,128)} %broadcast_in_dim.64), calls=%async_computation.14 | async-start | bytes 262144 | tf_op jit(solution)/shard_map/all_to_all | solution.py:69
  657.1 25.3 %copy-start.4 = (bf16[4,7,7,8,128]{4,3,2,1,0:T(8,128)(2,1)S(1)}, bf16[4,7,7,8,128]{4,3,2,1,0:T(8,128)(2,1)}, u32[]{:S(2)}) copy-start(bf16[4,7,7,8,128]{4,3,2,1,0:T(8,128)(2,1)} %copy-done.3) | copy-start | bytes 1204228
  682.2 3.9 collective-permute-start.6
  686.8 12.6 %all-to-all-start.15 = ((f32[16,1,3072]{2,1,0:T(1,128)}), f32[16,1,3072]{2,1,0:T(1,128)S(1)}, u32[]{:S(2)}, u32[]{:S(2)}) async-start(f32[16,1,3072]{2,1,0:T(1,128)} %broadcast_in_dim.65), calls=%async_computation.15 | async-start | bytes 393216 | tf_op jit(solution)/shard_map/all_to_all | solution.py:76
  699.6 1.2 collective-permute-start.7
  700.8 17.8 %copy-start.78 = (f32[2048]{0:T(1024)}, f32[2048]{0:T(1024)S(1)}, u32[]{:S(2)}) copy-start(f32[2048]{0:T(1024)S(1)} %get-tuple-element.277) | copy-start | bytes 24580
  726.2 10.9 all-to-all-start.16
  793.1 2.0 collective-permute-start.8
  795.8 11.1 all-to-all-start.17
  799.3 146.5 %all-reduce.30.cloned.1.call-start = ((), (), s32[]{:S(2)}) async-start(), calls=%async_computation.34 | async-start | bytes 11534336
  806.9 18.8 %collective-permute-start.9 = (f32[1280]{0:T(1024)S(1)}, f32[1280]{0:T(1024)}, u32[]{:S(2)}, u32[]{:S(2)}) collective-permute-start(f32[1280]{0:T(1024)S(1)} %reduce_sum.899), channel_id=1, source_target_pairs={{0,1},{1,0},{2,3},{3,2},{4,5},{5,4},{6,7},{7,6},{8,9},{9,8},{10,11... | collective-permute-start | bytes 15368 | tf_op jit(solution)/shard_map/ppermute | solution.py:77
  807.0 19.5 %slice-start = ((s8[12845056]{0:T(1024)(128)(4,1)}), s8[4194304]{0:T(1024)(128)(4,1)S(1)}, s32[]{:S(2)}) async-start(s8[12845056]{0:T(1024)(128)(4,1)} %bitcast.544), calls=%async_computation.35 | async-start | bytes 8388608
  807.0 19.4 %slice-start.4 = ((s8[12845056]{0:T(1024)(128)(4,1)}), s8[4194304]{0:T(1024)(128)(4,1)S(1)}, s32[]{:S(2)}) async-start(s8[12845056]{0:T(1024)(128)(4,1)} %bitcast.547), calls=%async_computation.39 | async-start | bytes 8388608
  807.0 19.4 %slice-start.1 = ((s8[12845056]{0:T(1024)(128)(4,1)}), s8[4194304]{0:T(1024)(128)(4,1)S(1)}, s32[]{:S(2)}) async-start(s8[12845056]{0:T(1024)(128)(4,1)} %bitcast.544), calls=%async_computation.36 | async-start | bytes 8388608
  807.1 19.4 %slice-start.2 = ((s8[12845056]{0:T(1024)(128)(4,1)}), s8[4194304]{0:T(1024)(128)(4,1)S(1)}, s32[]{:S(2)}) async-start(s8[12845056]{0:T(1024)(128)(4,1)} %bitcast.544), calls=%async_computation.37 | async-start | bytes 8388608
  807.1 19.4 %slice-start.3 = ((s8[12845056]{0:T(1024)(128)(4,1)}), s8[262144]{0:T(1024)(128)(4,1)S(1)}, s32[]{:S(2)}) async-start(s8[12845056]{0:T(1024)(128)(4,1)} %bitcast.544), calls=%async_computation.38 | async-start | bytes 524288
  807.1 19.4 %slice-start.5 = ((s8[12845056]{0:T(1024)(128)(4,1)}), s8[4194304]{0:T(1024)(128)(4,1)S(1)}, s32[]{:S(2)}) async-start(s8[12845056]{0:T(1024)(128)(4,1)} %bitcast.547), calls=%async_computation.40 | async-start | bytes 8388608
  807.1 19.4 %slice-start.6 = ((s8[12845056]{0:T(1024)(128)(4,1)}), s8[4194304]{0:T(1024)(128)(4,1)S(1)}, s32[]{:S(2)}) async-start(s8[12845056]{0:T(1024)(128)(4,1)} %bitcast.547), calls=%async_computation.41 | async-start | bytes 8388608
  807.1 19.4 %slice-start.7 = ((s8[12845056]{0:T(1024)(128)(4,1)}), s8[262144]{0:T(1024)(128)(4,1)S(1)}, s32[]{:S(2)}) async-start(s8[12845056]{0:T(1024)(128)(4,1)} %bitcast.547), calls=%async_computation.42 | async-start | bytes 524288
  850.0 156.2 %reduce-scatter.21.cloned.1.call-start = ((), (), s32[]{:S(2)}) async-start(), calls=%async_computation.29 | async-start | bytes 5898240 | tf_op jit(solution)/shard_map/reduce_scatter | solution.py:398
  864.4 207.5 %reduce-scatter.17.cloned.1.call-start = ((), (), s32[]{:S(2)}) async-start(), calls=%async_computation.27 | async-start | bytes 7077888 | tf_op jit(solution)/shard_map/reduce_scatter | solution.py:398
  889.2 204.8 %reduce-scatter.13.cloned.1.call-start = ((), (), s32[]{:S(2)}) async-start(), calls=%async_computation.25 | async-start | bytes 163840 | tf_op jit(solution)/shard_map/reduce_scatter | solution.py:399
  948.1 168.5 %reduce-scatter.15.cloned.1.call-start = ((), (), s32[]{:S(2)}) async-start(), calls=%async_computation.26 | async-start | bytes 737280 | tf_op jit(solution)/shard_map/reduce_scatter | solution.py:399
  950.7 188.4 %reduce-scatter.23.cloned.1.call-start = ((), (), s32[]{:S(2)}) async-start(), calls=%async_computation.30 | async-start | bytes 819200 | tf_op jit(solution)/shard_map/reduce_scatter | solution.py:399
  1006.2 157.5 %reduce-scatter.19.cloned.1.call-start = ((), (), s32[]{:S(2)}) async-start(), calls=%async_computation.28 | async-start | bytes 983040 | tf_op jit(solution)/shard_map/reduce_scatter | solution.py:399
  1016.7 55.2 %copy-start.254 = (bf16[1024,512]{1,0:T(8,128)(2,1)S(1)}, bf16[1024,512]{1,0:T(8,128)(2,1)}, u32[]{:S(2)}) copy-start(bf16[1024,512]{1,0:T(8,128)(2,1)} %all-gather.11.cloned.1.call-done) | copy-start | bytes 3145732
  1072.0 18.0 %copy-start.79 = (f32[2048]{0:T(1024)S(1)}, f32[2048]{0:T(1024)}, u32[]{:S(2)}) copy-start(f32[2048]{0:T(1024)} %copy-done.78) | copy-start | bytes 24580
  1072.0 18.0 %copy-start.88 = (f32[2048]{0:T(1024)S(1)}, f32[2048]{0:T(1024)}, u32[]{:S(2)}) copy-start(f32[2048]{0:T(1024)} %copy-done.87) | copy-start | bytes 24580
  1072.0 18.0 %copy-start.123 = (f32[512]{0:T(512)S(1)}, f32[512]{0:T(512)}, u32[]{:S(2)}) copy-start(f32[512]{0:T(512)} %copy-done.122) | copy-start | bytes 6148
  1072.0 18.0 %copy-start.127 = (f32[512]{0:T(512)S(1)}, f32[512]{0:T(512)}, u32[]{:S(2)}) copy-start(f32[512]{0:T(512)} %copy-done.126) | copy-start | bytes 6148
  1072.1 18.0 %copy-start.161 = (f32[512]{0:T(512)S(1)}, f32[512]{0:T(512)}, u32[]{:S(2)}) copy-start(f32[512]{0:T(512)} %copy-done.159) | copy-start | bytes 6148
  1072.1 18.0 %copy-start.189 = (f32[128]{0:T(128)S(1)}, f32[128]{0:T(128)}, u32[]{:S(2)}) copy-start(f32[128]{0:T(128)} %copy-done.188) | copy-start | bytes 1540
  1072.1 18.0 %copy-start.193 = (f32[128]{0:T(128)S(1)}, f32[128]{0:T(128)}, u32[]{:S(2)}) copy-start(f32[128]{0:T(128)} %copy-done.192) | copy-start | bytes 1540
  1072.1 18.0 %copy-start.197 = (f32[128]{0:T(128)S(1)}, f32[128]{0:T(128)}, u32[]{:S(2)}) copy-start(f32[128]{0:T(128)} %copy-done.196) | copy-start | bytes 1540
  1072.1 18.0 %copy-start.228 = (f32[32]{0:T(128)S(1)}, f32[32]{0:T(128)}, u32[]{:S(2)}) copy-start(f32[32]{0:T(128)} %copy-done.226) | copy-start | bytes 388
  (240 other events, 1338.6 us)
Sparse Core Ops, SparseCore 0:
  10.9 56.3 all-gather.10
  70.8 62.9 all-gather.8
  137.2 76.9 all-gather.12
  217.4 58.8 all-gather.14
  850.1 95.7 all-reduce.29
  949.4 56.6 reduce-scatter.20
  1010.1 61.7 reduce-scatter.16
  1074.8 19.1 reduce-scatter.12
  1096.3 20.2 reduce-scatter.14
  1118.7 20.3 reduce-scatter.22
  1141.4 22.2 reduce-scatter.18
where the time goes:
time: 1190 us; the launch traced here: 1170 us
  waiting for transfers between devices  410 us (34%)
  local copies, waits for them, and re-layouts  242 us (20%)
  matrix products  230 us (19%)
  other arithmetic  188 us (16%)
  starting transfers between devices  83.4 us (7%)
  between operations  20.4 us (2%)
    all_gather x4, waiting for transfers between devices, gather(): return lax.all_gather(value, AXES, axis=0, tiled=False)  123 us
    reduce_scatter x2, waiting for transfers between devices, scatter(): merged = lax.psum_scatter(merged, 'fsdp', scatter_dimension=0, tiled=False)  99.6 us
    dot_general x10, matrix products, dot_t(): lax.dot_general(grad.reshape(-1, shape[-1]), weight, (((1,), (1,)), ((),...  77.5 us
    dot_general x10, matrix products, weight_grad(): lax.dot_general(left.reshape(-1, left.shape[-1]), grad.reshape(-1, grad.s...  74.3 us
    dot_general x13, matrix products, dot(): jnp.dot(left.reshape(-1, shape[-1]), weight, preferred_element_type=F32)  70 us
    unnamed x606, local copies, waits for them, and re-layouts  68.4 us
    reduce_scatter x4, waiting for transfers between devices, scatter(): merged = lax.psum_scatter(merged, 'dp', scatter_dimension=0, tiled=False)  63 us
    all_to_all x13, starting transfers between devices, flat(): return jnp.sum(lax.all_to_all(copies, AXES, 0, 0), axis=0)  60.4 us
  transfers between devices with their start and end apart: 39, of which 26 were waited for; matrix products, arithmetic and copies ran while one was open for 30% of the time, Pallas kernels for 0%

commit v1 on v0

v1 whole, which is shorter than its diff:
```python
import jax
import jax.numpy as jnp
from jax import lax
from jax.experimental import pallas as pl
from jax.experimental.pallas import tpu as pltpu
from jax.sharding import PartitionSpec as P

EPSILON = 1e-05
HIGHEST = lax.Precision.HIGHEST
AXES = ("dp", "fsdp")
BF = jnp.bfloat16
F32 = jnp.float32


def by_clip(values, frames):
    return values.reshape(values.shape[:-2] + (-1, frames, values.shape[-1]))


def earlier(values):
    return jnp.concatenate([jnp.zeros_like(values[..., :1, :]), values[..., :-1, :]], axis=-2)


def later(values):
    return jnp.concatenate([values[..., 1:, :], jnp.zeros_like(values[..., :1, :])], axis=-2)


def taps_of(values, size):
    padded = jnp.pad(values, ((1, 1), (1, 1), (0, 0), (0, 0), (0, 0)))
    return [padded[r : r + size, c : c + size] for r in range(3) for c in range(3)]


def dot(left, weight):
    shape = left.shape
    flat = jnp.dot(left.reshape(-1, shape[-1]), weight, preferred_element_type=F32)
    return flat.reshape(shape[:-1] + (weight.shape[1],))


def dot_t(grad, weight):
    shape = grad.shape
    flat = lax.dot_general(
        grad.reshape(-1, shape[-1]), weight, (((1,), (1,)), ((), ())), preferred_element_type=F32
    )
    return flat.reshape(shape[:-1] + (weight.shape[0],))


def weight_grad(left, grad):
    return lax.dot_general(
        left.reshape(-1, left.shape[-1]),
        grad.reshape(-1, grad.shape[-1]),
        (((0,), (0,)), ((), ())),
        preferred_element_type=F32,
    )


def silu_slope(values):
    sig = jax.nn.sigmoid(values)
    return sig * (1.0 + values * (1.0 - sig))


def total_over(values):
    return jnp.sum(values, axis=tuple(range(values.ndim - 1)))


def silu_parts(norm):
    sig = 1.0 / (1.0 + jnp.exp(-norm))
    return sig, norm * sig


def call(body, grid, ins, in_blocks, outs, out_blocks, scratch=(), limit=56, flops=0, moved=0):
    def spec(block):
        if block is None:
            return pl.BlockSpec(memory_space=pltpu.VMEM)
        return pl.BlockSpec(block[0], block[1])

    return pl.pallas_call(
        body,
        grid=grid,
        in_specs=[spec(b) for b in in_blocks],
        out_specs=[spec(b) for b in out_blocks],
        out_shape=[jax.ShapeDtypeStruct(s, d) for s, d in outs],
        scratch_shapes=list(scratch),
        compiler_params=pltpu.CompilerParams(
            vmem_limit_bytes=limit * 1024 * 1024,
            dimension_semantics=("arbitrary",) * len(grid),
        ),
        cost_estimate=pl.CostEstimate(flops=flops, bytes_accessed=moved, transcendentals=0),
    )(*ins)


def whole(shape):
    return shape, lambda *_: (0,) * len(shape)


def kernel_reduce1(feats, weight, mask, slots, height, frames):
    c_in, middle = weight.shape
    half = height // 2
    rows = half * height * frames

    def body(x_ref, w_ref, m_ref, raw_ref, sum_ref):
        first = (pl.program_id(0) == 0) & (pl.program_id(1) == 0)

        @pl.when(first)
        def _():
            sum_ref[...] = jnp.zeros_like(sum_ref)

        raw = jnp.dot(x_ref[...], w_ref[...], preferred_element_type=F32)
        raw = raw.reshape(half * height, frames, middle)
        raw_ref[...] = raw.reshape(half, height, frames, middle)
        weight8 = m_ref[:, :1]
        sum_ref[0] += jnp.sum(raw, axis=0) * weight8
        sum_ref[1] += jnp.sum(raw * raw, axis=0) * weight8

    return call(
        body,
        (slots, 2),
        (feats, weight, mask),
        (
            ((rows, c_in), lambda c, h: (c * 2 + h, 0)),
            whole(weight.shape),
            ((frames, mask.shape[1]), lambda c, h: (c, 0)),
        ),
        (
            ((height, height, slots * frames, middle), F32),
            ((2, frames, middle), F32),
        ),
        (
            ((half, height, frames, middle), lambda c, h: (h, 0, c, 0)),
            whole((2, frames, middle)),
        ),
        flops=2 * feats.shape[0] * c_in * middle,
        moved=feats.size * 2 + feats.shape[0] * middle * 4,
    )


def kernel_conv_down(raw_a, alpha, beta, mask, taps):
    height, _, batch, middle = raw_a.shape
    half = height // 2
    rows = half * batch

    def body(a_ref, al_ref, be_ref, m_ref, *refs):
        w_refs, (act_ref, raw_ref, sum_ref, cols, w_ref) = refs[:9], refs[9:]
        step = pl.program_id(0)
        wide = 3 * middle

        @pl.when(step == 0)
        def _():
            sum_ref[...] = jnp.zeros_like(sum_ref)
            cols[...] = jnp.zeros_like(cols)
            for t in range(9):
                w_ref[t * middle : (t + 1) * middle] = taps[t].of(w_refs[t], 0)

        @pl.when(step > 0)
        def _():
            cols[:, :wide] = cols[:, 2 * wide :]

        al, be, m = al_ref[...], be_ref[...], m_ref[:, :1]
        for p in range(2):
            base = (1 + p) * wide
            for j in range(half):
                for q in range(2):
                    norm = a_ref[p, 2 * j + q] * al + be
                    act = (silu_parts(norm)[1] * m).astype(BF)
                    act_ref[p, 2 * j + q] = act
                    lane = base + (1 + q) * middle
                    cols[j * batch : (j + 1) * batch, lane : lane + middle] = act
                    if q == 1 and j + 1 < half:
                        cols[(j + 1) * batch : (j + 2) * batch, base : base + middle] = act
        raw = jnp.dot(cols[...], w_ref[...], preferred_element_type=F32)
        raw = raw.reshape(half, batch, middle)
        raw_ref[0] = raw
        sum_ref[0] += jnp.sum(raw, axis=0) * m
        sum_ref[1] += jnp.sum(raw * raw, axis=0) * m

    return call(
        body,
        (half,),
        (raw_a, alpha, beta, mask) + tuple(t.array for t in taps),
        (
            ((2, height, batch, middle), lambda i: (i, 0, 0, 0)),
            whole(alpha.shape),
            whole(beta.shape),
            whole(mask.shape),
        )
        + tuple(t.block() for t in taps),
        (
            (raw_a.shape, BF),
            ((half, half, batch, middle), F32),
            ((2, batch, middle), F32),
        ),
        (
            ((2, height, batch, middle), lambda i: (i, 0, 0, 0)),
            ((1, half, batch, middle), lambda i: (i, 0, 0, 0)),
            whole((2, batch, middle)),
        ),
        scratch=[pltpu.VMEM((rows, 9 * middle), BF), pltpu.VMEM((9 * middle, middle), BF)],
        flops=2 * half * rows * 9 * middle * middle,
        moved=raw_a.size * 6 + 18 * middle * middle,
    )


def kernel_conv_down_weights(act_a, grad):
    height, _, batch, middle = act_a.shape
    half = height // 2
    split = act_a.reshape(half, 2, half, 2, batch, middle)

    def body(a_ref, g_ref, out_ref, cols):
        step = pl.program_id(0)
        for r in range(3):
            for c in range(3):
                top, left = int(r == 0), int(c == 0)

                @pl.when(step == r * 3 + c)
                def _(r=r, c=c, top=top, left=left):
                    if top:
                        cols[0] = jnp.zeros_like(cols[0])
                    if left:
                        cols[:, 0] = jnp.zeros_like(cols[:, 0])
                    cols[top:, left:] = a_ref[
                        : half - top, int(r != 1), : half - left, int(c != 1)
                    ]

        taps = cols[...].reshape(half * half * batch, middle)
        out_ref[0] = lax.dot_general(
            taps, g_ref[...], (((0,), (0,)), ((), ())), preferred_element_type=F32
        ).astype(BF)

    return call(
        body,
        (9,),
        (split, grad.reshape(-1, middle)),
        (whole(split.shape), whole((half * half * batch, middle))),
        (((9, middle, middle), BF),),
        (((1, middle, middle), lambda t: (t, 0, 0)),),
        scratch=[pltpu.VMEM((half, half, batch, middle), BF)],
        flops=2 * half * half * batch * 9 * middle * middle,
        moved=act_a.size * 2 + grad.size * 2 + 18 * middle * middle,
    )[0]


def kernel_conv_down_back(grad, taps, raw_a, stats, mask):
    height, _, batch, middle = raw_a.shape
    half = height // 2
    rows = half * batch

    def body(g_ref, n_ref, a_ref, s_ref, m_ref, *refs):
        w_refs, (out_ref, sum_ref, here, below) = refs[:9], refs[9:]
        step = pl.program_id(0)

        @pl.when(step == 0)
        def _():
            sum_ref[...] = jnp.zeros_like(sum_ref)
            here[half] = jnp.zeros_like(here[half])
            below[half] = jnp.zeros_like(below[half])

        here[:half] = g_ref[0]

        @pl.when(step < half - 1)
        def _():
            below[:half] = n_ref[0]

        @pl.when(step == half - 1)
        def _():
            below[:half] = jnp.zeros_like(n_ref[0])

        def tap(ref, right, t):
            return lax.dot_general(
                ref[right : right + half].reshape(rows, middle),
                taps[t].of(w_refs[t], 0),
                (((1,), (1,)), ((), ())),
                preferred_element_type=F32,
            )

        al, be = s_ref[0:1], s_ref[1:2]
        mean, inv = s_ref[2:3], s_ref[3:4]
        m = m_ref[:, :1]
        plans = (
            (0, 0, ((here, 0, 4),)),
            (0, 1, ((here, 0, 5), (here, 1, 3))),
            (1, 0, ((here, 0, 7), (below, 0, 1))),
            (1, 1, ((here, 0, 8), (here, 1, 6), (below, 0, 2), (below, 1, 0))),
        )
        for p, q, parts in plans:
            back = tap(*parts[0])
            for part in parts[1:]:
                back = back + tap(*part)
            raw = a_ref[0, p, :, q]
            norm = raw * al + be
            sig, act = silu_parts(norm)
            slope = sig + act * (1.0 - sig)
            out = back.reshape(half, batch, middle) * slope * m
            out_ref[0, p, :, q] = out
            sum_ref[0] += jnp.sum(out, axis=0)
            sum_ref[1] += jnp.sum(out * ((raw - mean) * inv), axis=0)

    return call(
        body,
        (half,),
        (grad, grad, raw_a.reshape(half, 2, half, 2, batch, middle), stats, mask)
        + tuple(t.array for t in taps),
        (
            ((1, half, batch, middle), lambda i: (i, 0, 0, 0)),
            ((1, half, batch, middle), lambda i: (jnp.minimum(i + 1, half - 1), 0, 0, 0)),
            ((1, 2, half, 2, batch, middle), lambda i: (i, 0, 0, 0, 0, 0)),
            whole(stats.shape),
            whole(mask.shape),
        )
        + tuple(t.block() for t in taps),
        (
            ((half, 2, half, 2, batch, middle), F32),
            ((2, batch, middle), F32),
        ),
        (
            ((1, 2, half, 2, batch, middle), lambda i: (i, 0, 0, 0, 0, 0)),
            whole((2, batch, middle)),
        ),
        scratch=[pltpu.VMEM((half + 1, batch, middle), BF), pltpu.VMEM((half + 1, batch, middle), BF)],
        flops=2 * half * rows * 9 * middle * middle,
        moved=raw_a.size * 8 + 18 * middle * middle,
    )


def kernel_first_grad(grad, raw_a, feats, stats, mask, slots, frames):
    height, _, batch, middle = raw_a.shape
    half = height // 2
    rows = half * height * frames
    c_in = feats.shape[1]

    def body(g_ref, a_ref, x_ref, s_ref, m_ref, out_ref, w_ref, acc):
        first = (pl.program_id(0) == 0) & (pl.program_id(1) == 0)
        last = (pl.program_id(0) == slots - 1) & (pl.program_id(1) == 1)

        @pl.when(first)
        def _():
            acc[...] = jnp.zeros_like(acc)

        scale, mean, inv = s_ref[0:1], s_ref[1:2], s_ref[2:3]
        shift, spread = s_ref[3:4], s_ref[4:5]
        m = m_ref[:, :1]
        unit = (a_ref[...] - mean) * inv
        value = scale * (g_ref[...] - m * (shift + unit * spread))
        value = value.reshape(rows, middle).astype(BF)
        out_ref[...] = value
        acc[...] += lax.dot_general(
            x_ref[...], value, (((0,), (0,)), ((), ())), preferred_element_type=F32
        )

        @pl.when(last)
        def _():
            w_ref[...] = acc[...].astype(BF)

    block = (half, height, frames, middle)
    return call(
        body,
        (slots, 2),
        (grad.reshape(raw_a.shape), raw_a, feats, stats, mask),
        (
            (block, lambda c, h: (h, 0, c, 0)),
            (block, lambda c, h: (h, 0, c, 0)),
            ((rows, c_in), lambda c, h: (c * 2 + h, 0)),
            whole(stats.shape),
            ((frames, mask.shape[1]), lambda c, h: (c, 0)),
        ),
        (
            ((slots * 2 * rows, middle), BF),
            ((c_in, middle), BF),
        ),
        (
            ((rows, middle), lambda c, h: (c * 2 + h, 0)),
            whole((c_in, middle)),
        ),
        scratch=[pltpu.VMEM((c_in, middle), F32)],
        flops=2 * raw_a.size * c_in,
        moved=raw_a.size * 10 + feats.size * 2,
    )


def kernel_grad_features(grad, weight, sampled, height, slots, frames):
    c_in, middle = weight.shape
    half = height // 2
    rows = height * height * frames

    def body(g_ref, w_ref, s_ref, out_ref):
        value = lax.dot_general(
            g_ref[...], w_ref[...], (((1,), (1,)), ((), ())), preferred_element_type=F32
        )
        value = value.reshape(half, 2, half, 2, frames, c_in)
        even = value[:, 0, :, 0] + s_ref[...]
        line = jnp.stack([even, value[:, 0, :, 1]], axis=2)
        both = jnp.stack([line, value[:, 1]], axis=1)
        out_ref[...] = both.reshape(rows, c_in).astype(BF)

    return call(
        body,
        (slots,),
        (grad, weight, sampled),
        (
            ((rows, middle), lambda c: (c, 0)),
            whole(weight.shape),
            ((half, half, frames, c_in), lambda c: (0, 0, c, 0)),
        ),
        (((slots * rows, c_in), BF),),
        (((rows, c_in), lambda c: (c, 0)),),
        flops=2 * grad.size * c_in,
        moved=grad.size * 2 + slots * rows * c_in * 2 + sampled.size * 4,
    )[0]


CHUNK = 256


def fold(value):
    return jnp.sum(value.reshape(-1, 8, value.shape[-1]), axis=0)


def chunks(width):
    return [slice(b, min(b + CHUNK, width)) for b in range(0, width, CHUNK)]


def zero_first(*refs):
    @pl.when(pl.program_id(0) == 0)
    def _():
        for ref in refs:
            ref[...] = jnp.zeros_like(ref)


def row_block(half, batch, width):
    return (half, batch, width), lambda i: (i, 0, 0)


class Packed:
    def __init__(self, array, rows, first, count):
        self.array, self.rows, self.first, self.count = array, rows, first, count

    def block(self):
        size, index = self.rows * self.count, self.first // self.count
        return (self.array.shape[0], size, self.array.shape[2]), lambda *_: (0, index, 0)

    def of(self, ref, k):
        part = ref[:, k * self.rows : (k + 1) * self.rows, :]
        return part.reshape(-1, part.shape[-1])


def nt(left, right):
    return lax.dot_general(left, right, (((1,), (1,)), ((), ())), preferred_element_type=F32)


def tn(left, right):
    return lax.dot_general(left, right, (((0,), (0,)), ((), ())), preferred_element_type=F32)


def nn(left, right):
    return jnp.dot(left, right, preferred_element_type=F32)


def kernel_expand(raw_b, stats, mask, weight, half):
    _, batch, middle = raw_b.shape
    wide = weight.count * middle
    rows = half * batch

    def body(b_ref, s_ref, m_ref, w_ref, act_ref, raw_ref, sum_ref):
        zero_first(sum_ref)
        m = m_ref[...]

        @pl.loop(0, half)
        def _(j):
            for c in chunks(middle):
                norm = b_ref[j, :, c] * s_ref[0:1, c] + s_ref[1:2, c]
                act_ref[j, :, c] = (silu_parts(norm)[1] * m).astype(BF)

        m = m_ref[:, :1]
        act = act_ref[...].reshape(rows, middle)
        for k in range(weight.count):
            raw = nn(act, weight.of(w_ref, k)).reshape(half, batch, middle)
            span = slice(k * middle, (k + 1) * middle)
            raw_ref[:, :, span] = raw
            sum_ref[0, :, span] += fold(jnp.sum(raw, axis=0) * m)
            sum_ref[1, :, span] += fold(jnp.sum(raw * raw, axis=0) * m)

    pixels = half * half
    return call(
        body,
        (half,),
        (raw_b, stats, mask, weight.array),
        (row_block(half, batch, middle), whole(stats.shape), whole(mask.shape), weight.block()),
        (
            ((pixels, batch, middle), BF),
            ((pixels, batch, wide), F32),
            ((2, 8, wide), F32),
        ),
        (row_block(half, batch, middle), row_block(half, batch, wide), whole((2, 8, wide))),
        flops=2 * raw_b.size * wide,
        moved=raw_b.size * 6 + pixels * batch * wide * 4,
    )


def kernel_project(sampled, mask, weight, half):
    pixels, batch, c_in = sampled.shape
    middle = weight.array.shape[2]
    wide = weight.count * middle

    def body(x_ref, m_ref, w_ref, raw_ref, sum_ref):
        zero_first(sum_ref)
        m = m_ref[:, :1]
        left = x_ref[...].reshape(half * batch, c_in)
        for k in range(weight.count):
            raw = nn(left, weight.of(w_ref, k)).reshape(half, batch, middle)
            span = slice(k * middle, (k + 1) * middle)
            raw_ref[:, :, span] = raw
            sum_ref[0, :, span] += fold(jnp.sum(raw, axis=0) * m)
            sum_ref[1, :, span] += fold(jnp.sum(raw * raw, axis=0) * m)

    return call(
        body,
        (half,),
        (sampled, mask, weight.array),
        (row_block(half, batch, c_in), whole(mask.shape), weight.block()),
        (((pixels, batch, wide), F32), ((2, 8, wide), F32)),
        (row_block(half, batch, wide), whole((2, 8, wide))),
        flops=2 * sampled.size * wide,
        moved=sampled.size * 2 + pixels * batch * wide * 4,
    )


def kernel_block_one(raw_c, raw_p, stats, mask, weight, half):
    pixels, batch, wide = raw_c.shape
    middle = weight.array.shape[2]

    def body(c_ref, p_ref, s_ref, m_ref, w_ref, one_ref, raw_ref, sum_ref):
        zero_first(sum_ref)
        m = m_ref[...]

        @pl.loop(0, half)
        def _(j):
            for c in chunks(wide):
                total = c_ref[j, :, c] * s_ref[0:1, c] + p_ref[j, :, c] * s_ref[1:2, c] + s_ref[2:3, c]
                one_ref[j, :, c] = (silu_parts(total)[1] * m).astype(BF)

        m = m_ref[:, :1]
        raw = nn(one_ref[...].reshape(half * batch, wide), weight.of(w_ref, 0))
        raw = raw.reshape(half, batch, middle)
        raw_ref[...] = raw
        sum_ref[0] += fold(jnp.sum(raw, axis=0) * m)
        sum_ref[1] += fold(jnp.sum(raw * raw, axis=0) * m)

    return call(
        body,
        (half,),
        (raw_c, raw_p, stats, mask, weight.array),
        (
            row_block(half, batch, wide),
            row_block(half, batch, wide),
            whole(stats.shape),
            whole(mask.shape),
            weight.block(),
        ),
        (
            ((pixels, batch, wide), BF),
            ((pixels, batch, middle), F32),
            ((2, 8, middle), F32),
        ),
        (row_block(half, batch, wide), row_block(half, batch, middle), whole((2, 8, middle))),
        flops=2 * raw_c.size * middle,
        moved=raw_c.size * 10,
    )


def kernel_result(raw_e, block_one, cot, stats, mask, half):
    pixels, batch, wide = raw_e.shape

    def body(e_ref, o_ref, g_ref, s_ref, m_ref, res_ref, grad_ref, sum_ref):
        zero_first(sum_ref)
        m = m_ref[...]

        @pl.loop(0, half)
        def _(j):
            for c in chunks(wide):
                raw = e_ref[j, :, c]
                total = raw * s_ref[0:1, c] + s_ref[1:2, c] + o_ref[j, :, c].astype(F32)
                sig, act = silu_parts(total)
                res_ref[j, :, c] = (act * m).astype(BF)
                grad = g_ref[j, :, c].astype(F32) * m * (sig + act * (1.0 - sig))
                grad_ref[j, :, c] = grad
                sum_ref[0, :, c] += fold(grad)
                sum_ref[1, :, c] += fold(grad * ((raw - s_ref[2:3, c]) * s_ref[3:4, c]))

    return call(
        body,
        (half,),
        (raw_e, block_one, cot, stats, mask),
        (
            row_block(half, batch, wide),
            row_block(half, batch, wide),
            row_block(half, batch, wide),
            whole(stats.shape),
            whole(mask.shape),
        ),
        (
            ((pixels, batch, wide), BF),
            ((pixels, batch, wide), F32),
            ((2, 8, wide), F32),
        ),
        (row_block(half, batch, wide), row_block(half, batch, wide), whole((2, 8, wide))),
        flops=20 * raw_e.size,
        moved=raw_e.size * 14,
    )


def kernel_block_back(grad_narrow, raw_d, stats_d, weight, grad_total, raw_c, raw_p, stats, mask, half):
    pixels, batch, wide = raw_c.shape
    middle = raw_d.shape[2]

    def body(n_ref, d_ref, sd_ref, w_ref, t_ref, c_ref, p_ref, s_ref, m_ref, nar_ref, one_ref, sum_ref, back):
        zero_first(sum_ref)
        m = m_ref[...]

        @pl.loop(0, half)
        def _(j):
            for c in chunks(middle):
                unit = (d_ref[j, :, c] - sd_ref[1:2, c]) * sd_ref[2:3, c]
                value = sd_ref[0:1, c] * (
                    n_ref[j, :, c] - m * (sd_ref[3:4, c] + unit * sd_ref[4:5, c])
                )
                nar_ref[j, :, c] = value.astype(BF)

        left = nar_ref[...].reshape(half * batch, middle)
        back[...] = nt(left, weight.of(w_ref, 0)).reshape(half, batch, wide)

        @pl.loop(0, half)
        def _(j):
            for c in chunks(wide):
                raw_c, raw_p = c_ref[j, :, c], p_ref[j, :, c]
                total = raw_c * s_ref[0:1, c] + raw_p * s_ref[1:2, c] + s_ref[2:3, c]
                sig, act = silu_parts(total)
                grad = (t_ref[j, :, c] + back[j, :, c]) * m * (sig + act * (1.0 - sig))
                one_ref[j, :, c] = grad
                sum_ref[0, :, c] += fold(grad)
                sum_ref[1, :, c] += fold(grad * ((raw_c - s_ref[3:4, c]) * s_ref[4:5, c]))
                sum_ref[2, :, c] += fold(grad * ((raw_p - s_ref[5:6, c]) * s_ref[6:7, c]))

    return call(
        body,
        (half,),
        (grad_narrow, raw_d, stats_d, weight.array, grad_total, raw_c, raw_p, stats, mask),
        (
            row_block(half, batch, middle),
            row_block(half, batch, middle),
            whole(stats_d.shape),
            weight.block(),
            row_block(half, batch, wide),
            row_block(half, batch, wide),
            row_block(half, batch, wide),
            whole(stats.shape),
            whole(mask.shape),
        ),
        (
            ((pixels, batch, middle), BF),
            ((pixels, batch, wide), F32),
            ((3, 8, wide), F32),
        ),
        (row_block(half, batch, middle), row_block(half, batch, wide), whole((3, 8, wide))),
        scratch=[pltpu.VMEM((half, batch, wide), F32)],
        flops=2 * raw_c.size * middle,
        moved=raw_c.size * 16,
    )


def kernel_expand_back(grad_one, raw_c, raw_p, stats, weight, raw_b, stats_b, mask, half):
    pixels, batch, wide = raw_c.shape
    middle = raw_b.shape[2]

    def body(g_ref, c_ref, p_ref, s_ref, w_ref, b_ref, sb_ref, m_ref, wid_ref, sho_ref, out_ref, sum_ref):
        zero_first(sum_ref)
        m = m_ref[...]

        @pl.loop(0, half)
        def _(j):
            for c in chunks(wide):
                grad = g_ref[j, :, c]
                for raw_ref, to_ref, k in ((c_ref, wid_ref, 0), (p_ref, sho_ref, 5)):
                    unit = (raw_ref[j, :, c] - s_ref[k + 1 : k + 2, c]) * s_ref[k + 2 : k + 3, c]
                    value = s_ref[k : k + 1, c] * (
                        grad - m * (s_ref[k + 3 : k + 4, c] + unit * s_ref[k + 4 : k + 5, c])
                    )
                    to_ref[j, :, c] = value.astype(BF)

        m = m_ref[:, :1]
        back = None
        for k in range(weight.count):
            left = wid_ref[:, :, k * middle : (k + 1) * middle].reshape(half * batch, middle)
            part = nt(left, weight.of(w_ref, k))
            back = part if back is None else back + part
        raw = b_ref[...]
        sig, act = silu_parts(raw * sb_ref[0:1] + sb_ref[1:2])
        grad = back.reshape(half, batch, middle) * m * (sig + act * (1.0 - sig))
        out_ref[...] = grad
        sum_ref[0] += fold(jnp.sum(grad, axis=0))
        sum_ref[1] += fold(jnp.sum(grad * ((raw - sb_ref[2:3]) * sb_ref[3:4]), axis=0))

    return call(
        body,
        (half,),
        (grad_one, raw_c, raw_p, stats, weight.array, raw_b, stats_b, mask),
        (
            row_block(half, batch, wide),
            row_block(half, batch, wide),
            row_block(half, batch, wide),
            whole(stats.shape),
            weight.block(),
            row_block(half, batch, middle),
            whole(stats_b.shape),
            whole(mask.shape),
        ),
        (
            ((pixels, batch, wide), BF),
            ((pixels, batch, wide), BF),
            ((pixels, batch, middle), F32),
            ((2, 8, middle), F32),
        ),
        (
            row_block(half, batch, wide),
            row_block(half, batch, wide),
            row_block(half, batch, middle),
            whole((2, 8, middle)),
        ),
        flops=2 * raw_c.size * middle,
        moved=raw_c.size * 16,
    )


def kernel_sampled_back(grad, weight, half):
    pixels, batch, wide = grad.shape
    middle = weight.array.shape[2]
    c_in = weight.array.shape[0] * weight.rows

    def body(g_ref, w_ref, out_ref):
        back = None
        for k in range(weight.count):
            left = g_ref[:, :, k * middle : (k + 1) * middle].reshape(half * batch, middle)
            part = nt(left, weight.of(w_ref, k))
            back = part if back is None else back + part
        out_ref[...] = back.reshape(half, batch, c_in)

    return call(
        body,
        (half,),
        (grad, weight.array),
        (row_block(half, batch, wide), weight.block()),
        (((pixels, batch, c_in), F32),),
        (row_block(half, batch, c_in),),
        flops=2 * grad.size * c_in,
        moved=grad.size * 2 + pixels * batch * c_in * 4,
    )[0]


def kernel_join(excited, outputs, raw_g, stats_g, mask, weight, half):
    pixels, batch, middle = excited.shape
    group = middle // 4
    wide = weight.count * middle

    def body(x_ref, o1, o2, r_ref, sg_ref, m_ref, w_ref, join_ref, raw_ref, sum_ref):
        zero_first(sum_ref)
        m = m_ref[:, :group]
        join_ref[:, :, :group] = x_ref[...]
        join_ref[:, :, group : 2 * group] = o1[...]
        join_ref[:, :, 2 * group : 3 * group] = o2[...]
        act = silu_parts(r_ref[...] * sg_ref[0:1] + sg_ref[1:2])[1] * m
        join_ref[:, :, 3 * group :] = act.astype(BF)
        left = join_ref[...].reshape(half * batch, middle)
        m = m_ref[:, :1]
        for k in range(weight.count):
            raw = nn(left, weight.of(w_ref, k)).reshape(half, batch, middle)
            span = slice(k * middle, (k + 1) * middle)
            raw_ref[:, :, span] = raw
            sum_ref[0, :, span] += fold(jnp.sum(raw, axis=0) * m)
            sum_ref[1, :, span] += fold(jnp.sum(raw * raw, axis=0) * m)

    part = row_block(half, batch, group)
    return call(
        body,
        (half,),
        (excited, outputs[0], outputs[1], raw_g, stats_g, mask, weight.array),
        (part, part, part, part, whole(stats_g.shape), whole(mask.shape), weight.block()),
        (((pixels, batch, middle), BF), ((pixels, batch, wide), F32), ((2, 8, wide), F32)),
        (row_block(half, batch, middle), row_block(half, batch, wide), whole((2, 8, wide))),
        flops=2 * excited.size * wide,
        moved=excited.size * 4 + pixels * batch * wide * 4,
    )


def kernel_final_back(grad_total, raw_e, stats, mask, weight, raw_g, stats_g, half):
    pixels, batch, wide = raw_e.shape
    middle = weight.array.shape[2]
    group = middle // 4

    def body(g_ref, e_ref, s_ref, m_ref, w_ref, r_ref, sg_ref, fin_ref, out_ref, pre_ref, sum_ref):
        zero_first(sum_ref)
        m = m_ref[...]

        @pl.loop(0, half)
        def _(j):
            for c in chunks(wide):
                unit = (e_ref[j, :, c] - s_ref[1:2, c]) * s_ref[2:3, c]
                value = s_ref[0:1, c] * (
                    g_ref[j, :, c] - m * (s_ref[3:4, c] + unit * s_ref[4:5, c])
                )
                fin_ref[j, :, c] = value.astype(BF)

        back = None
        for k in range(weight.count):
            left = fin_ref[:, :, k * middle : (k + 1) * middle].reshape(half * batch, middle)
            part = nt(left, weight.of(w_ref, k))
            back = part if back is None else back + part
        back = back.reshape(half, batch, middle)
        out_ref[...] = back
        raw = r_ref[...]
        sig, act = silu_parts(raw * sg_ref[0:1] + sg_ref[1:2])
        pre = back[:, :, 3 * group :] * m_ref[:, :group] * (sig + act * (1.0 - sig))
        pre_ref[...] = pre
        sum_ref[0] += fold(jnp.sum(pre, axis=0))
        sum_ref[1] += fold(jnp.sum(pre * (raw - sg_ref[2:3]), axis=0))

    part = row_block(half, batch, group)
    return call(
        body,
        (half,),
        (grad_total, raw_e, stats, mask, weight.array, raw_g, stats_g),
        (
            row_block(half, batch, wide),
            row_block(half, batch, wide),
            whole(stats.shape),
            whole(mask.shape),
            weight.block(),
            part,
            whole(stats_g.shape),
        ),
        (
            ((pixels, batch, wide), BF),
            ((pixels, batch, middle), F32),
            ((pixels, batch, group), F32),
            ((2, 8, group), F32),
        ),
        (row_block(half, batch, wide), row_block(half, batch, middle), part, whole((2, 8, group))),
        flops=2 * raw_e.size * middle,
        moved=raw_e.size * 10,
    )


def kernel_weight_grad(left, right, dp, fsdp, rows, first, total, into=None):
    pixels, batch, depth = left.shape
    columns = right.shape[2]
    middle = min(columns, 512)
    owners = dp * fsdp

    def body(*refs):
        a_ref, b_ref, out_ref = refs[0], refs[1], refs[-1]
        value = tn(a_ref[...].reshape(-1, depth), b_ref[...].reshape(-1, middle)).astype(BF)
        value = value.reshape(dp, fsdp, rows, middle)
        for d in range(dp):
            out_ref[:, d] = value[d]

    ins = (left, right)
    in_specs = [
        pl.BlockSpec((pixels, batch, depth), lambda k: (0, 0, 0)),
        pl.BlockSpec((pixels, batch, middle), lambda k: (0, 0, k)),
    ]
    alias = {}
    if into is not None:
        ins += (into,)
        in_specs.append(pl.BlockSpec(memory_space=pl.ANY))
        alias = {2: 0}
    return pl.pallas_call(
        body,
        grid=(columns // middle,),
        in_specs=in_specs,
        out_specs=pl.BlockSpec((fsdp, dp, rows, middle), lambda k: (0, 0, first + k, 0)),
        out_shape=jax.ShapeDtypeStruct((fsdp, dp, total, middle), BF),
        input_output_aliases=alias,
        compiler_params=pltpu.CompilerParams(
            vmem_limit_bytes=56 * 1024 * 1024, dimension_semantics=("arbitrary",)
        ),
        cost_estimate=pl.CostEstimate(
            flops=2 * left.size * columns,
            bytes_accessed=left.size * 2 + right.size * 2 + owners * rows * columns * 2,
            transcendentals=0,
        ),
    )(*ins)


def frame_rows(rows):
    return lax.broadcasted_iota(jnp.int32, (1, rows, 128), 1)


def shift_frames(value, frames):
    shape = value.shape
    value = value.reshape(-1, frames, 128)
    spot = frame_rows(frames)
    before = jnp.where(spot == 0, 0.0, pltpu.roll(value, 1, 1))
    after_ = jnp.where(spot == frames - 1, 0.0, pltpu.roll(value, frames - 1, 1))
    return before.reshape(shape), after_.reshape(shape)


def nine_taps(pad, cols, half, batch):
    for r in range(3):
        for c in range(3):
            lane = (r * 3 + c) * 128
            part = pad[r : r + half, c : c + half]
            cols[:, lane : lane + 128] = part.reshape(half * half * batch, 128)


def clear_border(pad, half):
    pad[0] = jnp.zeros_like(pad[0])
    pad[half + 1] = jnp.zeros_like(pad[0])
    pad[:, 0] = jnp.zeros_like(pad[:, 0])
    pad[:, half + 1] = jnp.zeros_like(pad[:, 0])


def kernel_motion(rows_d, stats, mask, weight, windows, half):
    pixels, batch, middle = rows_d.shape
    narrow = weight.shape[1]

    def body(d_ref, s_ref, m_ref, w_ref, act_ref, raw_ref, win_ref, sq_ref):
        for c in chunks(middle):
            al, be, m = s_ref[0:1, c], s_ref[1:2, c], m_ref[...]

            @pl.loop(0, half)
            def _(i):
                for j in range(half):
                    act = silu_parts(d_ref[i * half + j, :, c] * al + be)[1] * m
                    act_ref[i * half + j, :, c] = act.astype(BF)

        raw = nn(act_ref[...].reshape(pixels * batch, middle), w_ref[...])
        raw_ref[...] = raw.reshape(pixels, batch, narrow)
        square = jnp.zeros((batch, narrow), F32)
        sums = [jnp.zeros((batch, narrow), F32) for _ in range(9)]
        for p in range(pixels):
            value = raw_ref[p]
            square = square + value * value
            for t in range(9):
                if windows[p // half][p % half][t]:
                    sums[t] = sums[t] + value
        for t in range(9):
            win_ref[t] = sums[t]
        sq_ref[...] = square

    return call(
        body,
        (1,),
        (rows_d, stats, mask, weight),
        (whole(rows_d.shape), whole(stats.shape), whole(mask.shape), whole(weight.shape)),
        (
            (rows_d.shape, BF),
            ((pixels, batch, narrow), F32),
            ((9, batch, narrow), F32),
            ((batch, narrow), F32),
        ),
        (
            whole(rows_d.shape),
            whole((pixels, batch, narrow)),
            whole((9, batch, narrow)),
            whole((batch, narrow)),
        ),
        flops=2 * rows_d.size * narrow,
        moved=rows_d.size * 6,
    )


def kernel_group(source, extra, taps, weight, mask, index, half, frames):
    pixels, batch, middle = source.shape
    group = 128

    def body(*refs):
        if index == 1:
            x_ref, e_ref, t_ref, w_ref, m_ref, first_ref, pad_ref, raw_ref, sum_ref, cols = refs
            excited = (x_ref[...].astype(F32) * e_ref[...]).astype(BF)
            first_ref[...] = excited
            piece = first_ref[:, :, group : 2 * group].astype(F32)
        else:
            x_ref, r_ref, s_ref, t_ref, w_ref, m_ref, first_ref, pad_ref, raw_ref, sum_ref, cols = refs
            act = silu_parts(r_ref[...] * s_ref[0:1] + s_ref[1:2])[1] * m_ref[:, :group]
            first_ref[...] = act.astype(BF)
            piece = x_ref[...].astype(F32) + first_ref[...].astype(F32)
        before, after_ = shift_frames(piece, frames)
        value = t_ref[0:1] * before + t_ref[1:2] * piece + t_ref[2:3] * after_
        clear_border(pad_ref, half)
        pad_ref[1 : half + 1, 1 : half + 1] = value.astype(BF).reshape(half, half, batch, group)
        nine_taps(pad_ref, cols, half, batch)
        raw = nn(cols[...], w_ref[...]).reshape(pixels, batch, group)
        raw_ref[...] = raw
        m = m_ref[:, :group]
        sum_ref[0] = fold(jnp.sum(raw, axis=0) * m)
        sum_ref[1] = fold(jnp.sum(raw * raw, axis=0) * m)

    block = (pixels, batch, group)
    if index == 1:
        ins = (source, extra, taps, weight, mask)
        first = (source.shape, BF)
        specs = tuple(whole(a.shape) for a in ins)
    else:
        ins = (source, extra[0], extra[1], taps, weight, mask)
        first = (block, BF)
        specs = ((block, lambda i: (0, 0, index)),) + tuple(whole(a.shape) for a in ins[1:])
    outs = (
        first,
        ((half + 2, half + 2, batch, group), BF),
        (block, F32),
        ((2, 8, group), F32),
    )
    return call(
        body,
        (1,),
        ins,
        specs,
        outs,
        tuple(whole(o[0]) for o in outs),
        scratch=[pltpu.VMEM((pixels * batch, 9 * group), BF)],
        flops=2 * pixels * batch * 9 * group * group,
        moved=pixels * batch * group * 12,
    )


def kernel_group_weights(pad, grad, half):
    pixels, batch, group = grad.shape

    def body(p_ref, g_ref, out_ref, cols):
        nine_taps(p_ref, cols, half, batch)
        out_ref[...] = tn(cols[...], g_ref[...].reshape(pixels * batch, group)).astype(BF)

    return call(
        body,
        (1,),
        (pad, grad),
        (whole(pad.shape), whole(grad.shape)),
        (((9 * group, group), BF),),
        (whole((9 * group, group)),),
        scratch=[pltpu.VMEM((pixels * batch, 9 * group), BF)],
        flops=2 * grad.size * 9 * group,
        moved=grad.size * 6,
    )[0]


def kernel_group_back(
    grad, raw, stats, weight, taps, excited, previous, joined, lower, mask, index, half, frames
):
    pixels, batch, group = grad.shape
    block = (pixels, batch, group)
    rows = pixels * batch

    def body(*refs):
        g_ref, r_ref, s_ref, w_ref, t_ref, x_ref, j_ref, m_ref = refs[:8]
        pad, cols = refs[-2:]
        m = m_ref[:, :group]
        raw = r_ref[...]
        value = s_ref[0:1] * g_ref[...] - m * (s_ref[2:3] + (raw - s_ref[1:2]) * s_ref[3:4])
        if index > 1:
            p_ref, l_ref, ls_ref, gg_ref, gp_ref, tg_ref, pre_ref, sum_ref = refs[8:16]
        else:
            g2_ref, g3_ref, d_ref, gg_ref, gp_ref, tg_ref, at_ref = refs[8:15]
        gg_ref[...] = value.astype(BF)
        clear_border(pad, half)
        pad[1 : half + 1, 1 : half + 1] = gg_ref[...].reshape(half, half, batch, group)
        nine_taps(pad, cols, half, batch)
        back = nn(cols[...], w_ref[...]).reshape(block)
        before, after_ = shift_frames(back, frames)
        below = t_ref[0:1] * after_ + t_ref[1:2] * back + t_ref[2:3] * before
        gp_ref[...] = below
        piece = x_ref[...].astype(F32)
        if index > 1:
            piece = piece + p_ref[...].astype(F32)
        tg_ref[0] = fold(jnp.sum(after_ * piece, axis=0))
        tg_ref[1] = fold(jnp.sum(back * piece, axis=0))
        tg_ref[2] = fold(jnp.sum(before * piece, axis=0))
        if index > 1:
            raw = l_ref[...]
            sig, act = silu_parts(raw * ls_ref[0:1] + ls_ref[1:2])
            pre = (j_ref[...] + below) * m * (sig + act * (1.0 - sig))
            pre_ref[...] = pre
            sum_ref[0] = fold(jnp.sum(pre, axis=0))
            sum_ref[1] = fold(jnp.sum(pre * (raw - ls_ref[2:3]), axis=0))
        else:
            for k, source in enumerate((j_ref, gp_ref, g2_ref, g3_ref)):
                span = slice(k * group, (k + 1) * group)
                at_ref[:, span] = jnp.sum(source[...] * d_ref[:, :, span].astype(F32), axis=0)

    column = lambda k: (block, lambda i: (0, 0, k))
    ins = [grad, raw, stats, weight, taps, excited, joined, mask]
    specs = [whole(a.shape) for a in ins]
    specs[5] = column(index)
    specs[6] = column(index - 1)
    outs = [(block, BF), (block, F32), ((3, 8, group), F32)]
    if index > 1:
        more = [previous, lower[0], lower[1]]
        outs += [(block, F32), ((2, 8, group), F32)]
    else:
        more = list(previous)
        outs += [((batch, 4 * group), F32)]
    return call(
        body,
        (1,),
        ins + more,
        specs + [whole(a.shape) for a in more],
        outs,
        [whole(o[0]) for o in outs],
        scratch=[
            pltpu.VMEM((half + 2, half + 2, batch, group), BF),
            pltpu.VMEM((rows, 9 * group), BF),
        ],
        flops=2 * rows * 9 * group * group,
        moved=rows * group * 24,
    )


def kernel_motion_back(
    joined, pieces, attend, rows_d, stats_d, raw_m, kmap, change, stats_m, weight, mask, half
):
    pixels, batch, middle = rows_d.shape
    narrow = raw_m.shape[2]
    group = middle // 4

    def body(j_ref, p1, p2, p3, e_ref, d_ref, sd_ref, r_ref, k_ref, c_ref, sm_ref, w_ref, m_ref, out_ref, mg_ref, sum_ref):
        zero_first(sum_ref)
        mn = m_ref[:, :narrow]
        grad = (k_ref[...] * c_ref[0] - c_ref[1]) * mn
        value = sm_ref[0:1] * grad - mn * (sm_ref[2:3] + (r_ref[...] - sm_ref[1:2]) * sm_ref[3:4])
        mg_ref[...] = value.astype(BF)
        back = nt(mg_ref[...].reshape(half * batch, narrow), w_ref[...])
        back = back.reshape(half, batch, middle)
        m = m_ref[:, :group]
        for k, ref in enumerate((j_ref, p1, p2, p3)):
            c = slice(k * group, (k + 1) * group)
            raw = d_ref[:, :, c]
            sig, act = silu_parts(raw * sd_ref[0:1, c] + sd_ref[1:2, c])
            out = (ref[...] * e_ref[:, c] + back[:, :, c]) * m * (sig + act * (1.0 - sig))
            out_ref[:, :, c] = out
            sum_ref[0, :, c] += fold(jnp.sum(out, axis=0))
            sum_ref[1, :, c] += fold(jnp.sum(out * (raw - sd_ref[2:3, c]), axis=0))

    part = row_block(half, batch, group)
    ins = (joined,) + tuple(pieces)
    ins += (attend, rows_d, stats_d, raw_m, kmap, change, stats_m, weight, mask)
    return call(
        body,
        (half,),
        ins,
        (
            part,
            part,
            part,
            part,
            whole(attend.shape),
            row_block(half, batch, middle),
            whole(stats_d.shape),
            row_block(half, batch, narrow),
            ((half, 1, narrow), lambda i: (i, 0, 0)),
            whole(change.shape),
            whole(stats_m.shape),
            whole(weight.shape),
            whole(mask.shape),
        ),
        (
            ((pixels, batch, middle), F32),
            ((pixels, batch, narrow), BF),
            ((2, 8, middle), F32),
        ),
        (row_block(half, batch, middle), row_block(half, batch, narrow), whole((2, 8, middle))),
        flops=2 * rows_d.size * narrow,
        moved=rows_d.size * 12,
    )


class Sums:
    def __init__(self, dp, fsdp):
        self.devices = dp * fsdp
        half = self.devices // 2
        self.groups = [[2 * i + c for i in range(half)] for c in range(2)]
        self.swap = [(i, i ^ 1) for i in range(self.devices)]

    def flat(self, values):
        size = values.shape[0]
        if size <= 2048:
            copies = jnp.broadcast_to(values[None], (self.devices, size))
            return jnp.sum(lax.all_to_all(copies, AXES, 0, 0), axis=0)
        core = lax.axis_index("fsdp") % 2
        halves = values.reshape(2, size // 2)
        mine = lax.dynamic_index_in_dim(halves, core, 0, False)
        other = lax.dynamic_index_in_dim(halves, 1 - core, 0, False)
        mine = mine + lax.ppermute(other, AXES, self.swap)
        copies = jnp.broadcast_to(mine[None], (self.devices // 2, size // 2))
        mine = jnp.sum(lax.all_to_all(copies, AXES, 0, 0, axis_index_groups=self.groups), axis=0)
        other = lax.ppermute(mine, AXES, self.swap)
        low = jnp.where(core == 0, mine, other)
        high = jnp.where(core == 0, other, mine)
        return jnp.concatenate([low, high])

    def __call__(self, *arrays):
        sizes = [a.size for a in arrays]
        extra = -sum(sizes) % 256
        parts = [a.reshape(-1) for a in arrays]
        if extra:
            parts.append(jnp.zeros((extra,), F32))
        merged = self.flat(jnp.concatenate(parts))
        out, begin = [], 0
        for a, size in zip(arrays, sizes):
            out.append(merged[begin : begin + size].reshape(a.shape))
            begin += size
        return out


def pairs_of(dp, fsdp):
    return [(i, i ^ 1) for i in range(dp * fsdp)]


def same_core(fsdp):
    return [[2 * i + c for i in range(fsdp // 2)] for c in range(2)]


def quick_gather(dp, fsdp, value):
    value = lax.all_to_all(jnp.broadcast_to(value[None], (dp,) + value.shape), "dp", 0, 0)
    value = lax.all_to_all(
        jnp.broadcast_to(value[None], (fsdp // 2,) + value.shape),
        "fsdp",
        0,
        0,
        axis_index_groups=same_core(fsdp),
    )
    other = lax.ppermute(value, AXES, pairs_of(dp, fsdp))
    core = lax.axis_index("fsdp") % 2
    low = jnp.where(core == 0, value, other)
    high = jnp.where(core == 0, other, value)
    both = jnp.stack([low, high], axis=2).swapaxes(0, 1)
    return both.reshape((dp * fsdp,) + both.shape[3:])


def quick_scatter(dp, fsdp, value):
    shape = value.shape[1:]
    value = value.astype(BF).reshape((dp, fsdp // 2, 2) + shape).transpose(2, 1, 0, 3, 4)
    core = lax.axis_index("fsdp") % 2
    mine = lax.dynamic_index_in_dim(value, core, 0, False)
    other = lax.dynamic_index_in_dim(value, 1 - core, 0, False)
    other = lax.ppermute(other, AXES, pairs_of(dp, fsdp))
    value = (mine.astype(F32) + other.astype(F32)).astype(BF)
    value = lax.all_to_all(value, "fsdp", 0, 0, axis_index_groups=same_core(fsdp))
    value = jnp.sum(value.astype(F32), axis=0).astype(BF)
    return jnp.sum(lax.all_to_all(value, "dp", 0, 0).astype(F32), axis=0)


def after(value, *others):
    return lax.optimization_barrier((value, others))[0]


def affine(total, square, count, gain, bias):
    mean = total / count
    inv = lax.rsqrt(square / count - mean * mean + EPSILON)
    alpha = gain * inv
    return mean, inv, alpha, bias - mean * alpha


def local(
    dp,
    fsdp,
    clip_count,
    frame_count,
    frame_mask,
    features,
    w_reduce1,
    w_spatial1,
    w_expand1,
    w_project1,
    w_reduce2,
    w_motion_in,
    w_motion_out,
    w_spatial2,
    w_expand2,
    gains,
    biases,
    motion_taps,
    temporal_taps,
    cotangent,
):
    devices = dp * fsdp
    sums = Sums(dp, fsdp)
    slots, frames, height = features.shape[:3]
    half = height // 2
    area = half * half
    c_in = features.shape[-1]
    middle = w_reduce1.shape[1]
    group = middle // 4
    wide = w_expand1.shape[1]
    narrow = w_motion_in.shape[1]
    valid = (
        (jnp.arange(slots)[:, None] < clip_count[0])
        & (jnp.arange(frames)[None, :] < frame_count[:, None])
        & (frame_mask == 1)
    ).astype(F32)
    mask = valid[None, None, :, :, None]
    mask_rows = jnp.broadcast_to(valid.reshape(-1, 1), (slots * frames, 256))
    fmask = valid[:, :, None]
    widths = [middle, middle, wide, wide, middle, narrow, middle, group, group, group, wide]
    starts = [sum(widths[:k]) for k in range(len(widths))]
    gain = [gains[s : s + w] for s, w in zip(starts, widths)]
    bias = [biases[s : s + w] for s, w in zip(starts, widths)]

    feats = features.transpose(0, 2, 3, 1, 4).reshape(-1, c_in)
    cot = cotangent.transpose(2, 3, 0, 1, 4)

    def gather(value):
        return lax.all_gather(value, AXES, axis=0, tiled=False)

    def rows_of(value):
        return jnp.pad(value, ((0, 0), (0, -value.shape[1] % middle))).reshape(
            value.shape[0], -1, middle
        )

    def columns_of(value):
        rows = value.shape[0]
        return value.reshape(rows, -1, middle).swapaxes(0, 1).reshape(-1, middle)

    own = middle // devices
    full_reduce1 = quick_gather(dp, fsdp, w_reduce1).reshape(c_in, middle)
    rows1, rowsp, rows2 = w_expand1.shape[0], w_project1.shape[0], w_reduce2.shape[0]
    blocks = wide // middle
    aligned = own % 16 == 0

    def gather_packed(*parts):
        value = gather(jnp.concatenate([part[0] for part in parts]))
        begin, flat, places = 0, [], []
        for part, rows, count in parts:
            places.append((rows * (1 if aligned else devices), begin // rows, count))
            mine = value[:, begin : begin + part.shape[0]]
            flat.append(mine.reshape(devices, -1, rows, middle).swapaxes(0, 1).reshape(-1, middle))
            begin += part.shape[0]
        array = value if aligned else jnp.concatenate(flat)[None]
        return [Packed(array, *place) for place in places]

    project1, expand1, reduce2, spatial1 = gather_packed(
        (columns_of(w_project1), rowsp, blocks),
        (columns_of(w_expand1), rows1, blocks),
        (w_reduce2, rows2, 1),
        (w_spatial1.reshape(-1, middle), own, 1),
    )
    taps1 = [Packed(spatial1.array, spatial1.rows, spatial1.first + t, 1) for t in range(9)]
    smalls = jnp.concatenate(
        [w_spatial2.reshape(1, -1), w_motion_in.reshape(1, -1), w_motion_out.reshape(1, -1)], axis=1
    )
    rowse = w_expand2.shape[0]
    late_rows = columns_of(w_expand2).shape[0]
    smalls = rows_of(smalls)[0]
    expand2, tail = gather_packed(
        (columns_of(w_expand2), rowse, blocks), (smalls, 1, smalls.shape[0])
    )
    if aligned:
        flat_small = tail.array[:, late_rows:].reshape(devices, -1)
    else:
        flat_small = (
            tail.array[0, late_rows * devices :]
            .reshape(-1, devices, middle)
            .swapaxes(0, 1)
            .reshape(devices, -1)
        )
    batch = slots * frames
    pixel_rows = (area, batch)
    size_s, size_m = w_spatial2.size, w_motion_in.size
    kernels = (
        flat_small[:, :size_s].reshape(devices, 27, -1).swapaxes(0, 1).reshape(3, 9, group, group)
    )
    small = flat_small[:, size_s : size_s + 2 * size_m].reshape(devices, 2, own, narrow)
    full_motion_in = small[:, 0].reshape(middle, narrow)
    full_motion_out = small[:, 1].reshape(middle, narrow).astype(F32)

    raw_a, sums_a = kernel_reduce1(feats, full_reduce1, mask_rows, slots, height, frames)
    sum_a, square_a, frame_total, pairs = sums(
        jnp.sum(sums_a[0], axis=0),
        jnp.sum(sums_a[1], axis=0),
        jnp.sum(valid),
        jnp.sum(valid[:, :-1] * valid[:, 1:]),
    )
    count_big = frame_total * (height * height)
    count = frame_total * area
    mean_a, inv_a, alpha_a, beta_a = affine(sum_a, square_a, count_big, gain[0], bias[0])
    act_a, raw_b, sums_b = kernel_conv_down(raw_a, alpha_a[None], beta_a[None], mask_rows, taps1)
    raw_b = raw_b.reshape(area, batch, middle)
    sampled = (
        features.reshape(slots, frames, half, 2, half, 2, c_in)[:, :, :, 0, :, 0]
        .transpose(2, 3, 0, 1, 4)
        .reshape(area, batch, c_in)
    )
    raw_p, sums_p = kernel_project(sampled, mask_rows, project1, half)

    def moments(raw):
        return total_over(raw * mask), total_over(raw * raw * mask)

    sum_b, square_b = sums(jnp.sum(sums_b[0], axis=0), jnp.sum(sums_b[1], axis=0))
    mean_b, inv_b, alpha_b, beta_b = affine(sum_b, square_b, count, gain[1], bias[1])
    act_b, raw_c, sums_c = kernel_expand(
        raw_b, jnp.stack([alpha_b, beta_b]), mask_rows, expand1, half
    )
    sums_c, sums_p = jnp.sum(sums_c, axis=1), jnp.sum(sums_p, axis=1)
    sum_c, square_c, sum_p, square_p = sums(sums_c[0], sums_c[1], sums_p[0], sums_p[1])
    mean_c, inv_c, alpha_c, beta_c = affine(sum_c, square_c, count, gain[2], bias[2])
    mean_p, inv_p, alpha_p, beta_p = affine(sum_p, square_p, count, gain[3], bias[3])
    stats_one = jnp.stack(
        [alpha_c, alpha_p, beta_c + beta_p, mean_c, inv_c, mean_p, inv_p, jnp.zeros_like(mean_p)]
    )
    block_one, rows_d, sums_d = kernel_block_one(
        raw_c, raw_p, stats_one, mask_rows, reduce2, half
    )

    sum_d, square_d = sums(jnp.sum(sums_d[0], axis=0), jnp.sum(sums_d[1], axis=0))
    mean_d, inv_d, alpha_d, beta_d = affine(sum_d, square_d, count, gain[4], bias[4])
    inside = [
        [
            [int(0 <= y - r + 1 < half and 0 <= x - c + 1 < half) for r in range(3) for c in range(3)]
            for x in range(half)
        ]
        for y in range(half)
    ]
    windows = jnp.array(inside, F32)
    act_d, raw_m, in_window, square_rows = kernel_motion(
        rows_d, jnp.stack([alpha_d, beta_d]), mask_rows, full_motion_in, inside, half
    )
    in_window = in_window.reshape(9, slots, frames, narrow)
    kmap = jnp.sum(windows[..., None] * motion_taps, axis=2)
    ksum = jnp.sum(kmap, axis=(0, 1))
    mapped = jnp.sum(in_window * motion_taps[:, None, None, :], axis=0)
    plain = in_window[4]
    vnext = later(fmask)
    pool_raw = (vnext / area) * (later(mapped * fmask) - fmask * plain)
    pool_one = (vnext / area) * (later(fmask) * ksum - fmask * area)
    flat_raw = pool_raw.reshape(-1, narrow)
    flat_valid = valid.reshape(-1, 1)
    gram = lax.dot_general(
        flat_raw * flat_valid, flat_raw, (((0,), (0,)), ((), ())), precision=HIGHEST
    )
    sum_m, square_m, pool_a, gram_aa = sums(
        total_over(plain * fmask),
        total_over(square_rows.reshape(plain.shape) * fmask),
        jnp.sum(flat_raw * flat_valid, axis=0), gram
    )
    mean_m, inv_m, alpha_m, beta_m = affine(sum_m, square_m, count, gain[5], bias[5])
    step = ksum / area - 1.0
    pool_b = pairs * step
    gram_ab = pool_a[:, None] * step[None, :]
    gram_bb = pairs * step[:, None] * step[None, :]
    pooled = alpha_m * pool_raw + beta_m * pool_one
    lifted = jnp.einsum("cfr,or->cfo", pooled, full_motion_out, precision=HIGHEST)
    gram_p = (
        alpha_m[:, None] * alpha_m * gram_aa
        + alpha_m[:, None] * beta_m * gram_ab
        + beta_m[:, None] * alpha_m * gram_ab.T
        + beta_m[:, None] * beta_m * gram_bb
    )
    sum_x = jnp.dot(full_motion_out, alpha_m * pool_a + beta_m * pool_b, precision=HIGHEST)
    square_x = jnp.sum(jnp.dot(full_motion_out, gram_p, precision=HIGHEST) * full_motion_out, axis=1)
    mean_x, inv_x, alpha_x, beta_x = affine(sum_x, square_x, frame_total, gain[6], bias[6])
    sigma = jax.nn.sigmoid(lifted * alpha_x + beta_x)
    attend1 = 2.0 * sigma
    attend_rows = attend1.reshape(batch, middle)
    tap_rows = [temporal_taps[k] for k in range(3)]
    excited, pad, raw, partial = kernel_group(
        act_d, attend_rows, tap_rows[0], kernels[0].reshape(-1, group), mask_rows, 1, half, frames
    )
    pads, raws, stats, outputs = [pad], [raw], [], []
    for k in range(3):
        total = jnp.sum(partial, axis=1)
        stats.append(affine(*sums(total[0], total[1]), count, gain[7 + k], bias[7 + k]))
        if k < 2:
            out, pad, raw, partial = kernel_group(
                excited,
                (raws[k], jnp.stack(stats[k][2:])),
                tap_rows[k + 1],
                kernels[k + 1].reshape(-1, group),
                mask_rows,
                k + 2,
                half,
                frames,
            )
            pads.append(pad)
            raws.append(raw)
            outputs.append(out)
    joined, raw_e, sums_e = kernel_join(
        excited, outputs, raws[2], jnp.stack(stats[2][2:]), mask_rows, expand2, half
    )
    sums_e = jnp.sum(sums_e, axis=1)
    mean_e, inv_e, alpha_e, beta_e = affine(
        *sums(sums_e[0], sums_e[1]), count, gain[10], bias[10]
    )
    def by_owner(values, number):
        return (
            values.astype(BF)
            .reshape(dp, fsdp, -1, number, middle)
            .transpose(1, 0, 3, 2, 4)
            .reshape(fsdp, dp, -1, middle)
        )

    shifts = [None] * 11
    spreads = [None] * 11

    def grad_raw(index, grad, raw, mean, inv, weight, number):
        unit = (raw - mean) * inv
        return gain[index] * inv * (grad - weight * (shifts[index] + unit * spreads[index]) / number)

    result, grad_total, sums_e = kernel_result(
        raw_e,
        block_one,
        cot.reshape(area, batch, wide),
        jnp.stack([alpha_e, beta_e, mean_e, inv_e]),
        mask_rows,
        half,
    )
    result = result.reshape(half, half, slots, frames, wide)
    shifts[10], spreads[10] = sums(jnp.sum(sums_e[0], axis=0), jnp.sum(sums_e[1], axis=0))

    def back_stats(index, mean, inv):
        scale = gain[index] * inv
        return [scale, mean, inv, shifts[index] / count, spreads[index] / count]

    def lower(k):
        return raws[k], jnp.stack([stats[k][2], stats[k][3], stats[k][0]])

    flipped = [kernels[k][::-1].transpose(0, 2, 1).reshape(9 * group, group) for k in range(3)]
    final_grad, grad_joined, grad_pre, partial = kernel_final_back(
        grad_total,
        raw_e,
        jnp.stack(back_stats(10, mean_e, inv_e)),
        mask_rows,
        expand2,
        *lower(2),
        half,
    )
    kernel_grads = [None] * 3
    temporal_grads = [None] * 3
    grad_pieces = [None] * 3
    for k in (2, 1, 0):
        mean, inv, alpha, _ = stats[k]
        partial = jnp.sum(partial, axis=1)
        shifts[7 + k], spreads[7 + k] = sums(partial[0], partial[1] * inv)
        got = kernel_group_back(
            grad_pre,
            raws[k],
            jnp.stack(
                [alpha, mean, alpha * shifts[7 + k] / count, alpha * inv * spreads[7 + k] / count]
            ),
            flipped[k],
            tap_rows[k],
            excited,
            outputs[k - 1] if k else (grad_pieces[1], grad_pieces[2], act_d),
            grad_joined,
            lower(k - 1) if k else None,
            mask_rows,
            k + 1,
            half,
            frames,
        )
        group_grad, grad_pieces[k], sums_t = got[:3]
        if k:
            grad_pre, partial = got[3:]
        else:
            grad_attend = got[3].reshape(slots, frames, middle)
        temporal_grads[k] = jnp.sum(sums_t, axis=1)
        kernel_grads[k] = kernel_group_weights(pads[k], group_grad, half)
    grad_kernels = rows_of(
        jnp.stack(kernel_grads).reshape(27, devices, -1).swapaxes(0, 1).astype(BF).reshape(devices, -1)
    )
    total_a = blocks * rowse + grad_kernels.shape[1]
    total_a += -total_a % 16
    if aligned:
        packed_a = kernel_weight_grad(joined, final_grad, dp, fsdp, rowse, 0, total_a)
        packed_a = lax.dynamic_update_slice(
            packed_a,
            grad_kernels.reshape(dp, fsdp, -1, middle).swapaxes(0, 1),
            (0, 0, blocks * rowse, 0),
        )
    else:
        packed_a = jnp.concatenate(
            [
                by_owner(weight_grad(joined, final_grad), blocks),
                grad_kernels.reshape(dp, fsdp, -1, middle).swapaxes(0, 1),
            ],
            axis=2,
        )
        packed_a = jnp.pad(
            packed_a, ((0, 0), (0, 0), (0, total_a - packed_a.shape[2]), (0, 0))
        )
    grad_attend, packed_a = lax.optimization_barrier((grad_attend, packed_a))
    mine_a = lax.psum_scatter(
        packed_a.reshape(-1, middle), "fsdp", scatter_dimension=0, tiled=True
    )
    grad_x = grad_attend * 2.0 * sigma * (1.0 - sigma)
    unit_x = (lifted - mean_x) * inv_x
    pool_unit = (pool_raw - mean_m * pool_one) * inv_m
    grad_e = jnp.einsum("cfo,or->cfr", grad_x, full_motion_out * alpha_x[:, None], precision=HIGHEST)
    shifts[6], spreads[6], first_t, second_t = sums(
        jnp.sum(grad_x, axis=(0, 1)),
        jnp.sum(grad_x * unit_x, axis=(0, 1)),
        jnp.sum(grad_e * pool_one, axis=(0, 1)),
        jnp.sum(grad_e * pool_unit, axis=(0, 1)),
    )
    lift_b = jnp.dot(
        full_motion_out, alpha_m[:, None] * gram_ab + beta_m[:, None] * gram_bb, precision=HIGHEST
    )
    lift_a = jnp.dot(
        full_motion_out, alpha_m[:, None] * gram_aa + beta_m[:, None] * gram_ab.T, precision=HIGHEST
    )
    unit_b = inv_x[:, None] * (lift_b - mean_x[:, None] * pool_b)
    unit_a = inv_x[:, None] * (lift_a - mean_x[:, None] * pool_a)
    unit_u = (unit_a - unit_b * mean_m) * inv_m
    pool_u = (pool_a - pool_b * mean_m) * inv_m
    back_x = full_motion_out * alpha_x[:, None]
    shifts[5] = first_t - jnp.sum(
        back_x * (shifts[6][:, None] * pool_b + spreads[6][:, None] * unit_b), axis=0
    ) / frame_total
    spreads[5] = second_t - jnp.sum(
        back_x * (shifts[6][:, None] * pool_u + spreads[6][:, None] * unit_u), axis=0
    ) / frame_total
    grad_lifted = alpha_x * (grad_x - fmask * (shifts[6] + unit_x * spreads[6]) / frame_total)
    grad_motion_out = jnp.einsum("cfo,cfr->or", grad_lifted, pooled, precision=HIGHEST)
    grad_pooled = jnp.einsum("cfo,or->cfr", grad_lifted, full_motion_out, precision=HIGHEST)
    grad_change = grad_pooled * vnext / area
    reduced_windows = later(
        fmask * (alpha_m * in_window + beta_m * jnp.sum(windows, axis=(0, 1))[:, None, None, None])
    )
    motion_tap_grad = jnp.sum(grad_change * reduced_windows, axis=(1, 2))
    grad_narrow, motion_grad, sums_narrow = kernel_motion_back(
        grad_joined,
        grad_pieces,
        attend_rows,
        rows_d,
        jnp.stack([alpha_d, beta_d, mean_d]),
        raw_m,
        kmap.reshape(area, 1, narrow),
        jnp.stack([earlier(grad_change), grad_change]).reshape(2, batch, narrow),
        jnp.stack(
            [alpha_m, mean_m, alpha_m * shifts[5] / count, alpha_m * inv_m * spreads[5] / count]
        ),
        full_motion_in,
        mask_rows,
        half,
    )
    grad_motion_in = weight_grad(act_d, motion_grad)
    sums_narrow = jnp.sum(sums_narrow, axis=1)
    shifts[4], spreads[4] = sums(sums_narrow[0], sums_narrow[1] * inv_d)
    small_grads = jnp.concatenate(
        [grad_motion_in.reshape(devices, -1), grad_motion_out.reshape(devices, -1)], axis=1
    )
    narrow_grad, grad_one, sums_one = kernel_block_back(
        grad_narrow,
        rows_d,
        jnp.stack(back_stats(4, mean_d, inv_d)),
        reduce2,
        grad_total,
        raw_c,
        raw_p,
        stats_one,
        mask_rows,
        half,
    )
    sums_one, mine_a = lax.optimization_barrier((sums_one, mine_a))
    mine_a = lax.psum_scatter(mine_a, "dp", scatter_dimension=0, tiled=True)
    sums_one = jnp.sum(sums_one, axis=1)
    shifts[2], spreads[2], spreads[3] = sums(sums_one[0], sums_one[1], sums_one[2])
    shifts[3] = shifts[2]
    widen_grad, shortcut_grad, grad_strided, sums_strided = kernel_expand_back(
        grad_one,
        raw_c,
        raw_p,
        jnp.stack(back_stats(2, mean_c, inv_c) + back_stats(3, mean_p, inv_p)),
        expand1,
        raw_b,
        jnp.stack([alpha_b, beta_b, mean_b, inv_b]),
        mask_rows,
        half,
    )
    if aligned:
        total = blocks * (rowsp + rows1) + rows2
        packed_b = kernel_weight_grad(
            block_one, narrow_grad, dp, fsdp, rows2, total // rows2 - 1, total
        )
        packed_b = kernel_weight_grad(
            act_b, widen_grad, dp, fsdp, rows1, blocks * rowsp // rows1, total, packed_b
        )
        packed_b = kernel_weight_grad(
            sampled, shortcut_grad, dp, fsdp, rowsp, 0, total, packed_b
        )
    else:
        packed_b = jnp.concatenate(
            [
                by_owner(weight_grad(sampled, shortcut_grad), blocks),
                by_owner(weight_grad(act_b, widen_grad), blocks),
                by_owner(weight_grad(block_one, narrow_grad), 1),
            ],
            axis=2,
        )
    sums_strided, packed_b, mine_a = lax.optimization_barrier((sums_strided, packed_b, mine_a))

    def columns_back(value, rows):
        return value.reshape(blocks, rows, middle).swapaxes(0, 1).reshape(rows, wide)

    mine_a = mine_a.astype(F32)
    own_expand2 = columns_back(mine_a[: blocks * rowse], rowse)
    own_kernels = mine_a[blocks * rowse :].reshape(-1)[:size_s]
    mine_b = packed_b.reshape(-1, middle)
    mine_b = lax.psum_scatter(mine_b, "fsdp", scatter_dimension=0, tiled=True)
    mine_b = lax.psum_scatter(mine_b, "dp", scatter_dimension=0, tiled=True).astype(F32)
    cut1 = blocks * rowsp
    cut2 = cut1 + blocks * rows1
    own_project1 = columns_back(mine_b[:cut1], rowsp)
    own_expand1 = columns_back(mine_b[cut1:cut2], rows1)
    own_reduce2 = mine_b[cut2:]
    grad_sampled = kernel_sampled_back(shortcut_grad, project1, half)
    shifts[1], spreads[1] = sums(jnp.sum(sums_strided[0], axis=0), jnp.sum(sums_strided[1], axis=0))
    strided_grad = grad_raw(
        1, grad_strided, raw_b, mean_b, inv_b, mask_rows[:, :1], count
    ).astype(BF)
    strided_grad = strided_grad.reshape(half, half, batch, middle)
    grad_spatial1 = kernel_conv_down_weights(act_a, strided_grad)
    strided_grad, grad_spatial1 = lax.optimization_barrier((strided_grad, grad_spatial1))
    own_spatial1 = quick_scatter(
        dp,
        fsdp,
        jnp.concatenate(
            [
                grad_spatial1.reshape(9, devices, own, middle)
                .swapaxes(0, 1)
                .reshape(devices, 9 * own, middle),
                rows_of(small_grads.astype(BF)),
            ],
            axis=1,
        ),
    )
    own_motion = own_spatial1[9 * own :].reshape(-1)[: 2 * size_m].reshape(2, own, narrow)
    own_spatial1 = own_spatial1[: 9 * own]
    grad_first, sums_first = kernel_conv_down_back(
        strided_grad,
        taps1,
        raw_a,
        jnp.stack([alpha_a, beta_a, mean_a, inv_a]),
        mask_rows,
    )
    shifts[0], spreads[0], motion_total, temporal_total = sums(
        jnp.sum(sums_first[0], axis=0),
        jnp.sum(sums_first[1], axis=0),
        motion_tap_grad,
        jnp.stack(temporal_grads),
    )
    first_grad, grad_reduce1 = kernel_first_grad(
        grad_first,
        raw_a,
        feats,
        jnp.stack([alpha_a, mean_a, inv_a, shifts[0] / count_big, spreads[0] / count_big]),
        mask_rows,
        slots,
        frames,
    )
    own_reduce1 = quick_scatter(dp, fsdp, grad_reduce1.reshape(devices, -1, middle))
    grad_features = kernel_grad_features(
        first_grad,
        full_reduce1,
        grad_sampled.reshape(half, half, slots * frames, c_in),
        height,
        slots,
        frames,
    )
    grad_features = grad_features.reshape(slots, height, height, frames, c_in)
    return (
        result.transpose(2, 3, 0, 1, 4),
        grad_features.transpose(0, 3, 1, 2, 4),
        own_reduce1,
        own_spatial1.reshape(9, own * middle),
        own_expand1,
        own_project1,
        own_reduce2,
        own_motion[0],
        own_motion[1],
        own_kernels.reshape(27, -1),
        own_expand2,
        jnp.concatenate(spreads),
        jnp.concatenate(shifts),
        motion_total,
        temporal_total,
    )


def solution(mesh):
    dp, fsdp = mesh.shape["dp"], mesh.shape["fsdp"]

    def run(*arrays):
        return local(dp, fsdp, *arrays)

    rows = P(AXES, None)
    columns = P(None, AXES)
    clips = P(AXES, None, None, None, None)
    return jax.shard_map(
        run,
        mesh=mesh,
        in_specs=(
            P(AXES),
            P(AXES),
            rows,
            clips,
            rows,
            columns,
            rows,
            rows,
            rows,
            rows,
            rows,
            columns,
            rows,
            P(),
            P(),
            P(),
            P(),
            clips,
        ),
        out_specs=(
            clips,
            clips,
            rows,
            columns,
            rows,
            rows,
            rows,
            rows,
            rows,
            columns,
            rows,
            P(),
            P(),
            P(),
            P(),
        ),
        check_vma=False,
    )
```

time: 1190 us -> 809 us (0.68)
  Pallas kernels: 0 us -> 340 us
  waiting for transfers between devices: 410 us -> 145 us
  matrix products: 230 us -> 8.09 us
  local copies, waits for them, and re-layouts: 242 us -> 88 us
  other arithmetic: 188 us -> 58.1 us
  blocking collectives: 0 us -> 71.5 us
  starting transfers between devices: 83.4 us -> 67 us
    pallas_call x0 -> x30, Pallas kernels: none -> 340 us  [the longest x26 304 us: call(): pl.pallas_call(body, grid=grid, in_specs=[spec(b) for b in in_blocks], ou...]
    reduce_scatter x6 -> x4, waiting for transfers between devices: 163 us -> 0.04 us  [the longest x1 0.02 us: local(): lax.psum_scatter(packed_a.reshape(-1, middle), 'fsdp', scatter_dimension=...]
    dot_general x23 -> x0, matrix products: 148 us -> none  [the longest x10 77.5 us: dot_t(): lax.dot_general(grad.reshape(-1, shape[-1]), weight, (((1,), (1,)), ((),...]
    all_gather x4 -> x2, waiting for transfers between devices: 123 us -> 42.7 us  [gather(): return lax.all_gather(value, AXES, axis=0, tiled=False)]
    convert_element_type x23 -> x3, other arithmetic: 83.4 us -> 8.14 us  [the longest x1 4.08 us: local(): strided_grad = grad_raw(1, grad_strided, raw_b, mean_b, inv_b, mask_rows[...]
    all_to_all x0 -> x6, blocking collectives: none -> 71.5 us  [the longest x3 40.2 us: flat(): lax.all_to_all(copies, AXES, 0, 0, axis_index_groups=self.groups)]
    dot_general x10 -> x1, matrix products: 74.3 us -> 2.9 us  [weight_grad(): lax.dot_general(left.reshape(-1, left.shape[-1]), grad.reshape(-1, grad.s...]
    unnamed x606 -> x136, local copies, waits for them, and re-layouts: 68.4 us -> 5.26 us
  transfers between devices with their start and end apart: 39 -> 37, of which waited for: 26 -> 25; matrix products, arithmetic and copies ran while one was open for 30% -> 13% of each run, Pallas kernels for 0% -> 32%
where the time goes in v1:
time: 809 us; the launch traced here: 796 us
  Pallas kernels  340 us (42%)
  waiting for transfers between devices  145 us (18%)
  local copies, waits for them, and re-layouts  88 us (11%)
  blocking collectives  71.5 us (9%)
  starting transfers between devices  67 us (8%)
  other arithmetic  58.1 us (7%)
  between operations  18.1 us (2%)
  matrix products  8.09 us (1%)
    pallas_call x26, Pallas kernels, call(): pl.pallas_call(body, grid=grid, in_specs=[spec(b) for b in in_blocks], ou...  304 us
    all_to_all x11, waiting for transfers between devices, flat(): return jnp.sum(lax.all_to_all(copies, AXES, 0, 0), axis=0)  45.5 us
    all_gather x2, waiting for transfers between devices, gather(): return lax.all_gather(value, AXES, axis=0, tiled=False)  42.7 us
    all_to_all x3, blocking collectives, flat(): lax.all_to_all(copies, AXES, 0, 0, axis_index_groups=self.groups)  40.2 us
    all_to_all x11, starting transfers between devices, flat(): return jnp.sum(lax.all_to_all(copies, AXES, 0, 0), axis=0)  36.9 us
    pallas_call x4, Pallas kernels, kernel_weight_grad(): pl.pallas_call(body, grid=(columns // middle,), in_specs=in_specs, out_sp...  36.3 us
    all_to_all x2, waiting for transfers between devices, quick_scatter(): lax.all_to_all(value, 'fsdp', 0, 0, axis_index_groups=same_core(fsdp))  28.6 us
    all_to_all x2, blocking collectives, flat(): return jnp.sum(lax.all_to_all(copies, AXES, 0, 0), axis=0)  19.1 us
  transfers between devices with their start and end apart: 37, of which 25 were waited for; matrix products, arithmetic and copies ran while one was open for 13% of the time, Pallas kernels for 32%

profile of v1, /device:TPU:0, one launch (start us, length us, event | category | flops | bytes accessed | tf_op | source)
XLA Modules:
  0.0 795.6 jit_solution(14640616165552737621)
XLA Ops:
  12.6 12.2 %all_to_all.138 = bf16[4,32,512]{2,1,0:T(8,128)(2,1)S(1)} all-to-all(bf16[4,32,512]{2,1,0:T(8,128)(2,1)S(1)} %broadcast_in_dim.60), channel_id=1, replica_groups=mesh['dp'=4,'fsdp'=8] {'dp'}, dimensions={0} | all-to-all | bytes 262144 | tf_op jit(solution)/shard_map/all_to_all | solution.py:1217
  25.7 3.7 all-to-all-start.1
  30.1 5.9 all-to-all-done.1
  39.9 14.4 %shard_map.298 = (f32[14,14,32,512]{3,2,1,0:T(8,128)}, f32[2,8,512]{2,1,0:T(8,128)}) custom-call(bf16[6272,1024]{1,0:T(8,128)(2,1)} %bitcast.322, bf16[1024,512]{1,0:T(8,128)(2,1)} %bitcast.338, f32[32,256]{1,0:T(8,128)} %broadcast_in_dim.63.m_ref.refs_4_.refs_5_.refs_7_), custom_call_target="tpu_custom_call" | custom-call | flops 6576668672 | bytes 25690112 | tf_op jit(solution)/shard_map/pallas_call | solution.py:75
  57.2 3.9 all-to-all-start.2
  66.7 3.4 all-to-all-done.2
  72.7 42.7 %all-gather.6.cloned.1.call-done = bf16[12800,512]{1,0:T(8,128)(2,1)} async-done(((bf16[400,512]{1,0:T(8,128)(2,1)}), bf16[12800,512]{1,0:T(8,128)(2,1)}) %all-gather.6.cloned.1.call-update) | async-done | bytes 13107216 | tf_op jit(solution)/shard_map/all_gather | solution.py:1306
  115.4 14.3 %shard_map.299 = (bf16[14,14,32,512]{3,2,1,0:T(8,128)(2,1)}, f32[7,7,32,512]{3,2,1,0:T(8,128)}, f32[2,32,512]{2,1,0:T(8,128)}) custom-call(f32[14,14,32,512]{3,2,1,0:T(8,128)} %get-tuple-element.91.a_ref, f32[1,512]{1,0:T(1,128)} %bitcast.427, f32[1,512]{1,0:T(1,128)} %bitcast.443, f32[32,256]{1,0:T(8,128)} %broadcast_in_dim.63.m_ref.refs_4_.refs_5_.refs_7_, ...), custom_call_target="tpu_custom_call" | custom-call | flops 7398752256 | bytes 23986176 | tf_op jit(solution)/shard_map/pallas_call | solution.py:75
  134.2 12.4 %shard_map.301 = (f32[49,32,2048]{2,1,0:T(8,128)}, f32[2,8,2048]{2,1,0:T(8,128)}) custom-call(bf16[49,32,1024]{2,1,0:T(8,128)(2,1)} %bitcast.331, f32[32,256]{1,0:T(8,128)} %broadcast_in_dim.63.m_ref.refs_4_.refs_5_.refs_7_, bf16[32,400,512]{2,1,0:T(8,128)(2,1)} %bitcast.301), custom_call_target="tpu_custom_call" | custom-call | flops 6576668672 | bytes 16056320 | tf_op jit(solution)/shard_map/pallas_call | solution.py:75
  148.4 11.0 %shard_map.300 = (bf16[49,32,512]{2,1,0:T(8,128)(2,1)}, f32[49,32,2048]{2,1,0:T(8,128)}, f32[2,8,2048]{2,1,0:T(8,128)}) custom-call(f32[49,32,512]{2,1,0:T(8,128)} %bitcast.318, f32[2,512]{1,0:T(2,128)} %pad_maximum_fusion.16.s_ref, f32[32,256]{1,0:T(8,128)} %broadcast_in_dim.63.m_ref.refs_4_.refs_5_.refs_7_, bf16[32,400,512]{2,1,0:T(8,128)(2,1)} %bitcast.302), custom_call_target="tpu_custom_call" | custom-call | flops 3288334336 | bytes 17661952 | tf_op jit(solution)/shard_map/pallas_call | solution.py:75
  161.9 17.9 %all_to_all.139 = f32[16,1,4096]{2,1,0:T(1,128)S(1)} all-to-all(f32[16,1,4096]{2,1,0:T(1,128)S(1)} %broadcast_in_dim.69), channel_id=1, replica_groups={{0,2,4,6,8,10,12,14,16,18,20,22,24,26,28,30},{1,3,5,7,9,11,13,15,17,19,..., dimensions={0} | all-to-all | bytes 524288 | tf_op jit(solution)/shard_map/all_to_all | solution.py:1188
  182.0 17.4 %shard_map.302 = (bf16[49,32,2048]{2,1,0:T(8,128)(2,1)}, f32[49,32,512]{2,1,0:T(8,128)}, f32[2,8,512]{2,1,0:T(8,128)}) custom-call(f32[49,32,2048]{2,1,0:T(8,128)} %get-tuple-element.95.c_ref, f32[49,32,2048]{2,1,0:T(8,128)} %get-tuple-element.96.p_ref, f32[8,2048]{1,0:T(8,128)} %stack.296.s_ref, f32[32,256]{1,0:T(8,128)} %broadcast_in_dim.63.m_ref.refs_4_.refs_5_.refs_7_, ...), custom_call_target="tpu_custom_call" | custom-call | flops 3288334336 | bytes 32112640 | tf_op jit(solution)/shard_map/pallas_call | solution.py:75
  206.8 5.4 all-to-all-done.5
  212.9 4.8 shard_map.303
  227.3 6.3 all-to-all-done.6
  237.0 4.3 shard_map.304
  246.3 6.2 all-to-all-done.7
  253.2 3.7 shard_map.305
  262.0 6.2 all-to-all-done.8
  268.9 3.7 shard_map.306
  273.4 8.9 %all_to_all.140 = f32[32,1,256]{2,1,0:T(1,128)S(1)} all-to-all(f32[32,1,256]{2,1,0:T(1,128)S(1)} %broadcast_in_dim.76), channel_id=1, replica_groups=mesh['dp'=4,'fsdp'=8] {'dp','fsdp'}, dimensions={0} | all-to-all | bytes 65536 | tf_op jit(solution)/shard_map/all_to_all | solution.py:1181
  283.1 10.2 %shard_map.307 = (bf16[49,32,512]{2,1,0:T(8,128)(2,1)}, f32[49,32,2048]{2,1,0:T(8,128)}, f32[2,8,2048]{2,1,0:T(8,128)}) custom-call(bf16[49,32,512]{2,1,0:T(8,128)(2,1)} %get-tuple-element.104.refs_0_.x_ref.refs_5_, bf16[49,32,128]{2,1,0:T(8,128)(2,1)} %get-tuple-element.107.o1.refs_8_, bf16[49,32,128]{2,1,0:T(8,128)(2,1)} %get-tuple-element.110.o2.refs_8_, ...), custom_call_target="tpu_custom_call" | custom-call | flops 3288334336 | bytes 16056320 | tf_op jit(solution)/shard_map/pallas_call | solution.py:75
  295.6 10.6 %all_to_all.141 = f32[16,1,2048]{2,1,0:T(1,128)S(1)} all-to-all(f32[16,1,2048]{2,1,0:T(1,128)S(1)} %broadcast_in_dim.77), channel_id=1, replica_groups={{0,2,4,6,8,10,12,14,16,18,20,22,24,26,28,30},{1,3,5,7,9,11,13,15,17,19,..., dimensions={0} | all-to-all | bytes 262144 | tf_op jit(solution)/shard_map/all_to_all | solution.py:1188
  306.4 6.7 copy.257
  314.0 21.4 %shard_map.308 = (bf16[49,32,2048]{2,1,0:T(8,128)(2,1)}, f32[49,32,2048]{2,1,0:T(8,128)}, f32[2,8,2048]{2,1,0:T(8,128)}) custom-call(f32[49,32,2048]{2,1,0:T(8,128)} %get-tuple-element.113.e_ref, bf16[49,32,2048]{2,1,0:T(8,128)(2,1)} %get-tuple-element.114.o_ref.refs_0_, bf16[49,32,2048]{2,1,0:T(8,128)(2,1)} %bitcast.321, ...), custom_call_target="tpu_custom_call" | custom-call | flops 64225280 | bytes 44957696 | tf_op jit(solution)/shard_map/pallas_call | solution.py:75
  338.5 3.7 all-to-all-start.11
  345.8 4.6 all-to-all-done.11
  353.1 17.1 %shard_map.309 = (bf16[49,32,2048]{2,1,0:T(8,128)(2,1)}, f32[49,32,512]{2,1,0:T(8,128)}, f32[49,32,128]{2,1,0:T(8,128)}, f32[2,8,128]{2,1,0:T(8,128)}) custom-call(f32[49,32,2048]{2,1,0:T(8,128)} %get-tuple-element.117.g_ref.t_ref, f32[49,32,2048]{2,1,0:T(8,128)} %get-tuple-element.113.e_ref, f32[5,2048]{1,0:T(8,128)} %stack.316.s_ref, ...), custom_call_target="tpu_custom_call" | custom-call | flops 3288334336 | bytes 32112640 | tf_op jit(solution)/shard_map/pallas_call | solution.py:75
  374.7 6.7 all-to-all-done.12
  382.6 5.4 shard_map.310
  392.0 7.9 shard_map.313
  401.1 5.5 shard_map.311
  408.0 5.8 all-to-all-start.14
  414.3 3.2 shard_map.316
  417.4 3.2 shard_map.315
  422.2 5.6 shard_map.312
  427.8 3.2 shard_map.314
  433.1 9.3 %dynamic_update_slice.3 = bf16[8,4,96,512]{3,2,1,0:T(8,128)(2,1)} dynamic-update-slice(bf16[8,4,96,512]{3,2,1,0:T(8,128)(2,1)} %shard_map.313, bf16[8,4,27,512]{3,2,1,0:T(8,128)(2,1)S(1)} %bitcast.340, s32[]{:T(128)} %constant.103.clone.1, s32[]{:T(128)} %constant.103.clone.1, s32[]{:T(128)} %constant.115.clone.1, s32[]{:T(128)} %constant.103.clone.1) | dynamic-update-slice | bytes 1769476 | tf_op jit(solution)/shard_map/dynamic_update_slice | solution.py:1567
  443.6 5.4 all-to-all-start.15
  450.2 7.3 all-to-all-done.15
  462.1 9.2 %shard_map.317 = (f32[49,32,512]{2,1,0:T(8,128)}, bf16[49,32,32]{2,1,0:T(8,128)(2,1)}, f32[2,8,512]{2,1,0:T(8,128)}) custom-call(f32[49,32,512]{2,1,0:T(8,128)} %get-tuple-element.119.refs_6_.j_ref, f32[49,32,128]{2,1,0:T(8,128)} %get-tuple-element.128.p1, f32[49,32,128]{2,1,0:T(8,128)} %get-tuple-element.126.refs_8_.p2, ...), custom_call_target="tpu_custom_call" | custom-call | flops 51380224 | bytes 9633792 | tf_op jit(solution)/shard_map/pallas_call | solution.py:75
  472.2 10.2 %all_to_all.142 = f32[32,1,1024]{2,1,0:T(1,128)S(1)} all-to-all(f32[32,1,1024]{2,1,0:T(1,128)S(1)} %broadcast_in_dim.85), channel_id=1, replica_groups=mesh['dp'=4,'fsdp'=8] {'dp','fsdp'}, dimensions={0} | all-to-all | bytes 262144 | tf_op jit(solution)/shard_map/all_to_all | solution.py:1181
  483.7 26.6 %shard_map.318 = (bf16[49,32,512]{2,1,0:T(8,128)(2,1)}, f32[49,32,2048]{2,1,0:T(8,128)}, f32[3,8,2048]{2,1,0:T(8,128)}) custom-call(f32[49,32,512]{2,1,0:T(8,128)} %get-tuple-element.140.n_ref, f32[49,32,512]{2,1,0:T(8,128)} %get-tuple-element.99.d_ref, f32[5,512]{1,0:T(8,128)} %stack.348.sd_ref, bf16[32,400,512]{2,1,0:T(8,128)(2,1)} %bitcast.304, ...), custom_call_target="tpu_custom_call" | custom-call | flops 3288334336 | bytes 51380224 | tf_op jit(solution)/shard_map/pallas_call | solution.py:75
  513.5 3.5 all-to-all-start.17
  517.9 8.0 %all-to-all-done.17 = f32[16,1,3072]{2,1,0:T(1,128)S(1)} async-done(((f32[16,1,3072]{2,1,0:T(1,128)}), f32[16,1,3072]{2,1,0:T(1,128)S(1)}, u32[]{:S(2)}, u32[]{:S(2)}) %all-to-all-start.17) | async-done | bytes 196640 | tf_op jit(solution)/shard_map/all_to_all | solution.py:1188
  526.1 8.6 %shard_map.320.refs_2_ = bf16[8,4,256,512]{3,2,1,0:T(8,128)(2,1)} custom-call(bf16[49,32,2048]{2,1,0:T(8,128)(2,1)} %get-tuple-element.114.o_ref.refs_0_, bf16[49,32,512]{2,1,0:T(8,128)(2,1)} %get-tuple-element.151.refs_1_), custom_call_target="tpu_custom_call" | custom-call | flops 3288334336 | bytes 10125312 | tf_op jit(solution)/shard_map/pallas_call | solution.py:871
  536.8 22.9 %shard_map.319 = (bf16[49,32,2048]{2,1,0:T(8,128)(2,1)}, bf16[49,32,2048]{2,1,0:T(8,128)(2,1)}, f32[49,32,512]{2,1,0:T(8,128)}, f32[2,8,512]{2,1,0:T(8,128)}) custom-call(f32[49,32,2048]{2,1,0:T(8,128)} %get-tuple-element.142.g_ref, f32[49,32,2048]{2,1,0:T(8,128)} %get-tuple-element.95.c_ref, f32[49,32,2048]{2,1,0:T(8,128)} %get-tuple-element.96.p_ref, ...), custom_call_target="tpu_custom_call" | custom-call | flops 3288334336 | bytes 51380224 | tf_op jit(solution)/shard_map/pallas_call | solution.py:75
  559.6 8.0 %shard_map.321.refs_2_ = bf16[8,4,256,512]{3,2,1,0:T(8,128)(2,1)} custom-call(bf16[49,32,512]{2,1,0:T(8,128)(2,1)} %get-tuple-element.149.refs_0_, bf16[49,32,2048]{2,1,0:T(8,128)(2,1)} %get-tuple-element.150.refs_1_, bf16[8,4,256,512]{3,2,1,0:T(8,128)(2,1)} %shard_map.320.refs_2_), custom_call_target="tpu_custom_call", output_to_operand_aliasing={{}: (2, {})} | custom-call | flops 3288334336 | bytes 10125312 | tf_op jit(solution)/shard_map/pallas_call | solution.py:871
  567.6 11.8 %shard_map.322 = bf16[8,4,256,512]{3,2,1,0:T(8,128)(2,1)} custom-call(bf16[49,32,1024]{2,1,0:T(8,128)(2,1)} %bitcast.332, bf16[49,32,2048]{2,1,0:T(8,128)(2,1)} %get-tuple-element.148.refs_1_.g_ref, bf16[8,4,256,512]{3,2,1,0:T(8,128)(2,1)} %shard_map.321.refs_2_), custom_call_target="tpu_custom_call", output_to_operand_aliasing={{}: (2, {})} | custom-call | flops 6576668672 | bytes 13828096 | tf_op jit(solution)/shard_map/pallas_call | solution.py:871
  596.2 3.7 all-to-all-done.18
  600.0 4.1 multiply_convert_fusion
  604.1 15.7 %shard_map.323 = bf16[9,512,512]{2,1,0:T(8,128)(2,1)} custom-call(bf16[7,2,7,2,32,512]{5,4,3,2,1,0:T(8,128)(2,1)} %bitcast.467, bf16[1568,512]{1,0:T(8,128)(2,1)} %bitcast.326), custom_call_target="tpu_custom_call" | custom-call | flops 7398752256 | bytes 12746752 | tf_op jit(solution)/shard_map/pallas_call | solution.py:75
  626.4 19.8 %shard_map.324 = (f32[7,2,7,2,32,512]{5,4,3,2,1,0:T(8,128)}, f32[2,32,512]{2,1,0:T(8,128)}) custom-call(bf16[7,7,32,512]{3,2,1,0:T(8,128)(2,1)} %bitcast.327, bf16[7,7,32,512]{3,2,1,0:T(8,128)(2,1)} %bitcast.328, f32[7,2,7,2,32,512]{5,4,3,2,1,0:T(8,128)} %bitcast.317, f32[4,512]{1,0:T(4,128)} %pad_maximum_fusion.13.s_ref, ...), custom_call_target="tpu_custom_call" | custom-call | flops 7398752256 | bytes 30408704 | tf_op jit(solution)/shard_map/pallas_call | solution.py:75
  648.7 11.7 %all_to_all.143 = f32[16,1,1280]{2,1,0:T(1,128)S(1)} all-to-all(f32[16,1,1280]{2,1,0:T(1,128)S(1)} %broadcast_in_dim.89), channel_id=1, replica_groups={{0,2,4,6,8,10,12,14,16,18,20,22,24,26,28,30},{1,3,5,7,9,11,13,15,17,19,..., dimensions={0} | all-to-all | bytes 163840 | tf_op jit(solution)/shard_map/all_to_all | solution.py:1188
  662.3 21.4 %shard_map.325 = (bf16[6272,512]{1,0:T(8,128)(2,1)}, bf16[1024,512]{1,0:T(8,128)(2,1)}) custom-call(f32[14,14,32,512]{3,2,1,0:T(8,128)} %bitcast.329, f32[14,14,32,512]{3,2,1,0:T(8,128)} %get-tuple-element.91.a_ref, bf16[6272,1024]{1,0:T(8,128)(2,1)} %bitcast.324, f32[5,512]{1,0:T(8,128)} %stack.365.s_ref, ...), custom_call_target="tpu_custom_call" | custom-call | flops 6576668672 | bytes 44957696 | tf_op jit(solution)/shard_map/pallas_call | solution.py:75
  688.0 3.7 all-to-all-start.20
  694.8 3.3 copy.288
  700.3 3.6 all-to-all-start.22
  705.2 26.4 %all-to-all-done.22 = bf16[4,4,146,512]{3,1,2,0:T(4,128)(2,1)S(1)} async-done(((bf16[4,4,146,512]{3,1,2,0:T(4,128)(2,1)}), bf16[4,4,146,512]{3,1,2,0:T(4,128)(2,1)S(1)}, u32[]{:S(2)}, u32[]{:S(2)}) %all-to-all-start.22) | async-done | bytes 2392096 | tf_op jit(solution)/shard_map/all_to_all | solution.py:1241
  731.7 3.3 all-to-all-start.21
  735.0 6.7 copy.366
  744.3 5.1 all-to-all-start.23
  749.5 13.6 %shard_map.326 = f32[49,32,1024]{2,1,0:T(8,128)} custom-call(bf16[49,32,2048]{2,1,0:T(8,128)(2,1)} %get-tuple-element.148.refs_1_.g_ref, bf16[32,400,512]{2,1,0:T(8,128)(2,1)} %bitcast.315), custom_call_target="tpu_custom_call" | custom-call | flops 6576668672 | bytes 12845056 | tf_op jit(solution)/shard_map/pallas_call | solution.py:75
  767.7 13.7 %shard_map.327 = bf16[6272,1024]{1,0:T(8,128)(2,1)} custom-call(bf16[6272,512]{1,0:T(8,128)(2,1)} %get-tuple-element.161.g_ref, bf16[1024,512]{1,0:T(8,128)(2,1)} %bitcast.339, f32[7,7,32,1024]{3,2,1,0:T(8,128)} %bitcast.320), custom_call_target="tpu_custom_call" | custom-call | flops 6576668672 | bytes 25690112 | tf_op jit(solution)/shard_map/pallas_call | solution.py:75
  (472 shorter events, 161.3 us)
Async XLA Ops:
  7.2 22.9 %copy-start.61 = (s32[4,8]{1,0:T(4,128)S(1)}, s32[4,8]{1,0:T(4,128)}, u32[]{:S(2)}) copy-start(s32[4,8]{1,0:T(4,128)} %param.21) | copy-start | bytes 388
  7.2 22.9 %copy-start.64 = (s32[4]{0:T(128)S(1)}, s32[4]{0:T(128)}, u32[]{:S(2)}) copy-start(s32[4]{0:T(128)} %param.20) | copy-start | bytes 52
  7.2 108.2 %all-gather.6.cloned.1.call-start = ((), (), s32[]{:S(2)}) async-start(), calls=%async_computation.32 | async-start | bytes 13516800 | tf_op jit(solution)/shard_map/all_gather | solution.py:1306
  25.7 10.3 %all-to-all-start.1 = ((bf16[4,4,32,512]{3,2,1,0:T(8,128)(2,1)}), bf16[4,4,32,512]{3,2,1,0:T(8,128)(2,1)S(1)}, u32[]{:S(2)}, u32[]{:S(2)}) async-start(bf16[4,4,32,512]{3,2,1,0:T(8,128)(2,1)} %broadcast_in_dim.61), calls=%async_computation.1 | async-start | bytes 1048576 | tf_op jit(solution)/shard_map/all_to_all | solution.py:1218
  30.1 412.3 %copy-start.62 = (f32[4,8]{1,0:T(4,128)}, f32[4,8]{1,0:T(4,128)S(1)}, u32[]{:S(2)}) copy-start(f32[4,8]{1,0:T(4,128)S(1)} %get-tuple-element.292) | copy-start | bytes 388
  36.0 1.9 collective-permute-start
  36.1 182.4 %copy-start.35 = (f32[32]{0:T(128)}, f32[32]{0:T(128)S(1)}, u32[]{:S(2)}) copy-start(f32[32]{0:T(128)S(1)} %broadcast_in_dim.62) | copy-start | bytes 388
  37.4 182.8 %copy-start.25 = (f32[4,7]{1,0:T(4,128)}, f32[4,7]{1,0:T(4,128)S(1)}, u32[]{:S(2)}) copy-start(f32[4,7]{1,0:T(4,128)S(1)} %get-tuple-element.393) | copy-start | bytes 340
  39.9 21.3 %copy-start.49 = (bf16[16,32]{1,0:T(8,128)(2,1)S(1)}, bf16[16,32]{1,0:T(8,128)(2,1)}, u32[]{:S(2)}) copy-start(bf16[16,32]{1,0:T(8,128)(2,1)} %param.29) | copy-start | bytes 3076
  39.9 21.4 %copy-start.50 = (bf16[16,32]{1,0:T(8,128)(2,1)S(1)}, bf16[16,32]{1,0:T(8,128)(2,1)}, u32[]{:S(2)}) copy-start(bf16[16,32]{1,0:T(8,128)(2,1)} %param.28) | copy-start | bytes 3076
  39.9 21.5 %copy-start.17 = (bf16[27,512]{1,0:T(8,128)(2,1)S(1)}, bf16[27,512]{1,0:T(8,128)(2,1)}, u32[]{:S(2)}) copy-start(bf16[27,512]{1,0:T(8,128)(2,1)} %param.30) | copy-start | bytes 82948
  39.9 21.8 %copy-start.10 = (bf16[16,2048]{1,0:T(8,128)(2,1)S(1)}, bf16[16,2048]{1,0:T(8,128)(2,1)}, u32[]{:S(2)}) copy-start(bf16[16,2048]{1,0:T(8,128)(2,1)} %param.31) | copy-start | bytes 196612
  57.2 12.9 %all-to-all-start.2 = ((f32[32,1,1280]{2,1,0:T(1,128)}), f32[32,1,1280]{2,1,0:T(1,128)S(1)}, u32[]{:S(2)}, u32[]{:S(2)}) async-start(f32[32,1,1280]{2,1,0:T(1,128)} %broadcast_in_dim.65), calls=%async_computation.2 | async-start | bytes 327680 | tf_op jit(solution)/shard_map/all_to_all | solution.py:1181
  61.1 142.8 %all-gather.8.cloned.1.call-start = ((), (), s32[]{:S(2)}) async-start(), calls=%async_computation.33 | async-start | bytes 3244032 | tf_op jit(solution)/shard_map/all_gather | solution.py:1306
  131.4 16.2 %all-to-all-start.3 = ((f32[32,1,1024]{2,1,0:T(1,128)}), f32[32,1,1024]{2,1,0:T(1,128)S(1)}, u32[]{:S(2)}, u32[]{:S(2)}) async-start(f32[32,1,1024]{2,1,0:T(1,128)} %broadcast_in_dim.68), calls=%async_computation.3 | async-start | bytes 262144 | tf_op jit(solution)/shard_map/all_to_all | solution.py:1181
  147.8 369.5 %copy-start.31 = (f32[512]{0:T(512)}, f32[512]{0:T(512)S(1)}, u32[]{:S(2)}) copy-start(f32[512]{0:T(512)S(1)} %get-tuple-element.315) | copy-start | bytes 6148
  147.8 369.5 %copy-start.32 = (f32[512]{0:T(512)}, f32[512]{0:T(512)S(1)}, u32[]{:S(2)}) copy-start(f32[512]{0:T(512)S(1)} %get-tuple-element.316) | copy-start | bytes 6148
  148.4 31.7 %copy-start.47 = (f32[3,3,128]{2,1,0:T(4,128)S(1)}, f32[3,3,128]{2,1,0:T(4,128)}, u32[]{:S(2)}) copy-start(f32[3,3,128]{2,1,0:T(4,128)} %param.35) | copy-start | bytes 13828
  160.5 1.2 collective-permute-start.1
  180.0 1.2 collective-permute-start.2
  200.9 11.2 %all-to-all-start.5 = ((f32[32,1,1024]{2,1,0:T(1,128)}), f32[32,1,1024]{2,1,0:T(1,128)S(1)}, u32[]{:S(2)}, u32[]{:S(2)}) async-start(f32[32,1,1024]{2,1,0:T(1,128)} %broadcast_in_dim.70), calls=%async_computation.5 | async-start | bytes 262144 | tf_op jit(solution)/shard_map/all_to_all | solution.py:1181
  203.9 238.5 %copy-start.46 = (f32[4,8]{1,0:T(4,128)}, f32[4,8]{1,0:T(4,128)S(1)}, u32[]{:S(2)}) copy-start(f32[4,8]{1,0:T(4,128)S(1)} %get-tuple-element.392) | copy-start | bytes 388
  203.9 256.6 %copy-start.60 = (f32[4,8]{1,0:T(4,128)}, f32[4,8]{1,0:T(4,128)S(1)}, u32[]{:S(2)}) copy-start(f32[4,8]{1,0:T(4,128)S(1)} %get-tuple-element.391) | copy-start | bytes 388
  221.1 221.4 %copy-start.34 = (f32[4,8,32]{2,1,0:T(8,128)}, f32[4,8,32]{2,1,0:T(8,128)S(1)}, u32[]{:S(2)}) copy-start(f32[4,8,32]{2,1,0:T(8,128)S(1)} %get-tuple-element.301) | copy-start | bytes 12292
  222.3 11.3 %all-to-all-start.6 = ((f32[32,1,1280]{2,1,0:T(1,128)}), f32[32,1,1280]{2,1,0:T(1,128)S(1)}, u32[]{:S(2)}, u32[]{:S(2)}) async-start(f32[32,1,1280]{2,1,0:T(1,128)} %broadcast_in_dim.73), calls=%async_computation.6 | async-start | bytes 327680 | tf_op jit(solution)/shard_map/all_to_all | solution.py:1181
  225.2 217.3 %copy-start.51 = (f32[32]{0:T(128)}, f32[32]{0:T(128)S(1)}, u32[]{:S(2)}) copy-start(f32[32]{0:T(128)S(1)} %get-tuple-element.253) | copy-start | bytes 388
  234.6 225.3 %copy-start.36 = (f32[32]{0:T(128)}, f32[32]{0:T(128)S(1)}, u32[]{:S(2)}) copy-start(f32[32]{0:T(128)S(1)} %get-tuple-element.299) | copy-start | bytes 388
  234.6 346.1 %copy-start.48 = (f32[32]{0:T(128)}, f32[32]{0:T(128)S(1)}, u32[]{:S(2)}) copy-start(f32[32]{0:T(128)S(1)} %get-tuple-element.298) | copy-start | bytes 388
  236.0 224.6 %copy-start.23 = (f32[512]{0:T(512)}, f32[512]{0:T(512)S(1)}, u32[]{:S(2)}) copy-start(f32[512]{0:T(512)S(1)} %get-tuple-element.295) | copy-start | bytes 6148
  236.0 224.6 %copy-start.37 = (f32[512]{0:T(512)}, f32[512]{0:T(512)S(1)}, u32[]{:S(2)}) copy-start(f32[512]{0:T(512)S(1)} %get-tuple-element.296) | copy-start | bytes 6148
  236.0 224.6 %copy-start.38 = (f32[512]{0:T(512)}, f32[512]{0:T(512)S(1)}, u32[]{:S(2)}) copy-start(f32[512]{0:T(512)S(1)} %get-tuple-element.297) | copy-start | bytes 6148
  236.3 224.3 %copy-start.7 = (f32[4,8,512]{2,1,0:T(8,128)}, f32[4,8,512]{2,1,0:T(8,128)S(1)}, u32[]{:S(2)}) copy-start(f32[4,8,512]{2,1,0:T(8,128)S(1)} %fusion.39) | copy-start | bytes 196612
  242.6 9.8 %all-to-all-start.7 = ((f32[32,1,256]{2,1,0:T(1,128)}), f32[32,1,256]{2,1,0:T(1,128)S(1)}, u32[]{:S(2)}, u32[]{:S(2)}) async-start(f32[32,1,256]{2,1,0:T(1,128)} %broadcast_in_dim.74), calls=%async_computation.7 | async-start | bytes 65536 | tf_op jit(solution)/shard_map/all_to_all | solution.py:1181
  258.3 9.8 %all-to-all-start.8 = ((f32[32,1,256]{2,1,0:T(1,128)}), f32[32,1,256]{2,1,0:T(1,128)S(1)}, u32[]{:S(2)}, u32[]{:S(2)}) async-start(f32[32,1,256]{2,1,0:T(1,128)} %broadcast_in_dim.75), calls=%async_computation.8 | async-start | bytes 65536 | tf_op jit(solution)/shard_map/all_to_all | solution.py:1181
  294.3 1.2 collective-permute-start.3
  306.4 7.0 collective-permute-start.4
  336.4 1.4 collective-permute-start.5
  338.5 11.9 %all-to-all-start.11 = ((f32[16,1,2048]{2,1,0:T(1,128)}), f32[16,1,2048]{2,1,0:T(1,128)S(1)}, u32[]{:S(2)}, u32[]{:S(2)}) async-start(f32[16,1,2048]{2,1,0:T(1,128)} %broadcast_in_dim.78), calls=%async_computation.11 | async-start | bytes 262144 | tf_op jit(solution)/shard_map/all_to_all | solution.py:1188
  350.5 1.2 collective-permute-start.6
  371.6 9.8 %all-to-all-start.12 = ((f32[32,1,256]{2,1,0:T(1,128)}), f32[32,1,256]{2,1,0:T(1,128)S(1)}, u32[]{:S(2)}, u32[]{:S(2)}) async-start(f32[32,1,256]{2,1,0:T(1,128)} %broadcast_in_dim.79), calls=%async_computation.12 | async-start | bytes 65536 | tf_op jit(solution)/shard_map/all_to_all | solution.py:1181
  389.4 10.5 %all-to-all-start.13 = ((f32[32,1,256]{2,1,0:T(1,128)}), f32[32,1,256]{2,1,0:T(1,128)S(1)}, u32[]{:S(2)}, u32[]{:S(2)}) async-start(f32[32,1,256]{2,1,0:T(1,128)} %broadcast_in_dim.80), calls=%async_computation.13 | async-start | bytes 65536 | tf_op jit(solution)/shard_map/all_to_all | solution.py:1181
  408.0 13.1 %all-to-all-start.14 = ((f32[32,1,256]{2,1,0:T(1,128)}), f32[32,1,256]{2,1,0:T(1,128)S(1)}, u32[]{:S(2)}, u32[]{:S(2)}) async-start(f32[32,1,256]{2,1,0:T(1,128)} %broadcast_in_dim.81), calls=%async_computation.14 | async-start | bytes 65536 | tf_op jit(solution)/shard_map/all_to_all | solution.py:1181
  413.8 96.5 %reduce-scatter.5.cloned.1.call-start = ((), (), s32[]{:S(2)}) async-start(), calls=%async_computation.28 | async-start | bytes 3538944 | tf_op jit(solution)/shard_map/reduce_scatter | solution.py:1584
  442.5 28.9 %copy-start.8 = (f32[4,8,512]{2,1,0:T(8,128)}, f32[4,8,512]{2,1,0:T(8,128)S(1)}, u32[]{:S(2)}) copy-start(f32[4,8,512]{2,1,0:T(8,128)S(1)} %get-tuple-element.274) | copy-start | bytes 196612
  443.6 14.0 %all-to-all-start.15 = ((f32[32,1,1280]{2,1,0:T(1,128)}), f32[32,1,1280]{2,1,0:T(1,128)S(1)}, u32[]{:S(2)}, u32[]{:S(2)}) async-start(f32[32,1,1280]{2,1,0:T(1,128)} %broadcast_in_dim.83), calls=%async_computation.15 | async-start | bytes 327680 | tf_op jit(solution)/shard_map/all_to_all | solution.py:1181
  511.5 1.2 collective-permute-start.7
  513.5 12.4 %all-to-all-start.17 = ((f32[16,1,3072]{2,1,0:T(1,128)}), f32[16,1,3072]{2,1,0:T(1,128)S(1)}, u32[]{:S(2)}, u32[]{:S(2)}) async-start(f32[16,1,3072]{2,1,0:T(1,128)} %broadcast_in_dim.86), calls=%async_computation.18 | async-start | bytes 393216 | tf_op jit(solution)/shard_map/all_to_all | solution.py:1188
  517.0 62.4 %reduce-scatter.7.cloned.1.call-start = ((), (), s32[]{:S(2)}) async-start(), calls=%async_computation.29 | async-start | bytes 491520 | tf_op jit(solution)/shard_map/reduce_scatter | solution.py:1657
  526.0 8.7 %collective-permute-start.8 = (f32[3072]{0:T(1024)S(1)}, f32[3072]{0:T(1024)S(1)}, u32[]{:S(2)}, u32[]{:S(2)}) collective-permute-start(f32[3072]{0:T(1024)S(1)} %reduce_sum.643), channel_id=1, source_target_pairs={{0,1},{1,0},{2,3},{3,2},{4,5},{5,4},{6,7},{7,6},{8,9},{9,8},{10,11... | collective-permute-start | bytes 36872 | tf_op jit(solution)/shard_map/ppermute | solution.py:1189
  534.7 169.3 %reduce-scatter.9.cloned.1.call-start = ((), (), s32[]{:S(2)}) async-start(), calls=%async_computation.30 | async-start | bytes 9437184 | tf_op jit(solution)/shard_map/reduce_scatter | solution.py:1701
  588.8 11.1 %all-to-all-start.18 = ((f32[32,1,1024]{2,1,0:T(1,128)}), f32[32,1,1024]{2,1,0:T(1,128)S(1)}, u32[]{:S(2)}, u32[]{:S(2)}) async-start(f32[32,1,1024]{2,1,0:T(1,128)} %broadcast_in_dim.87), calls=%async_computation.20 | async-start | bytes 262144 | tf_op jit(solution)/shard_map/all_to_all | solution.py:1181
  626.3 65.4 %collective-permute-start.12 = (bf16[4,4,146,512]{3,1,2,0:T(4,128)(2,1)S(1)}, bf16[4,4,146,512]{3,1,2,0:T(4,128)(2,1)}, u32[]{:S(2)}, u32[]{:S(2)}) collective-permute-start(bf16[4,4,146,512]{3,1,2,0:T(4,128)(2,1)S(1)} %copy.286), channel_id=1, source_target_pairs={{0,1},{1,0},{2,3},{3,2},{4,5},{5,4},{6,7},{7,6},{8,9},{9,8},{10,11... | collective-permute-start | bytes 7176200 | tf_op jit(solution)/shard_map/ppermute | solution.py:1239
  626.4 20.7 %copy-start.45 = (f32[288]{0:T(512)S(1)}, f32[288]{0:T(512)}, u32[]{:S(2)}) copy-start(f32[288]{0:T(512)} %reshape.565) | copy-start | bytes 3460
  626.4 35.2 %copy-start.22 = (f32[512]{0:T(512)S(1)}, f32[512]{0:T(512)}, u32[]{:S(2)}) copy-start(f32[512]{0:T(512)} %get-tuple-element.318) | copy-start | bytes 6148
  626.4 35.3 %copy-start.28 = (f32[512]{0:T(512)S(1)}, f32[512]{0:T(512)}, u32[]{:S(2)}) copy-start(f32[512]{0:T(512)} %get-tuple-element.319) | copy-start | bytes 6148
  626.4 35.3 %copy-start.30 = (f32[512]{0:T(512)S(1)}, f32[512]{0:T(512)}, u32[]{:S(2)}) copy-start(f32[512]{0:T(512)} %get-tuple-element.320) | copy-start | bytes 6148
  647.3 1.3 collective-permute-start.9
  660.4 1.2 collective-permute-start.10
  685.0 2.0 collective-permute-start.11
  688.0 12.3 %all-to-all-start.20 = ((bf16[4,4,32,512]{3,2,1,0:T(8,128)(2,1)}), bf16[4,4,32,512]{3,2,1,0:T(8,128)(2,1)S(1)}, u32[]{:S(2)}, u32[]{:S(2)}) async-start(bf16[4,4,32,512]{3,2,1,0:T(8,128)(2,1)} %fusion.13), calls=%async_computation.22 | async-start | bytes 1048576 | tf_op jit(solution)/shard_map/all_to_all | solution.py:1241
  700.3 31.4 %all-to-all-start.22 = ((bf16[4,4,146,512]{3,1,2,0:T(4,128)(2,1)}), bf16[4,4,146,512]{3,1,2,0:T(4,128)(2,1)S(1)}, u32[]{:S(2)}, u32[]{:S(2)}) async-start(bf16[4,4,146,512]{3,1,2,0:T(4,128)(2,1)} %copy.288), calls=%async_computation.24 | async-start | bytes 4784128 | tf_op jit(solution)/shard_map/all_to_all | solution.py:1241
  703.9 80.5 %reduce-scatter.11.cloned.1.call-start = ((), (), s32[]{:S(2)}) async-start(), calls=%async_computation.31 | async-start | bytes 1310720 | tf_op jit(solution)/shard_map/reduce_scatter | solution.py:1702
  731.7 12.6 %all-to-all-start.21 = ((bf16[4,32,512]{2,1,0:T(8,128)(2,1)}), bf16[4,32,512]{2,1,0:T(8,128)(2,1)S(1)}, u32[]{:S(2)}, u32[]{:S(2)}) async-start(bf16[4,32,512]{2,1,0:T(8,128)(2,1)} %reduce_sum.655), calls=%async_computation.23 | async-start | bytes 262144 | tf_op jit(solution)/shard_map/all_to_all | solution.py:1243
  744.3 37.8 %all-to-all-start.23 = ((bf16[4,146,512]{2,1,0:T(8,128)(2,1)}), bf16[4,146,512]{2,1,0:T(8,128)(2,1)S(1)}, u32[]{:S(2)}, u32[]{:S(2)}) async-start(bf16[4,146,512]{2,1,0:T(8,128)(2,1)} %copy.289), calls=%async_computation.25 | async-start | bytes 1245184 | tf_op jit(solution)/shard_map/all_to_all | solution.py:1243
  (38 other events, 441.5 us)
Sparse Core Ops, SparseCore 0:
  12.0 103.4 all-gather.5
  118.9 59.5 all-gather.7
  442.5 47.0 reduce-scatter.4
  534.8 18.8 reduce-scatter.6
  579.6 69.5 reduce-scatter.8
  706.8 26.1 reduce-scatter.10

commit v2 on v1

--- a/solution.py
+++ b/solution.py
@@ -62,7 +62,7 @@
 
 
 def silu_parts(norm):
-    sig = 1.0 / (1.0 + jnp.exp(-norm))
+    sig = 0.5 * jnp.tanh(0.5 * norm) + 0.5
     return sig, norm * sig
 
 
@@ -91,54 +91,106 @@
     return shape, lambda *_: (0,) * len(shape)
 
 
-def kernel_reduce1(feats, weight, mask, slots, height, frames):
+def mean_of(raw, weight):
+    return jnp.sum(raw * weight, axis=0, keepdims=True) / jnp.maximum(jnp.sum(weight), 1.0)
+
+
+def kernel_reduce1(feats, weight, mask, height, frames):
     c_in, middle = weight.shape
+    slots = feats.shape[0]
     half = height // 2
-    rows = half * height * frames
-
-    def body(x_ref, w_ref, m_ref, raw_ref, sum_ref):
+    rows = 2 * height * frames
+
+    def body(x_ref, w_ref, m_ref, raw_ref, off_ref, sum_ref):
         first = (pl.program_id(0) == 0) & (pl.program_id(1) == 0)
 
         @pl.when(first)
         def _():
             sum_ref[...] = jnp.zeros_like(sum_ref)
-
-        raw = jnp.dot(x_ref[...], w_ref[...], preferred_element_type=F32)
-        raw = raw.reshape(half * height, frames, middle)
-        raw_ref[...] = raw.reshape(half, height, frames, middle)
-        weight8 = m_ref[:, :1]
-        sum_ref[0] += jnp.sum(raw, axis=0) * weight8
-        sum_ref[1] += jnp.sum(raw * raw, axis=0) * weight8
+            few = nn(x_ref[0, : height * frames], w_ref[...]).reshape(height, frames, middle)
+            off_ref[0:1] = mean_of(jnp.sum(few, axis=0) * (1.0 / height), m_ref[:frames, :1])
+
+        left = x_ref[...].reshape(2 * rows, c_in)
+        m = m_ref[:, :1].reshape(2, 1, 1, frames, 1)
+        for c in chunks(middle):
+            raw = nn(left, w_ref[:, c]).reshape(2, 2, height, frames, -1)
+            offset = off_ref[0:1, c]
+            sum_ref[0, :, c] += jnp.sum(jnp.sum(raw, axis=(1, 2)) * m[:, 0, 0], axis=0)
+            sum_ref[1, :, c] += jnp.sum(jnp.sum(raw * raw, axis=(1, 2)) * m[:, 0, 0], axis=0)
+            low = raw - offset
+            raw_ref[:, :, :, c] = jnp.concatenate([low[0], low[1]], axis=2).astype(BF)
 
     return call(
         body,
-        (slots, 2),
+        (slots // 2, half),
         (feats, weight, mask),
         (
-            ((rows, c_in), lambda c, h: (c * 2 + h, 0)),
+            ((2, rows, c_in), lambda c, h: (c, h, 0)),
             whole(weight.shape),
-            ((frames, mask.shape[1]), lambda c, h: (c, 0)),
-        ),
-        (
-            ((height, height, slots * frames, middle), F32),
+            ((2 * frames, mask.shape[1]), lambda c, h: (c, 0)),
+        ),
+        (
+            ((height, height, slots * frames, middle), BF),
+            ((8, middle), F32),
             ((2, frames, middle), F32),
         ),
         (
-            ((half, height, frames, middle), lambda c, h: (h, 0, c, 0)),
+            ((2, height, 2 * frames, middle), lambda c, h: (h, 0, c, 0)),
+            whole((8, middle)),
             whole((2, frames, middle)),
         ),
-        flops=2 * feats.shape[0] * c_in * middle,
-        moved=feats.size * 2 + feats.shape[0] * middle * 4,
-    )
-
-
-def kernel_conv_down(raw_a, alpha, beta, mask, taps):
+        flops=2 * feats.size * middle,
+        moved=feats.size * 2 + feats.size // c_in * middle * 2,
+    )
+
+
+def exchange_shape(width):
+    return (lax.psum(1, AXES), 1, width)
+
+
+def send_sums(send_ref, sum_ref, last=True):
+    def send():
+        rows = [jnp.sum(sum_ref[n], axis=0, keepdims=True) for n in range(sum_ref.shape[0])]
+        row = jnp.concatenate(rows, axis=1)
+        send_ref[...] = jnp.broadcast_to(row[None], send_ref.shape)
+
+    if last is True:
+        send()
+    else:
+        pl.when(last)(send)
+
+
+def kernel_act(raw_a, stats, mask):
     height, _, batch, middle = raw_a.shape
+    block = (2, height, batch, middle), lambda i: (i, 0, 0, 0)
+
+    def body(a_ref, s_ref, m_ref, act_ref):
+        m = m_ref[...]
+        for c in chunks(middle):
+            al, be = s_ref[0:1, c], s_ref[1:2, c]
+            for p in range(2):
+                for j in range(height):
+                    act_ref[p, j, :, c] = (silu_parts(a_ref[p, j, :, c].astype(F32) * al + be)[1] * m).astype(BF)
+
+    return call(
+        body,
+        (height // 2,),
+        (raw_a, stats, mask),
+        (block, whole(stats.shape), whole(mask.shape)),
+        ((raw_a.shape, BF),),
+        (block,),
+        flops=10 * raw_a.size,
+        moved=raw_a.size * 6,
+    )[0]
+
+
+def kernel_conv_down(act_a, mask, taps):
+    height, _, batch, middle = act_a.shape
     half = height // 2
     rows = half * batch
 
-    def body(a_ref, al_ref, be_ref, m_ref, *refs):
-        w_refs, (act_ref, raw_ref, sum_ref, cols, w_ref) = refs[:9], refs[9:]
+    def body(a_ref, m_ref, *refs):
+        w_refs, (raw_ref, send_ref, cols, w_ref, sum_ref) = refs[:9], refs[9:]
         step = pl.program_id(0)
         wide = 3 * middle
 
@@ -153,14 +205,12 @@
         def _():
             cols[:, :wide] = cols[:, 2 * wide :]
 
-        al, be, m = al_ref[...], be_ref[...], m_ref[:, :1]
+        m = m_ref[:, :1]
         for p in range(2):
             base = (1 + p) * wide
             for j in range(half):
                 for q in range(2):
-                    norm = a_ref[p, 2 * j + q] * al + be
-                    act = (silu_parts(norm)[1] * m).astype(BF)
-                    act_ref[p, 2 * j + q] = act
+                    act = a_ref[p, 2 * j + q]
                     lane = base + (1 + q) * middle
                     cols[j * batch : (j + 1) * batch, lane : lane + middle] = act
                     if q == 1 and j + 1 < half:
@@ -170,38 +220,34 @@
         raw_ref[0] = raw
         sum_ref[0] += jnp.sum(raw, axis=0) * m
         sum_ref[1] += jnp.sum(raw * raw, axis=0) * m
+        send_sums(send_ref, sum_ref, step == half - 1)
 
     return call(
         body,
         (half,),
-        (raw_a, alpha, beta, mask) + tuple(t.array for t in taps),
-        (
-            ((2, height, batch, middle), lambda i: (i, 0, 0, 0)),
-            whole(alpha.shape),
-            whole(beta.shape),
-            whole(mask.shape),
-        )
+        (act_a, mask) + tuple(t.array for t in taps),
+        (((2, height, batch, middle), lambda i: (i, 0, 0, 0)), whole(mask.shape))
         + tuple(t.block() for t in taps),
         (
-            (raw_a.shape, BF),
             ((half, half, batch, middle), F32),
-            ((2, batch, middle), F32),
-        ),
-        (
-            ((2, height, batch, middle), lambda i: (i, 0, 0, 0)),
+            (exchange_shape(2 * middle), F32),
+        ),
+        (
             ((1, half, batch, middle), lambda i: (i, 0, 0, 0)),
-            whole((2, batch, middle)),
-        ),
-        scratch=[pltpu.VMEM((rows, 9 * middle), BF), pltpu.VMEM((9 * middle, middle), BF)],
+            whole(exchange_shape(2 * middle)),
+        ),
+        scratch=[pltpu.VMEM((rows, 9 * middle), BF), pltpu.VMEM((9 * middle, middle), BF), pltpu.VMEM((2, batch, middle), F32)],
         flops=2 * half * rows * 9 * middle * middle,
-        moved=raw_a.size * 6 + 18 * middle * middle,
-    )
-
-
-def kernel_conv_down_weights(act_a, grad):
+        moved=act_a.size * 2 + 18 * middle * middle,
+    )
+
+
+def kernel_conv_down_weights(act_a, grad, dp, fsdp):
     height, _, batch, middle = act_a.shape
     half = height // 2
     split = act_a.reshape(half, 2, half, 2, batch, middle)
+    own = middle // (dp * fsdp)
+    aligned = own % 16 == 0
 
     def body(a_ref, g_ref, out_ref, cols):
         step = pl.program_id(0)
@@ -219,22 +265,37 @@
                         : half - top, int(r != 1), : half - left, int(c != 1)
                     ]
 
-        taps = cols[...].reshape(half * half * batch, middle)
-        out_ref[0] = lax.dot_general(
-            taps, g_ref[...], (((0,), (0,)), ((), ())), preferred_element_type=F32
-        ).astype(BF)
-
-    return call(
+        value = tn(cols[...].reshape(half * half * batch, middle), g_ref[...]).astype(BF)
+        if not aligned:
+            out_ref[0] = value
+            return
+        value = value.reshape(dp, fsdp // 2, 2, own, middle)
+        for place, d in enumerate(by_low_bit(dp)):
+            for f in range(fsdp // 2):
+                for core in range(2):
+                    out_ref[core, place, f] = value[d, f, core]
+
+    if aligned:
+        out = ((2, dp, fsdp // 2, 9 * own, middle), BF)
+        out_block = (2, dp, fsdp // 2, own, middle), lambda t: (0, 0, 0, t, 0)
+    else:
+        out = ((9, middle, middle), BF)
+        out_block = (1, middle, middle), lambda t: (t, 0, 0)
+    value = call(
         body,
         (9,),
         (split, grad.reshape(-1, middle)),
         (whole(split.shape), whole((half * half * batch, middle))),
-        (((9, middle, middle), BF),),
-        (((1, middle, middle), lambda t: (t, 0, 0)),),
+        (out,),
+        (out_block,),
         scratch=[pltpu.VMEM((half, half, batch, middle), BF)],
         flops=2 * half * half * batch * 9 * middle * middle,
         moved=act_a.size * 2 + grad.size * 2 + 18 * middle * middle,
     )[0]
+    if not aligned:
+        value = value.reshape(9, dp, fsdp // 2, 2, own, middle).transpose(3, 1, 2, 0, 4, 5)
+        value = value.reshape(2, dp, fsdp // 2, 9 * own, middle)[:, jnp.array(by_low_bit(dp))]
+    return value
 
 
 def kernel_conv_down_back(grad, taps, raw_a, stats, mask):
@@ -243,7 +304,7 @@
     rows = half * batch
 
     def body(g_ref, n_ref, a_ref, s_ref, m_ref, *refs):
-        w_refs, (out_ref, sum_ref, here, below) = refs[:9], refs[9:]
+        w_refs, (out_ref, send_ref, here, below, sum_ref) = refs[:9], refs[9:]
         step = pl.program_id(0)
 
         @pl.when(step == 0)
@@ -283,14 +344,15 @@
             back = tap(*parts[0])
             for part in parts[1:]:
                 back = back + tap(*part)
-            raw = a_ref[0, p, :, q]
+            raw = a_ref[0, p, :, q].astype(F32)
             norm = raw * al + be
             sig, act = silu_parts(norm)
             slope = sig + act * (1.0 - sig)
             out = back.reshape(half, batch, middle) * slope * m
-            out_ref[0, p, :, q] = out
+            out_ref[0, p, :, q] = out.astype(BF)
             sum_ref[0] += jnp.sum(out, axis=0)
             sum_ref[1] += jnp.sum(out * ((raw - mean) * inv), axis=0)
+        send_sums(send_ref, sum_ref, step == half - 1)
 
     return call(
         body,
@@ -306,103 +368,145 @@
         )
         + tuple(t.block() for t in taps),
         (
-            ((half, 2, half, 2, batch, middle), F32),
-            ((2, batch, middle), F32),
+            ((half, 2, half, 2, batch, middle), BF),
+            (exchange_shape(2 * middle), F32),
         ),
         (
             ((1, 2, half, 2, batch, middle), lambda i: (i, 0, 0, 0, 0, 0)),
-            whole((2, batch, middle)),
-        ),
-        scratch=[pltpu.VMEM((half + 1, batch, middle), BF), pltpu.VMEM((half + 1, batch, middle), BF)],
+            whole(exchange_shape(2 * middle)),
+        ),
+        scratch=[
+            pltpu.VMEM((half + 1, batch, middle), BF),
+            pltpu.VMEM((half + 1, batch, middle), BF),
+            pltpu.VMEM((2, batch, middle), F32),
+        ],
         flops=2 * half * rows * 9 * middle * middle,
         moved=raw_a.size * 8 + 18 * middle * middle,
     )
 
 
-def kernel_first_grad(grad, raw_a, feats, stats, mask, slots, frames):
+def kernel_first_grad(grad, raw_a, feats, stats, mask, frames):
     height, _, batch, middle = raw_a.shape
     half = height // 2
     rows = half * height * frames
-    c_in = feats.shape[1]
+    line = height * frames
+    slots, _, c_in = feats.shape
 
     def body(g_ref, a_ref, x_ref, s_ref, m_ref, out_ref, w_ref, acc):
         first = (pl.program_id(0) == 0) & (pl.program_id(1) == 0)
-        last = (pl.program_id(0) == slots - 1) & (pl.program_id(1) == 1)
+        last = (pl.program_id(0) == slots // 2 - 1) & (pl.program_id(1) == 1)
 
         @pl.when(first)
         def _():
             acc[...] = jnp.zeros_like(acc)
 
-        scale, mean, inv = s_ref[0:1], s_ref[1:2], s_ref[2:3]
-        shift, spread = s_ref[3:4], s_ref[4:5]
-        m = m_ref[:, :1]
-        unit = (a_ref[...] - mean) * inv
-        value = scale * (g_ref[...] - m * (shift + unit * spread))
-        value = value.reshape(rows, middle).astype(BF)
-        out_ref[...] = value
-        acc[...] += lax.dot_general(
-            x_ref[...], value, (((0,), (0,)), ((), ())), preferred_element_type=F32
-        )
+        m = m_ref[...]
+        for c in chunks(middle):
+            scale, mean, shift, spread = (s_ref[n : n + 1, c] for n in range(4))
+            for r in range(half):
+                raw = a_ref[r, :, :, c].astype(F32)
+                value = scale * g_ref[r, :, :, c].astype(F32) - m * (shift + (raw - mean) * spread)
+                for clip in range(2):
+                    part = value[:, clip * frames : (clip + 1) * frames]
+                    out_ref[clip, r * line : (r + 1) * line, c] = part.reshape(line, -1).astype(BF)
+        for clip in range(2):
+            acc[...] += tn(x_ref[clip], out_ref[clip])
 
         @pl.when(last)
         def _():
             w_ref[...] = acc[...].astype(BF)
 
-    block = (half, height, frames, middle)
+    block = (half, height, 2 * frames, middle), lambda c, h: (h, 0, c, 0)
     return call(
         body,
-        (slots, 2),
+        (slots // 2, 2),
         (grad.reshape(raw_a.shape), raw_a, feats, stats, mask),
         (
-            (block, lambda c, h: (h, 0, c, 0)),
-            (block, lambda c, h: (h, 0, c, 0)),
-            ((rows, c_in), lambda c, h: (c * 2 + h, 0)),
+            block,
+            block,
+            ((2, rows, c_in), lambda c, h: (c, h, 0)),
             whole(stats.shape),
-            ((frames, mask.shape[1]), lambda c, h: (c, 0)),
-        ),
-        (
-            ((slots * 2 * rows, middle), BF),
+            ((2 * frames, mask.shape[1]), lambda c, h: (c, 0)),
+        ),
+        (
+            ((slots, 2 * rows, middle), BF),
             ((c_in, middle), BF),
         ),
         (
-            ((rows, middle), lambda c, h: (c * 2 + h, 0)),
+            ((2, rows, middle), lambda c, h: (c, h, 0)),
             whole((c_in, middle)),
         ),
         scratch=[pltpu.VMEM((c_in, middle), F32)],
         flops=2 * raw_a.size * c_in,
-        moved=raw_a.size * 10 + feats.size * 2,
-    )
-
-
-def kernel_grad_features(grad, weight, sampled, height, slots, frames):
+        moved=raw_a.size * 6 + feats.size * 2,
+    )
+
+
+def kernel_grad_features(grad, weight, shortcut, project, height, frames, pair, into=None):
     c_in, middle = weight.shape
+    slots, all_rows, _ = grad.shape
     half = height // 2
-    rows = height * height * frames
-
-    def body(g_ref, w_ref, s_ref, out_ref):
-        value = lax.dot_general(
-            g_ref[...], w_ref[...], (((1,), (1,)), ((), ())), preferred_element_type=F32
+    pixels, batch, wide = shortcut.shape
+    size = 256
+    parts = c_in // size
+
+    def body(g_ref, w_ref, s_ref, p_ref, *refs):
+        out_ref = refs[-1]
+        even = None
+        for k in range(project.count):
+            left = s_ref[:, :, k * middle : (k + 1) * middle].reshape(pixels * 2 * frames, middle)
+            part = nt(left, project.of(p_ref, k))
+            even = part if even is None else even + part
+        even = even.reshape(half, half, 2, frames, size)
+        for clip in range(2):
+            value = nt(g_ref[clip], w_ref[...]).reshape(half, 2, half, 2, frames, size)
+            both = jnp.stack([value[:, 0, :, 0] + even[:, :, clip], value[:, 0, :, 1]], axis=2)
+            line = jnp.stack([both, value[:, 1]], axis=1)
+            out_ref[clip] = line.reshape(all_rows, size).astype(BF)
+
+    groups, _, _ = project.array.shape
+    if groups == 1:
+        size_rows = project.rows // parts
+        project_block = pl.BlockSpec((1, project.count * project.rows, middle), lambda n: (0, 0, 0))
+    else:
+        project_block = pl.BlockSpec(
+            (groups // parts, project.count * project.rows, middle), lambda n: (n, 0, 0)
         )
-        value = value.reshape(half, 2, half, 2, frames, c_in)
-        even = value[:, 0, :, 0] + s_ref[...]
-        line = jnp.stack([even, value[:, 0, :, 1]], axis=2)
-        both = jnp.stack([line, value[:, 1]], axis=1)
-        out_ref[...] = both.reshape(rows, c_in).astype(BF)
-
-    return call(
-        body,
-        (slots,),
-        (grad, weight, sampled),
-        (
-            ((rows, middle), lambda c: (c, 0)),
-            whole(weight.shape),
-            ((half, half, frames, c_in), lambda c: (0, 0, c, 0)),
-        ),
-        (((slots * rows, c_in), BF),),
-        (((rows, c_in), lambda c: (c, 0)),),
-        flops=2 * grad.size * c_in,
-        moved=grad.size * 2 + slots * rows * c_in * 2 + sampled.size * 4,
-    )[0]
+    if groups == 1:
+
+        def of(ref, k):
+            begin = k * project.rows + pl.program_id(0) * size_rows
+            return ref[0, pl.ds(pl.multiple_of(begin, size_rows), size_rows), :]
+
+        project.of = of
+    ins = (grad, weight, shortcut, project.array)
+    in_specs = [
+        pl.BlockSpec((2, all_rows, middle), lambda n: (pair, 0, 0)),
+        pl.BlockSpec((size, middle), lambda n: (n, 0)),
+        pl.BlockSpec((pixels, 2 * frames, wide), lambda n: (0, pair, 0)),
+        project_block,
+    ]
+    alias = {}
+    if into is not None:
+        ins += (into,)
+        in_specs.append(pl.BlockSpec(memory_space=pl.ANY))
+        alias = {4: 0}
+    return pl.pallas_call(
+        body,
+        grid=(parts,),
+        in_specs=in_specs,
+        out_specs=pl.BlockSpec((2, all_rows, size), lambda n: (pair, 0, n)),
+        out_shape=jax.ShapeDtypeStruct((slots, all_rows, c_in), BF),
+        input_output_aliases=alias,
+        compiler_params=pltpu.CompilerParams(
+            vmem_limit_bytes=56 * 1024 * 1024, dimension_semantics=("arbitrary",)
+        ),
+        cost_estimate=pl.CostEstimate(
+            flops=(grad.size + shortcut.size) * c_in,
+            bytes_accessed=grad.size + shortcut.size + slots * all_rows * c_in,
+            transcendentals=0,
+        ),
+    )(*ins)
 
 
 CHUNK = 256
@@ -435,6 +539,12 @@
         size, index = self.rows * self.count, self.first // self.count
         return (self.array.shape[0], size, self.array.shape[2]), lambda *_: (0, index, 0)
 
+    def part(self, ref, k, size):
+        if self.array.shape[0] == 1:
+            return ref[0, k * size : (k + 1) * size, :]
+        parts = size // self.rows
+        return ref[k * parts : (k + 1) * parts].reshape(size, -1)
+
     def of(self, ref, k):
         part = ref[:, k * self.rows : (k + 1) * self.rows, :]
         return part.reshape(-1, part.shape[-1])
@@ -457,22 +567,29 @@
     wide = weight.count * middle
     rows = half * batch
 
-    def body(b_ref, s_ref, m_ref, w_ref, act_ref, raw_ref, sum_ref):
+    def body(b_ref, s_ref, m_ref, w_ref, act_ref, raw_ref, off_ref, sum_ref):
         zero_first(sum_ref)
         m = m_ref[...]
 
-        @pl.loop(0, half)
-        def _(j):
-            for c in chunks(middle):
-                norm = b_ref[j, :, c] * s_ref[0:1, c] + s_ref[1:2, c]
-                act_ref[j, :, c] = (silu_parts(norm)[1] * m).astype(BF)
+        for c in chunks(middle):
+            al, be = s_ref[0:1, c], s_ref[1:2, c]
+            for j in range(half):
+                act_ref[j, :, c] = (silu_parts(b_ref[j, :, c] * al + be)[1] * m).astype(BF)
+
+
+        @pl.when(pl.program_id(0) == 0)
+        def _():
+            for k in range(weight.count):
+                few = nn(act_ref[half // 2], weight.of(w_ref, k))
+                off_ref[0:1, k * middle : (k + 1) * middle] = mean_of(few, m_ref[:, :1])
 
         m = m_ref[:, :1]
         act = act_ref[...].reshape(rows, middle)
         for k in range(weight.count):
             raw = nn(act, weight.of(w_ref, k)).reshape(half, batch, middle)
             span = slice(k * middle, (k + 1) * middle)
-            raw_ref[:, :, span] = raw
+            offset = off_ref[0:1, span]
+            raw_ref[:, :, span] = (raw - offset).astype(BF)
             sum_ref[0, :, span] += fold(jnp.sum(raw, axis=0) * m)
             sum_ref[1, :, span] += fold(jnp.sum(raw * raw, axis=0) * m)
 
@@ -484,10 +601,10 @@
         (row_block(half, batch, middle), whole(stats.shape), whole(mask.shape), weight.block()),
         (
             ((pixels, batch, middle), BF),
-            ((pixels, batch, wide), F32),
+            ((pixels, batch, wide), BF), ((8, wide), F32),
             ((2, 8, wide), F32),
         ),
-        (row_block(half, batch, middle), row_block(half, batch, wide), whole((2, 8, wide))),
+        (row_block(half, batch, middle), row_block(half, batch, wide), whole((8, wide)), whole((2, 8, wide))),
         flops=2 * raw_b.size * wide,
         moved=raw_b.size * 6 + pixels * batch * wide * 4,
     )
@@ -498,14 +615,22 @@
     middle = weight.array.shape[2]
     wide = weight.count * middle
 
-    def body(x_ref, m_ref, w_ref, raw_ref, sum_ref):
+    def body(x_ref, m_ref, w_ref, raw_ref, off_ref, sum_ref):
         zero_first(sum_ref)
+
+        @pl.when(pl.program_id(0) == 0)
+        def _():
+            for k in range(weight.count):
+                few = nn(x_ref[half // 2], weight.of(w_ref, k))
+                off_ref[0:1, k * middle : (k + 1) * middle] = mean_of(few, m_ref[:, :1])
+
         m = m_ref[:, :1]
         left = x_ref[...].reshape(half * batch, c_in)
         for k in range(weight.count):
             raw = nn(left, weight.of(w_ref, k)).reshape(half, batch, middle)
             span = slice(k * middle, (k + 1) * middle)
-            raw_ref[:, :, span] = raw
+            offset = off_ref[0:1, span]
+            raw_ref[:, :, span] = (raw - offset).astype(BF)
             sum_ref[0, :, span] += fold(jnp.sum(raw, axis=0) * m)
             sum_ref[1, :, span] += fold(jnp.sum(raw * raw, axis=0) * m)
 
@@ -514,8 +639,8 @@
         (half,),
         (sampled, mask, weight.array),
         (row_block(half, batch, c_in), whole(mask.shape), weight.block()),
-        (((pixels, batch, wide), F32), ((2, 8, wide), F32)),
-        (row_block(half, batch, wide), whole((2, 8, wide))),
+        (((pixels, batch, wide), BF), ((8, wide), F32), ((2, 8, wide), F32)),
+        (row_block(half, batch, wide), whole((8, wide)), whole((2, 8, wide))),
         flops=2 * sampled.size * wide,
         moved=sampled.size * 2 + pixels * batch * wide * 4,
     )
@@ -525,22 +650,27 @@
     pixels, batch, wide = raw_c.shape
     middle = weight.array.shape[2]
 
-    def body(c_ref, p_ref, s_ref, m_ref, w_ref, one_ref, raw_ref, sum_ref):
+    def body(c_ref, p_ref, s_ref, m_ref, w_ref, one_ref, raw_ref, send_ref, sum_ref):
         zero_first(sum_ref)
         m = m_ref[...]
 
-        @pl.loop(0, half)
-        def _(j):
-            for c in chunks(wide):
-                total = c_ref[j, :, c] * s_ref[0:1, c] + p_ref[j, :, c] * s_ref[1:2, c] + s_ref[2:3, c]
-                one_ref[j, :, c] = (silu_parts(total)[1] * m).astype(BF)
-
+        raw = None
+        for k in range(wide // middle):
+            for c in chunks(middle):
+                c = slice(k * middle + c.start, k * middle + c.stop)
+                al, ap, be = s_ref[0:1, c], s_ref[1:2, c], s_ref[2:3, c]
+                for j in range(half):
+                    total = c_ref[j, :, c].astype(F32) * al + p_ref[j, :, c].astype(F32) * ap + be
+                    one_ref[j, :, c] = (silu_parts(total)[1] * m).astype(BF)
+            left = one_ref[:, :, k * middle : (k + 1) * middle].reshape(half * batch, middle)
+            part = nn(left, weight.part(w_ref, k, middle))
+            raw = part if raw is None else raw + part
+        raw = raw.reshape(half, batch, middle)
         m = m_ref[:, :1]
-        raw = nn(one_ref[...].reshape(half * batch, wide), weight.of(w_ref, 0))
-        raw = raw.reshape(half, batch, middle)
         raw_ref[...] = raw
         sum_ref[0] += fold(jnp.sum(raw, axis=0) * m)
         sum_ref[1] += fold(jnp.sum(raw * raw, axis=0) * m)
+        send_sums(send_ref, sum_ref, pl.program_id(0) == half - 1)
 
     return call(
         body,
@@ -556,9 +686,10 @@
         (
             ((pixels, batch, wide), BF),
             ((pixels, batch, middle), F32),
-            ((2, 8, middle), F32),
-        ),
-        (row_block(half, batch, wide), row_block(half, batch, middle), whole((2, 8, middle))),
+            (exchange_shape(2 * middle), F32),
+        ),
+        (row_block(half, batch, wide), row_block(half, batch, middle), whole(exchange_shape(2 * middle))),
+        scratch=[pltpu.VMEM((2, 8, middle), F32)],
         flops=2 * raw_c.size * middle,
         moved=raw_c.size * 10,
     )
@@ -566,23 +697,30 @@
 
 def kernel_result(raw_e, block_one, cot, stats, mask, half):
     pixels, batch, wide = raw_e.shape
+    slots, _, _, frames, _ = cot.shape
 
     def body(e_ref, o_ref, g_ref, s_ref, m_ref, res_ref, grad_ref, sum_ref):
         zero_first(sum_ref)
         m = m_ref[...]
-
-        @pl.loop(0, half)
-        def _(j):
-            for c in chunks(wide):
-                raw = e_ref[j, :, c]
-                total = raw * s_ref[0:1, c] + s_ref[1:2, c] + o_ref[j, :, c].astype(F32)
-                sig, act = silu_parts(total)
-                res_ref[j, :, c] = (act * m).astype(BF)
-                grad = g_ref[j, :, c].astype(F32) * m * (sig + act * (1.0 - sig))
-                grad_ref[j, :, c] = grad
-                sum_ref[0, :, c] += fold(grad)
-                sum_ref[1, :, c] += fold(grad * ((raw - s_ref[2:3, c]) * s_ref[3:4, c]))
-
+        for c in chunks(wide):
+            al, be, mean = s_ref[0:1, c], s_ref[1:2, c], s_ref[2:3, c]
+            first = second = None
+            for j in range(half):
+                raw = e_ref[j, :, c].astype(F32)
+                sig, act = silu_parts(raw * al + be + o_ref[j, :, c].astype(F32))
+                res = act * m
+                for s in range(slots):
+                    res_ref[s, 0, j, :, c] = res[s * frames : (s + 1) * frames].astype(BF)
+                cot = jnp.concatenate([g_ref[s, 0, j, :, c].astype(F32) for s in range(slots)])
+                grad = cot * m * (sig + act * (1.0 - sig))
+                grad_ref[j, :, c] = grad.astype(BF)
+                other = grad * (raw - mean)
+                first = grad if first is None else first + grad
+                second = other if second is None else second + other
+            sum_ref[0, :, c] += fold(first)
+            sum_ref[1, :, c] += fold(second)
+
+    outside = (slots, 1, half, frames, wide), lambda i: (0, i, 0, 0, 0)
     return call(
         body,
         (half,),
@@ -590,16 +728,16 @@
         (
             row_block(half, batch, wide),
             row_block(half, batch, wide),
-            row_block(half, batch, wide),
+            outside,
             whole(stats.shape),
             whole(mask.shape),
         ),
         (
+            (cot.shape, BF),
             ((pixels, batch, wide), BF),
-            ((pixels, batch, wide), F32),
             ((2, 8, wide), F32),
         ),
-        (row_block(half, batch, wide), row_block(half, batch, wide), whole((2, 8, wide))),
+        (outside, row_block(half, batch, wide), whole((2, 8, wide))),
         flops=20 * raw_e.size,
         moved=raw_e.size * 14,
     )
@@ -613,29 +751,28 @@
         zero_first(sum_ref)
         m = m_ref[...]
 
-        @pl.loop(0, half)
-        def _(j):
-            for c in chunks(middle):
-                unit = (d_ref[j, :, c] - sd_ref[1:2, c]) * sd_ref[2:3, c]
-                value = sd_ref[0:1, c] * (
-                    n_ref[j, :, c] - m * (sd_ref[3:4, c] + unit * sd_ref[4:5, c])
-                )
+        for c in chunks(middle):
+            scale, mean, shift, spread = (sd_ref[n : n + 1, c] for n in range(4))
+            for j in range(half):
+                value = scale * n_ref[j, :, c] - m * (shift + (d_ref[j, :, c] - mean) * spread)
                 nar_ref[j, :, c] = value.astype(BF)
 
         left = nar_ref[...].reshape(half * batch, middle)
-        back[...] = nt(left, weight.of(w_ref, 0)).reshape(half, batch, wide)
-
-        @pl.loop(0, half)
-        def _(j):
-            for c in chunks(wide):
-                raw_c, raw_p = c_ref[j, :, c], p_ref[j, :, c]
-                total = raw_c * s_ref[0:1, c] + raw_p * s_ref[1:2, c] + s_ref[2:3, c]
-                sig, act = silu_parts(total)
-                grad = (t_ref[j, :, c] + back[j, :, c]) * m * (sig + act * (1.0 - sig))
-                one_ref[j, :, c] = grad
-                sum_ref[0, :, c] += fold(grad)
-                sum_ref[1, :, c] += fold(grad * ((raw_c - s_ref[3:4, c]) * s_ref[4:5, c]))
-                sum_ref[2, :, c] += fold(grad * ((raw_p - s_ref[5:6, c]) * s_ref[6:7, c]))
+        for k in range(wide // middle):
+            back[k] = nt(left, weight.part(w_ref, k, middle)).reshape(half, batch, middle)
+            for d in chunks(middle):
+                c = slice(k * middle + d.start, k * middle + d.stop)
+                al, ap, be, mean_c, _, mean_p = (s_ref[n : n + 1, c] for n in range(6))
+                sums = [None] * 3
+                for j in range(half):
+                    raw_c, raw_p = c_ref[j, :, c].astype(F32), p_ref[j, :, c].astype(F32)
+                    sig, act = silu_parts(raw_c * al + raw_p * ap + be)
+                    grad = (t_ref[j, :, c].astype(F32) + back[k, j, :, d]) * m * (sig + act * (1.0 - sig))
+                    one_ref[j, :, c] = grad.astype(BF)
+                    parts = (grad, grad * (raw_c - mean_c), grad * (raw_p - mean_p))
+                    sums = [p if t is None else t + p for t, p in zip(sums, parts)]
+                for n in range(3):
+                    sum_ref[n, :, c] += fold(sums[n])
 
     return call(
         body,
@@ -654,11 +791,11 @@
         ),
         (
             ((pixels, batch, middle), BF),
-            ((pixels, batch, wide), F32),
+            ((pixels, batch, wide), BF),
             ((3, 8, wide), F32),
         ),
         (row_block(half, batch, middle), row_block(half, batch, wide), whole((3, 8, wide))),
-        scratch=[pltpu.VMEM((half, batch, wide), F32)],
+        scratch=[pltpu.VMEM((wide // middle, half, batch, middle), F32)],
         flops=2 * raw_c.size * middle,
         moved=raw_c.size * 16,
     )
@@ -668,33 +805,31 @@
     pixels, batch, wide = raw_c.shape
     middle = raw_b.shape[2]
 
-    def body(g_ref, c_ref, p_ref, s_ref, w_ref, b_ref, sb_ref, m_ref, wid_ref, sho_ref, out_ref, sum_ref):
+    def body(g_ref, c_ref, p_ref, s_ref, w_ref, b_ref, sb_ref, m_ref, wid_ref, sho_ref, out_ref, send_ref, sum_ref):
         zero_first(sum_ref)
         m = m_ref[...]
-
-        @pl.loop(0, half)
-        def _(j):
-            for c in chunks(wide):
-                grad = g_ref[j, :, c]
-                for raw_ref, to_ref, k in ((c_ref, wid_ref, 0), (p_ref, sho_ref, 5)):
-                    unit = (raw_ref[j, :, c] - s_ref[k + 1 : k + 2, c]) * s_ref[k + 2 : k + 3, c]
-                    value = s_ref[k : k + 1, c] * (
-                        grad - m * (s_ref[k + 3 : k + 4, c] + unit * s_ref[k + 4 : k + 5, c])
-                    )
-                    to_ref[j, :, c] = value.astype(BF)
-
-        m = m_ref[:, :1]
         back = None
         for k in range(weight.count):
+            for c in chunks(middle):
+                c = slice(k * middle + c.start, k * middle + c.stop)
+                rows_s = [s_ref[n : n + 1, c] for n in range(8)]
+                for j in range(half):
+                    grad = g_ref[j, :, c].astype(F32)
+                    for raw_ref, to_ref, n in ((c_ref, wid_ref, 0), (p_ref, sho_ref, 4)):
+                        scale, mean, shift, spread = rows_s[n : n + 4]
+                        value = scale * grad - m * (shift + (raw_ref[j, :, c].astype(F32) - mean) * spread)
+                        to_ref[j, :, c] = value.astype(BF)
             left = wid_ref[:, :, k * middle : (k + 1) * middle].reshape(half * batch, middle)
             part = nt(left, weight.of(w_ref, k))
             back = part if back is None else back + part
+        m = m_ref[:, :1]
         raw = b_ref[...]
         sig, act = silu_parts(raw * sb_ref[0:1] + sb_ref[1:2])
         grad = back.reshape(half, batch, middle) * m * (sig + act * (1.0 - sig))
         out_ref[...] = grad
         sum_ref[0] += fold(jnp.sum(grad, axis=0))
         sum_ref[1] += fold(jnp.sum(grad * ((raw - sb_ref[2:3]) * sb_ref[3:4]), axis=0))
+        send_sums(send_ref, sum_ref, pl.program_id(0) == half - 1)
 
     return call(
         body,
@@ -714,42 +849,18 @@
             ((pixels, batch, wide), BF),
             ((pixels, batch, wide), BF),
             ((pixels, batch, middle), F32),
-            ((2, 8, middle), F32),
+            (exchange_shape(2 * middle), F32),
         ),
         (
             row_block(half, batch, wide),
             row_block(half, batch, wide),
             row_block(half, batch, middle),
-            whole((2, 8, middle)),
-        ),
+            whole(exchange_shape(2 * middle)),
+        ),
+        scratch=[pltpu.VMEM((2, 8, middle), F32)],
         flops=2 * raw_c.size * middle,
         moved=raw_c.size * 16,
     )
-
-
-def kernel_sampled_back(grad, weight, half):
-    pixels, batch, wide = grad.shape
-    middle = weight.array.shape[2]
-    c_in = weight.array.shape[0] * weight.rows
-
-    def body(g_ref, w_ref, out_ref):
-        back = None
-        for k in range(weight.count):
-            left = g_ref[:, :, k * middle : (k + 1) * middle].reshape(half * batch, middle)
-            part = nt(left, weight.of(w_ref, k))
-            back = part if back is None else back + part
-        out_ref[...] = back.reshape(half, batch, c_in)
-
-    return call(
-        body,
-        (half,),
-        (grad, weight.array),
-        (row_block(half, batch, wide), weight.block()),
-        (((pixels, batch, c_in), F32),),
-        (row_block(half, batch, c_in),),
-        flops=2 * grad.size * c_in,
-        moved=grad.size * 2 + pixels * batch * c_in * 4,
-    )[0]
 
 
 def kernel_join(excited, outputs, raw_g, stats_g, mask, weight, half):
@@ -757,7 +868,7 @@
     group = middle // 4
     wide = weight.count * middle
 
-    def body(x_ref, o1, o2, r_ref, sg_ref, m_ref, w_ref, join_ref, raw_ref, sum_ref):
+    def body(x_ref, o1, o2, r_ref, sg_ref, m_ref, w_ref, join_ref, raw_ref, off_ref, sum_ref):
         zero_first(sum_ref)
         m = m_ref[:, :group]
         join_ref[:, :, :group] = x_ref[...]
@@ -765,12 +876,20 @@
         join_ref[:, :, 2 * group : 3 * group] = o2[...]
         act = silu_parts(r_ref[...] * sg_ref[0:1] + sg_ref[1:2])[1] * m
         join_ref[:, :, 3 * group :] = act.astype(BF)
+
+        @pl.when(pl.program_id(0) == 0)
+        def _():
+            for k in range(weight.count):
+                few = nn(join_ref[half // 2], weight.of(w_ref, k))
+                off_ref[0:1, k * middle : (k + 1) * middle] = mean_of(few, m_ref[:, :1])
+
         left = join_ref[...].reshape(half * batch, middle)
         m = m_ref[:, :1]
         for k in range(weight.count):
             raw = nn(left, weight.of(w_ref, k)).reshape(half, batch, middle)
             span = slice(k * middle, (k + 1) * middle)
-            raw_ref[:, :, span] = raw
+            offset = off_ref[0:1, span]
+            raw_ref[:, :, span] = (raw - offset).astype(BF)
             sum_ref[0, :, span] += fold(jnp.sum(raw, axis=0) * m)
             sum_ref[1, :, span] += fold(jnp.sum(raw * raw, axis=0) * m)
 
@@ -780,8 +899,8 @@
         (half,),
         (excited, outputs[0], outputs[1], raw_g, stats_g, mask, weight.array),
         (part, part, part, part, whole(stats_g.shape), whole(mask.shape), weight.block()),
-        (((pixels, batch, middle), BF), ((pixels, batch, wide), F32), ((2, 8, wide), F32)),
-        (row_block(half, batch, middle), row_block(half, batch, wide), whole((2, 8, wide))),
+        (((pixels, batch, middle), BF), ((pixels, batch, wide), BF), ((8, wide), F32), ((2, 8, wide), F32)),
+        (row_block(half, batch, middle), row_block(half, batch, wide), whole((8, wide)), whole((2, 8, wide))),
         flops=2 * excited.size * wide,
         moved=excited.size * 4 + pixels * batch * wide * 4,
     )
@@ -792,21 +911,20 @@
     middle = weight.array.shape[2]
     group = middle // 4
 
-    def body(g_ref, e_ref, s_ref, m_ref, w_ref, r_ref, sg_ref, fin_ref, out_ref, pre_ref, sum_ref):
+    def body(g_ref, e_ref, s_ref, m_ref, w_ref, r_ref, sg_ref, fin_ref, out_ref, pre_ref, send_ref, sum_ref):
         zero_first(sum_ref)
         m = m_ref[...]
 
-        @pl.loop(0, half)
-        def _(j):
-            for c in chunks(wide):
-                unit = (e_ref[j, :, c] - s_ref[1:2, c]) * s_ref[2:3, c]
-                value = s_ref[0:1, c] * (
-                    g_ref[j, :, c] - m * (s_ref[3:4, c] + unit * s_ref[4:5, c])
-                )
-                fin_ref[j, :, c] = value.astype(BF)
-
         back = None
         for k in range(weight.count):
+            for c in chunks(middle):
+                c = slice(k * middle + c.start, k * middle + c.stop)
+                scale, mean, shift, spread = (s_ref[n : n + 1, c] for n in range(4))
+                for j in range(half):
+                    value = scale * g_ref[j, :, c].astype(F32) - m * (
+                        shift + (e_ref[j, :, c].astype(F32) - mean) * spread
+                    )
+                    fin_ref[j, :, c] = value.astype(BF)
             left = fin_ref[:, :, k * middle : (k + 1) * middle].reshape(half * batch, middle)
             part = nt(left, weight.of(w_ref, k))
             back = part if back is None else back + part
@@ -818,6 +936,7 @@
         pre_ref[...] = pre
         sum_ref[0] += fold(jnp.sum(pre, axis=0))
         sum_ref[1] += fold(jnp.sum(pre * (raw - sg_ref[2:3]), axis=0))
+        send_sums(send_ref, sum_ref, pl.program_id(0) == half - 1)
 
     part = row_block(half, batch, group)
     return call(
@@ -837,9 +956,10 @@
             ((pixels, batch, wide), BF),
             ((pixels, batch, middle), F32),
             ((pixels, batch, group), F32),
-            ((2, 8, group), F32),
-        ),
-        (row_block(half, batch, wide), row_block(half, batch, middle), part, whole((2, 8, group))),
+            (exchange_shape(2 * group), F32),
+        ),
+        (row_block(half, batch, wide), row_block(half, batch, middle), part, whole(exchange_shape(2 * group))),
+        scratch=[pltpu.VMEM((2, 8, group), F32)],
         flops=2 * raw_e.size * middle,
         moved=raw_e.size * 10,
     )
@@ -970,12 +1090,12 @@
 
     def body(*refs):
         if index == 1:
-            x_ref, e_ref, t_ref, w_ref, m_ref, first_ref, pad_ref, raw_ref, sum_ref, cols = refs
+            x_ref, e_ref, t_ref, w_ref, m_ref, first_ref, pad_ref, raw_ref, send_ref, cols, sum_ref = refs
             excited = (x_ref[...].astype(F32) * e_ref[...]).astype(BF)
             first_ref[...] = excited
             piece = first_ref[:, :, group : 2 * group].astype(F32)
         else:
-            x_ref, r_ref, s_ref, t_ref, w_ref, m_ref, first_ref, pad_ref, raw_ref, sum_ref, cols = refs
+            x_ref, r_ref, s_ref, t_ref, w_ref, m_ref, first_ref, pad_ref, raw_ref, send_ref, cols, sum_ref = refs
             act = silu_parts(r_ref[...] * s_ref[0:1] + s_ref[1:2])[1] * m_ref[:, :group]
             first_ref[...] = act.astype(BF)
             piece = x_ref[...].astype(F32) + first_ref[...].astype(F32)
@@ -989,6 +1109,7 @@
         m = m_ref[:, :group]
         sum_ref[0] = fold(jnp.sum(raw, axis=0) * m)
         sum_ref[1] = fold(jnp.sum(raw * raw, axis=0) * m)
+        send_sums(send_ref, sum_ref)
 
     block = (pixels, batch, group)
     if index == 1:
@@ -1003,7 +1124,7 @@
         first,
         ((half + 2, half + 2, batch, group), BF),
         (block, F32),
-        ((2, 8, group), F32),
+        (exchange_shape(2 * group), F32),
     )
     return call(
         body,
@@ -1012,7 +1133,7 @@
         specs,
         outs,
         tuple(whole(o[0]) for o in outs),
-        scratch=[pltpu.VMEM((pixels * batch, 9 * group), BF)],
+        scratch=[pltpu.VMEM((pixels * batch, 9 * group), BF), pltpu.VMEM((2, 8, group), F32)],
         flops=2 * pixels * batch * 9 * group * group,
         moved=pixels * batch * group * 12,
     )
@@ -1047,12 +1168,12 @@
 
     def body(*refs):
         g_ref, r_ref, s_ref, w_ref, t_ref, x_ref, j_ref, m_ref = refs[:8]
-        pad, cols = refs[-2:]
+        pad, cols, sum_ref = refs[-3:]
         m = m_ref[:, :group]
         raw = r_ref[...]
         value = s_ref[0:1] * g_ref[...] - m * (s_ref[2:3] + (raw - s_ref[1:2]) * s_ref[3:4])
         if index > 1:
-            p_ref, l_ref, ls_ref, gg_ref, gp_ref, tg_ref, pre_ref, sum_ref = refs[8:16]
+            p_ref, l_ref, ls_ref, gg_ref, gp_ref, tg_ref, pre_ref, send_ref = refs[8:16]
         else:
             g2_ref, g3_ref, d_ref, gg_ref, gp_ref, tg_ref, at_ref = refs[8:15]
         gg_ref[...] = value.astype(BF)
@@ -1076,6 +1197,7 @@
             pre_ref[...] = pre
             sum_ref[0] = fold(jnp.sum(pre, axis=0))
             sum_ref[1] = fold(jnp.sum(pre * (raw - ls_ref[2:3]), axis=0))
+            send_sums(send_ref, sum_ref)
         else:
             for k, source in enumerate((j_ref, gp_ref, g2_ref, g3_ref)):
                 span = slice(k * group, (k + 1) * group)
@@ -1089,7 +1211,7 @@
     outs = [(block, BF), (block, F32), ((3, 8, group), F32)]
     if index > 1:
         more = [previous, lower[0], lower[1]]
-        outs += [(block, F32), ((2, 8, group), F32)]
+        outs += [(block, F32), (exchange_shape(2 * group), F32)]
     else:
         more = list(previous)
         outs += [((batch, 4 * group), F32)]
@@ -1103,6 +1225,7 @@
         scratch=[
             pltpu.VMEM((half + 2, half + 2, batch, group), BF),
             pltpu.VMEM((rows, 9 * group), BF),
+            pltpu.VMEM((2, 8, group), F32),
         ],
         flops=2 * rows * 9 * group * group,
         moved=rows * group * 24,
@@ -1116,7 +1239,7 @@
     narrow = raw_m.shape[2]
     group = middle // 4
 
-    def body(j_ref, p1, p2, p3, e_ref, d_ref, sd_ref, r_ref, k_ref, c_ref, sm_ref, w_ref, m_ref, out_ref, mg_ref, sum_ref):
+    def body(j_ref, p1, p2, p3, e_ref, d_ref, sd_ref, r_ref, k_ref, c_ref, sm_ref, w_ref, m_ref, out_ref, mg_ref, send_ref, sum_ref):
         zero_first(sum_ref)
         mn = m_ref[:, :narrow]
         grad = (k_ref[...] * c_ref[0] - c_ref[1]) * mn
@@ -1133,6 +1256,7 @@
             out_ref[:, :, c] = out
             sum_ref[0, :, c] += fold(jnp.sum(out, axis=0))
             sum_ref[1, :, c] += fold(jnp.sum(out * (raw - sd_ref[2:3, c]), axis=0))
+        send_sums(send_ref, sum_ref, pl.program_id(0) == half - 1)
 
     part = row_block(half, batch, group)
     ins = (joined,) + tuple(pieces)
@@ -1159,9 +1283,10 @@
         (
             ((pixels, batch, middle), F32),
             ((pixels, batch, narrow), BF),
-            ((2, 8, middle), F32),
-        ),
-        (row_block(half, batch, middle), row_block(half, batch, narrow), whole((2, 8, middle))),
+            (exchange_shape(2 * middle), F32),
+        ),
+        (row_block(half, batch, middle), row_block(half, batch, narrow), whole(exchange_shape(2 * middle))),
+        scratch=[pltpu.VMEM((2, 8, middle), F32)],
         flops=2 * rows_d.size * narrow,
         moved=rows_d.size * 12,
     )
@@ -1191,6 +1316,10 @@
         high = jnp.where(core == 0, other, mine)
         return jnp.concatenate([low, high])
 
+    def ready(self, copies, count):
+        total = jnp.sum(lax.all_to_all(copies, AXES, 0, 0, tiled=True), axis=(0, 1))
+        return list(total.reshape(count, -1))
+
     def __call__(self, *arrays):
         sizes = [a.size for a in arrays]
         extra = -sum(sizes) % 256
@@ -1230,27 +1359,47 @@
     return both.reshape((dp * fsdp,) + both.shape[3:])
 
 
-def quick_scatter(dp, fsdp, value):
-    shape = value.shape[1:]
-    value = value.astype(BF).reshape((dp, fsdp // 2, 2) + shape).transpose(2, 1, 0, 3, 4)
+def scatter_cores(dp, fsdp, value):
     core = lax.axis_index("fsdp") % 2
     mine = lax.dynamic_index_in_dim(value, core, 0, False)
     other = lax.dynamic_index_in_dim(value, 1 - core, 0, False)
     other = lax.ppermute(other, AXES, pairs_of(dp, fsdp))
-    value = (mine.astype(F32) + other.astype(F32)).astype(BF)
+    return (mine.astype(F32) + other.astype(F32)).astype(BF)
+
+
+def scatter_halves(dp, value, bit):
+    mine = (lax.axis_index("dp") >> bit) & 1
+    other = lax.dynamic_index_in_dim(value, 1 - mine, 0, False)
+    other = lax.ppermute(other, "dp", [(i, i ^ (1 << bit)) for i in range(dp)])
+    mine = lax.dynamic_index_in_dim(value, mine, 0, False)
+    return (mine.astype(F32) + other.astype(F32)).astype(BF)
+
+
+def scatter_fsdp(fsdp, value):
     value = lax.all_to_all(value, "fsdp", 0, 0, axis_index_groups=same_core(fsdp))
-    value = jnp.sum(value.astype(F32), axis=0).astype(BF)
+    return jnp.sum(value.astype(F32), axis=0)
+
+
+def scatter_dp(value):
     return jnp.sum(lax.all_to_all(value, "dp", 0, 0).astype(F32), axis=0)
+
+
+def by_low_bit(count):
+    order = [0]
+    while len(order) < count:
+        order = [2 * i for i in order] + [2 * i + 1 for i in order]
+    return order
 
 
 def after(value, *others):
     return lax.optimization_barrier((value, others))[0]
 
 
-def affine(total, square, count, gain, bias):
+def affine(total, square, count, gain, bias, offset=0.0):
     mean = total / count
     inv = lax.rsqrt(square / count - mean * mean + EPSILON)
     alpha = gain * inv
+    mean = mean - offset
     return mean, inv, alpha, bias - mean * alpha
 
 
@@ -1299,8 +1448,7 @@
     gain = [gains[s : s + w] for s, w in zip(starts, widths)]
     bias = [biases[s : s + w] for s, w in zip(starts, widths)]
 
-    feats = features.transpose(0, 2, 3, 1, 4).reshape(-1, c_in)
-    cot = cotangent.transpose(2, 3, 0, 1, 4)
+    feats = features.transpose(0, 2, 3, 1, 4).reshape(slots, -1, c_in)
 
     def gather(value):
         return lax.all_gather(value, AXES, axis=0, tiled=False)
@@ -1366,7 +1514,7 @@
     full_motion_in = small[:, 0].reshape(middle, narrow)
     full_motion_out = small[:, 1].reshape(middle, narrow).astype(F32)
 
-    raw_a, sums_a = kernel_reduce1(feats, full_reduce1, mask_rows, slots, height, frames)
+    raw_a, off_a, sums_a = kernel_reduce1(feats, full_reduce1, mask_rows, height, frames)
     sum_a, square_a, frame_total, pairs = sums(
         jnp.sum(sums_a[0], axis=0),
         jnp.sum(sums_a[1], axis=0),
@@ -1375,28 +1523,31 @@
     )
     count_big = frame_total * (height * height)
     count = frame_total * area
-    mean_a, inv_a, alpha_a, beta_a = affine(sum_a, square_a, count_big, gain[0], bias[0])
-    act_a, raw_b, sums_b = kernel_conv_down(raw_a, alpha_a[None], beta_a[None], mask_rows, taps1)
+    mean_a, inv_a, alpha_a, beta_a = affine(
+        sum_a, square_a, count_big, gain[0], bias[0], off_a[0]
+    )
+    act_a = kernel_act(raw_a, jnp.stack([alpha_a, beta_a]), mask_rows)
+    raw_b, sums_b = kernel_conv_down(act_a, mask_rows, taps1)
     raw_b = raw_b.reshape(area, batch, middle)
     sampled = (
         features.reshape(slots, frames, half, 2, half, 2, c_in)[:, :, :, 0, :, 0]
         .transpose(2, 3, 0, 1, 4)
         .reshape(area, batch, c_in)
     )
-    raw_p, sums_p = kernel_project(sampled, mask_rows, project1, half)
+    raw_p, off_p, sums_p = kernel_project(sampled, mask_rows, project1, half)
 
     def moments(raw):
         return total_over(raw * mask), total_over(raw * raw * mask)
 
-    sum_b, square_b = sums(jnp.sum(sums_b[0], axis=0), jnp.sum(sums_b[1], axis=0))
+    sum_b, square_b = sums.ready(sums_b, 2)
     mean_b, inv_b, alpha_b, beta_b = affine(sum_b, square_b, count, gain[1], bias[1])
-    act_b, raw_c, sums_c = kernel_expand(
+    act_b, raw_c, off_c, sums_c = kernel_expand(
         raw_b, jnp.stack([alpha_b, beta_b]), mask_rows, expand1, half
     )
     sums_c, sums_p = jnp.sum(sums_c, axis=1), jnp.sum(sums_p, axis=1)
     sum_c, square_c, sum_p, square_p = sums(sums_c[0], sums_c[1], sums_p[0], sums_p[1])
-    mean_c, inv_c, alpha_c, beta_c = affine(sum_c, square_c, count, gain[2], bias[2])
-    mean_p, inv_p, alpha_p, beta_p = affine(sum_p, square_p, count, gain[3], bias[3])
+    mean_c, inv_c, alpha_c, beta_c = affine(sum_c, square_c, count, gain[2], bias[2], off_c[0])
+    mean_p, inv_p, alpha_p, beta_p = affine(sum_p, square_p, count, gain[3], bias[3], off_p[0])
     stats_one = jnp.stack(
         [alpha_c, alpha_p, beta_c + beta_p, mean_c, inv_c, mean_p, inv_p, jnp.zeros_like(mean_p)]
     )
@@ -1404,7 +1555,7 @@
         raw_c, raw_p, stats_one, mask_rows, reduce2, half
     )
 
-    sum_d, square_d = sums(jnp.sum(sums_d[0], axis=0), jnp.sum(sums_d[1], axis=0))
+    sum_d, square_d = sums.ready(sums_d, 2)
     mean_d, inv_d, alpha_d, beta_d = affine(sum_d, square_d, count, gain[4], bias[4])
     inside = [
         [
@@ -1460,8 +1611,7 @@
     )
     pads, raws, stats, outputs = [pad], [raw], [], []
     for k in range(3):
-        total = jnp.sum(partial, axis=1)
-        stats.append(affine(*sums(total[0], total[1]), count, gain[7 + k], bias[7 + k]))
+        stats.append(affine(*sums.ready(partial, 2), count, gain[7 + k], bias[7 + k]))
         if k < 2:
             out, pad, raw, partial = kernel_group(
                 excited,
@@ -1476,12 +1626,12 @@
             pads.append(pad)
             raws.append(raw)
             outputs.append(out)
-    joined, raw_e, sums_e = kernel_join(
+    joined, raw_e, off_e, sums_e = kernel_join(
         excited, outputs, raws[2], jnp.stack(stats[2][2:]), mask_rows, expand2, half
     )
     sums_e = jnp.sum(sums_e, axis=1)
     mean_e, inv_e, alpha_e, beta_e = affine(
-        *sums(sums_e[0], sums_e[1]), count, gain[10], bias[10]
+        *sums(sums_e[0], sums_e[1]), count, gain[10], bias[10], off_e[0]
     )
     def by_owner(values, number):
         return (
@@ -1501,17 +1651,17 @@
     result, grad_total, sums_e = kernel_result(
         raw_e,
         block_one,
-        cot.reshape(area, batch, wide),
-        jnp.stack([alpha_e, beta_e, mean_e, inv_e]),
+        cotangent.transpose(0, 2, 3, 1, 4),
+        jnp.stack([alpha_e, beta_e, mean_e]),
         mask_rows,
         half,
     )
-    result = result.reshape(half, half, slots, frames, wide)
-    shifts[10], spreads[10] = sums(jnp.sum(sums_e[0], axis=0), jnp.sum(sums_e[1], axis=0))
+    sums_e = jnp.sum(sums_e, axis=1)
+    shifts[10], spreads[10] = sums(sums_e[0], sums_e[1] * inv_e)
 
     def back_stats(index, mean, inv):
         scale = gain[index] * inv
-        return [scale, mean, inv, shifts[index] / count, spreads[index] / count]
+        return [scale, mean, scale * shifts[index] / count, scale * inv * spreads[index] / count]
 
     def lower(k):
         return raws[k], jnp.stack([stats[k][2], stats[k][3], stats[k][0]])
@@ -1531,8 +1681,8 @@
     grad_pieces = [None] * 3
     for k in (2, 1, 0):
         mean, inv, alpha, _ = stats[k]
-        partial = jnp.sum(partial, axis=1)
-        shifts[7 + k], spreads[7 + k] = sums(partial[0], partial[1] * inv)
+        shifts[7 + k], spreads[7 + k] = sums.ready(partial, 2)
+        spreads[7 + k] = spreads[7 + k] * inv
         got = kernel_group_back(
             grad_pre,
             raws[k],
@@ -1563,12 +1713,10 @@
     total_a = blocks * rowse + grad_kernels.shape[1]
     total_a += -total_a % 16
     if aligned:
-        packed_a = kernel_weight_grad(joined, final_grad, dp, fsdp, rowse, 0, total_a)
-        packed_a = lax.dynamic_update_slice(
-            packed_a,
-            grad_kernels.reshape(dp, fsdp, -1, middle).swapaxes(0, 1),
-            (0, 0, blocks * rowse, 0),
-        )
+        packed_a = kernel_weight_grad(joined, final_grad, dp, fsdp, rowse, 0, blocks * rowse)
+        rest = grad_kernels.reshape(dp, fsdp, -1, middle).swapaxes(0, 1)
+        rest = jnp.pad(rest, ((0, 0), (0, 0), (0, -rest.shape[2] % 16), (0, 0)))
+        packed_a = jnp.concatenate([packed_a, rest], axis=2)
     else:
         packed_a = jnp.concatenate(
             [
@@ -1580,10 +1728,6 @@
         packed_a = jnp.pad(
             packed_a, ((0, 0), (0, 0), (0, total_a - packed_a.shape[2]), (0, 0))
         )
-    grad_attend, packed_a = lax.optimization_barrier((grad_attend, packed_a))
-    mine_a = lax.psum_scatter(
-        packed_a.reshape(-1, middle), "fsdp", scatter_dimension=0, tiled=True
-    )
     grad_x = grad_attend * 2.0 * sigma * (1.0 - sigma)
     unit_x = (lifted - mean_x) * inv_x
     pool_unit = (pool_raw - mean_m * pool_one) * inv_m
@@ -1593,6 +1737,10 @@
         jnp.sum(grad_x * unit_x, axis=(0, 1)),
         jnp.sum(grad_e * pool_one, axis=(0, 1)),
         jnp.sum(grad_e * pool_unit, axis=(0, 1)),
+    )
+    shifts[6], packed_a = lax.optimization_barrier((shifts[6], packed_a))
+    mine_a = lax.psum_scatter(
+        packed_a.reshape(-1, middle), "fsdp", scatter_dimension=0, tiled=True
     )
     lift_b = jnp.dot(
         full_motion_out, alpha_m[:, None] * gram_ab + beta_m[:, None] * gram_bb, precision=HIGHEST
@@ -1636,8 +1784,8 @@
         half,
     )
     grad_motion_in = weight_grad(act_d, motion_grad)
-    sums_narrow = jnp.sum(sums_narrow, axis=1)
-    shifts[4], spreads[4] = sums(sums_narrow[0], sums_narrow[1] * inv_d)
+    shifts[4], spreads[4] = sums.ready(sums_narrow, 2)
+    spreads[4] = spreads[4] * inv_d
     small_grads = jnp.concatenate(
         [grad_motion_in.reshape(devices, -1), grad_motion_out.reshape(devices, -1)], axis=1
     )
@@ -1656,13 +1804,29 @@
     sums_one, mine_a = lax.optimization_barrier((sums_one, mine_a))
     mine_a = lax.psum_scatter(mine_a, "dp", scatter_dimension=0, tiled=True)
     sums_one = jnp.sum(sums_one, axis=1)
-    shifts[2], spreads[2], spreads[3] = sums(sums_one[0], sums_one[1], sums_one[2])
+    shifts[2], spreads[2], spreads[3], motion_total, temporal_total = sums(
+        sums_one[0],
+        sums_one[1] * inv_c,
+        sums_one[2] * inv_p,
+        motion_tap_grad,
+        jnp.stack(temporal_grads),
+    )
     shifts[3] = shifts[2]
+    stats_two = jnp.stack(back_stats(2, mean_c, inv_c) + back_stats(3, mean_p, inv_p))
+    total = blocks * (rowsp + rows1)
+    if aligned:
+        packed_r = kernel_weight_grad(block_one, narrow_grad, dp, fsdp, rows2, 0, rows2)
+    else:
+        packed_r = by_owner(weight_grad(block_one, narrow_grad), 1)
+    stats_two, packed_r = lax.optimization_barrier((stats_two, packed_r))
+    mine_r = lax.psum_scatter(
+        packed_r.reshape(-1, middle), "fsdp", scatter_dimension=0, tiled=True
+    )
     widen_grad, shortcut_grad, grad_strided, sums_strided = kernel_expand_back(
         grad_one,
         raw_c,
         raw_p,
-        jnp.stack(back_stats(2, mean_c, inv_c) + back_stats(3, mean_p, inv_p)),
+        stats_two,
         expand1,
         raw_b,
         jnp.stack([alpha_b, beta_b, mean_b, inv_b]),
@@ -1670,12 +1834,8 @@
         half,
     )
     if aligned:
-        total = blocks * (rowsp + rows1) + rows2
         packed_b = kernel_weight_grad(
-            block_one, narrow_grad, dp, fsdp, rows2, total // rows2 - 1, total
-        )
-        packed_b = kernel_weight_grad(
-            act_b, widen_grad, dp, fsdp, rows1, blocks * rowsp // rows1, total, packed_b
+            act_b, widen_grad, dp, fsdp, rows1, blocks * rowsp // rows1, total
         )
         packed_b = kernel_weight_grad(
             sampled, shortcut_grad, dp, fsdp, rowsp, 0, total, packed_b
@@ -1685,11 +1845,13 @@
             [
                 by_owner(weight_grad(sampled, shortcut_grad), blocks),
                 by_owner(weight_grad(act_b, widen_grad), blocks),
-                by_owner(weight_grad(block_one, narrow_grad), 1),
             ],
             axis=2,
         )
-    sums_strided, packed_b, mine_a = lax.optimization_barrier((sums_strided, packed_b, mine_a))
+    shifts[1], spreads[1] = sums.ready(sums_strided, 2)
+    shifts[1], spreads[1], packed_b, mine_a, mine_r = lax.optimization_barrier(
+        (shifts[1], spreads[1], packed_b, mine_a, mine_r)
+    )
 
     def columns_back(value, rows):
         return value.reshape(blocks, rows, middle).swapaxes(0, 1).reshape(rows, wide)
@@ -1699,69 +1861,65 @@
     own_kernels = mine_a[blocks * rowse :].reshape(-1)[:size_s]
     mine_b = packed_b.reshape(-1, middle)
     mine_b = lax.psum_scatter(mine_b, "fsdp", scatter_dimension=0, tiled=True)
+    strided_grad = grad_raw(
+        1, grad_strided, raw_b, mean_b, inv_b, mask_rows[:, :1], count
+    ).astype(BF)
+    strided_grad = strided_grad.reshape(half, half, batch, middle)
+    sum_c1 = scatter_cores(dp, fsdp, kernel_conv_down_weights(act_a, strided_grad, dp, fsdp))
+    strided_grad, sum_c1 = lax.optimization_barrier((strided_grad, sum_c1))
+    sum_c = scatter_halves(dp, sum_c1.reshape((2, -1) + sum_c1.shape[1:]), 0)
+    grad_first, sums_first = kernel_conv_down_back(
+        strided_grad,
+        taps1,
+        raw_a,
+        jnp.stack([alpha_a, beta_a, mean_a, inv_a]),
+        mask_rows,
+    )
+    shifts[0], spreads[0] = sums.ready(sums_first, 2)
+    stats_first = jnp.stack(
+        [
+            alpha_a,
+            mean_a,
+            alpha_a * shifts[0] / count_big,
+            alpha_a * inv_a * spreads[0] / count_big,
+        ]
+    )
+    stats_first, sum_c, mine_b = lax.optimization_barrier((stats_first, sum_c, mine_b))
+    mine_b = jnp.concatenate([mine_b.reshape(dp, -1, middle), mine_r.reshape(dp, -1, middle)], axis=1)
+    mine_b = mine_b.reshape(-1, middle)
     mine_b = lax.psum_scatter(mine_b, "dp", scatter_dimension=0, tiled=True).astype(F32)
     cut1 = blocks * rowsp
     cut2 = cut1 + blocks * rows1
     own_project1 = columns_back(mine_b[:cut1], rowsp)
     own_expand1 = columns_back(mine_b[cut1:cut2], rows1)
     own_reduce2 = mine_b[cut2:]
-    grad_sampled = kernel_sampled_back(shortcut_grad, project1, half)
-    shifts[1], spreads[1] = sums(jnp.sum(sums_strided[0], axis=0), jnp.sum(sums_strided[1], axis=0))
-    strided_grad = grad_raw(
-        1, grad_strided, raw_b, mean_b, inv_b, mask_rows[:, :1], count
-    ).astype(BF)
-    strided_grad = strided_grad.reshape(half, half, batch, middle)
-    grad_spatial1 = kernel_conv_down_weights(act_a, strided_grad)
-    strided_grad, grad_spatial1 = lax.optimization_barrier((strided_grad, grad_spatial1))
-    own_spatial1 = quick_scatter(
-        dp,
-        fsdp,
-        jnp.concatenate(
-            [
-                grad_spatial1.reshape(9, devices, own, middle)
-                .swapaxes(0, 1)
-                .reshape(devices, 9 * own, middle),
-                rows_of(small_grads.astype(BF)),
-            ],
-            axis=1,
-        ),
-    )
-    own_motion = own_spatial1[9 * own :].reshape(-1)[: 2 * size_m].reshape(2, own, narrow)
-    own_spatial1 = own_spatial1[: 9 * own]
-    grad_first, sums_first = kernel_conv_down_back(
-        strided_grad,
-        taps1,
-        raw_a,
-        jnp.stack([alpha_a, beta_a, mean_a, inv_a]),
-        mask_rows,
-    )
-    shifts[0], spreads[0], motion_total, temporal_total = sums(
-        jnp.sum(sums_first[0], axis=0),
-        jnp.sum(sums_first[1], axis=0),
-        motion_tap_grad,
-        jnp.stack(temporal_grads),
-    )
+    for bit in range(1, dp.bit_length() - 1):
+        sum_c = scatter_halves(dp, sum_c.reshape((2, -1) + sum_c.shape[1:]), bit)
+    sum_c = sum_c.reshape(fsdp // 2, -1, middle)
     first_grad, grad_reduce1 = kernel_first_grad(
-        grad_first,
-        raw_a,
-        feats,
-        jnp.stack([alpha_a, mean_a, inv_a, shifts[0] / count_big, spreads[0] / count_big]),
-        mask_rows,
-        slots,
-        frames,
-    )
-    own_reduce1 = quick_scatter(dp, fsdp, grad_reduce1.reshape(devices, -1, middle))
-    grad_features = kernel_grad_features(
-        first_grad,
-        full_reduce1,
-        grad_sampled.reshape(half, half, slots * frames, c_in),
-        height,
-        slots,
-        frames,
-    )
+        grad_first, raw_a, feats, stats_first, mask_rows, frames
+    )
+    grad_reduce1, sum_c = lax.optimization_barrier((grad_reduce1, sum_c))
+    sum_d = jnp.concatenate(
+        [grad_reduce1.reshape(devices, -1, middle), rows_of(small_grads.astype(BF))], axis=1
+    )
+    rows_d = sum_d.shape[1]
+    sum_d = sum_d.reshape((dp, fsdp // 2, 2) + sum_d.shape[1:]).transpose(2, 1, 0, 3, 4)
+    sum_d = scatter_cores(dp, fsdp, sum_d).reshape(fsdp // 2, -1, middle)
+    both = scatter_fsdp(fsdp, jnp.concatenate([sum_d, sum_c], axis=1))
+    own_spatial1 = both[dp * rows_d :]
+    sum_d = scatter_dp(both[: dp * rows_d].astype(BF).reshape(dp, rows_d, middle))
+    rows_first = c_in // devices
+    own_reduce1 = sum_d[:rows_first]
+    own_motion = sum_d[rows_first:].reshape(-1)[: 2 * size_m].reshape(2, own, narrow)
+    grad_features = None
+    for pair in range(slots // 2):
+        grad_features = kernel_grad_features(
+            first_grad, full_reduce1, shortcut_grad, project1, height, frames, pair, grad_features
+        )
     grad_features = grad_features.reshape(slots, height, height, frames, c_in)
     return (
-        result.transpose(2, 3, 0, 1, 4),
+        result.transpose(0, 3, 1, 2, 4),
         grad_features.transpose(0, 3, 1, 2, 4),
         own_reduce1,
         own_spatial1.reshape(9, own * middle),

time: 809 us -> 708 us (0.88)
  local copies, waits for them, and re-layouts: 88 us -> 54.5 us
  blocking collectives: 71.5 us -> 40.8 us
  Pallas kernels: 340 us -> 320 us
  waiting for transfers between devices: 145 us -> 129 us
  starting transfers between devices: 67 us -> 75.7 us
    pallas_call x26 -> x25, Pallas kernels: 304 us -> 259 us  [call(): pl.pallas_call(body, grid=grid, in_specs=[spec(b) for b in in_blocks], ou...]
    all_to_all x11 -> x3, waiting for transfers between devices: 45.5 us -> 9.85 us  [flat(): return jnp.sum(lax.all_to_all(copies, AXES, 0, 0), axis=0)]
    all_to_all x4 -> x13, starting transfers between devices: 15.7 us -> 48.8 us  [the longest x10 35.6 us: ready(): total = jnp.sum(lax.all_to_all(copies, AXES, 0, 0, tiled=True), axis=(0, 1))]
    all_to_all x11 -> x3, starting transfers between devices: 36.9 us -> 11.4 us  [flat(): return jnp.sum(lax.all_to_all(copies, AXES, 0, 0), axis=0)]
    pallas_call x0 -> x2, Pallas kernels: none -> 24.2 us  [kernel_grad_features(): pl.pallas_call(body, grid=(parts,), in_specs=in_specs, out_specs=pl.Block...]
    all_to_all x3 -> x1, blocking collectives: 31.3 us -> 9.81 us  [ready(): total = jnp.sum(lax.all_to_all(copies, AXES, 0, 0, tiled=True), axis=(0, 1))]
    all_to_all x4 -> x13, waiting for transfers between devices: 28.6 us -> 46.5 us  [the longest x10 38.5 us: ready(): total = jnp.sum(lax.all_to_all(copies, AXES, 0, 0, tiled=True), axis=(0, 1))]
    all_gather x2, waiting for transfers between devices: 42.7 us -> 28.3 us  [gather(): return lax.all_gather(value, AXES, axis=0, tiled=False)]
  transfers between devices with their start and end apart: 37 -> 39, of which waited for: 25 -> 25; matrix products, arithmetic and copies ran while one was open for 13% -> 11% of each run, Pallas kernels for 32% -> 35%
where the time goes in v2:
time: 708 us; the launch traced here: 696 us
  Pallas kernels  320 us (45%)
  waiting for transfers between devices  129 us (18%)
  starting transfers between devices  75.7 us (11%)
  local copies, waits for them, and re-layouts  54.5 us (8%)
  other arithmetic  52.2 us (7%)
  blocking collectives  40.8 us (6%)
  between operations  18.2 us (3%)
    pallas_call x25, Pallas kernels, call(): pl.pallas_call(body, grid=grid, in_specs=[spec(b) for b in in_blocks], ou...  259 us
    all_to_all x10, waiting for transfers between devices, ready(): total = jnp.sum(lax.all_to_all(copies, AXES, 0, 0, tiled=True), axis=(0, 1))  38.5 us
    pallas_call x4, Pallas kernels, kernel_weight_grad(): pl.pallas_call(body, grid=(columns // middle,), in_specs=in_specs, out_sp...  36.6 us
    all_to_all x10, starting transfers between devices, ready(): total = jnp.sum(lax.all_to_all(copies, AXES, 0, 0, tiled=True), axis=(0, 1))  35.6 us
    all_to_all x2, blocking collectives, flat(): lax.all_to_all(copies, AXES, 0, 0, axis_index_groups=self.groups)  31 us
    all_gather x2, waiting for transfers between devices, gather(): return lax.all_gather(value, AXES, axis=0, tiled=False)  28.3 us
    pallas_call x2, Pallas kernels, kernel_grad_features(): pl.pallas_call(body, grid=(parts,), in_specs=in_specs, out_specs=pl.Block...  24.2 us
  transfers between devices with their start and end apart: 39, of which 25 were waited for; matrix products, arithmetic and copies ran while one was open for 11% of the time, Pallas kernels for 35%

profile of v2, /device:TPU:0, one launch (start us, length us, event | category | flops | bytes accessed | tf_op | source)
XLA Modules:
  0.0 695.8 jit_solution(14724642987461791972)
XLA Ops:
  12.6 6.3 all-to-all-start
  19.4 5.6 all-to-all-done
  25.8 3.7 all-to-all-start.1
  31.1 5.1 all-to-all-done.1
  40.0 16.6 %shard_map.298 = (bf16[14,14,32,512]{3,2,1,0:T(8,128)(2,1)}, f32[8,512]{1,0:T(8,128)}, f32[2,8,512]{2,1,0:T(8,128)}) custom-call(bf16[4,1568,1024]{2,1,0:T(8,128)(2,1)} %bitcast.302, bf16[1024,512]{1,0:T(8,128)(2,1)} %bitcast.311, f32[32,256]{1,0:T(8,128)} %broadcast_in_dim.37.m_ref.refs_4_.refs_5_.refs_7_), custom_call_target="tpu_custom_call" | custom-call | flops 6576668672 | bytes 19267584 | tf_op jit(solution)/shard_map/pallas_call | solution.py:75
  59.5 3.8 all-to-all-start.2
  68.3 3.5 all-to-all-done.2
  75.8 9.1 %shard_map.299.a_ref = bf16[14,14,32,512]{3,2,1,0:T(8,128)(2,1)} custom-call(bf16[14,14,32,512]{3,2,1,0:T(8,128)(2,1)} %get-tuple-element.103.a_ref, f32[2,512]{1,0:T(2,128)} %pad_maximum_fusion.17.s_ref, f32[32,256]{1,0:T(8,128)} %broadcast_in_dim.37.m_ref.refs_4_.refs_5_.refs_7_), custom_call_target="tpu_custom_call" | custom-call | flops 32112640 | bytes 19267584 | tf_op jit(solution)/shard_map/pallas_call | solution.py:75
  84.8 28.3 %all-gather.6.cloned.1.call-done = bf16[12800,512]{1,0:T(8,128)(2,1)} async-done(((bf16[400,512]{1,0:T(8,128)(2,1)}), bf16[12800,512]{1,0:T(8,128)(2,1)}) %all-gather.6.cloned.1.call-update) | async-done | bytes 13107216 | tf_op jit(solution)/shard_map/all_gather | solution.py:1454
  113.1 13.5 %shard_map.300 = (f32[7,7,32,512]{3,2,1,0:T(8,128)}, f32[32,1,1024]{2,1,0:T(1,128)}) custom-call(bf16[14,14,32,512]{3,2,1,0:T(8,128)(2,1)} %shard_map.299.a_ref, f32[32,256]{1,0:T(8,128)} %broadcast_in_dim.37.m_ref.refs_4_.refs_5_.refs_7_, bf16[32,400,512]{2,1,0:T(8,128)(2,1)} %bitcast.271, bf16[32,400,512]{2,1,0:T(8,128)(2,1)} %bitcast.272, ...), custom_call_target="tpu_custom_call" | custom-call | flops 7398752256 | bytes 11141120 | tf_op jit(solution)/shard_map/pallas_call | solution.py:75
  129.4 13.0 %shard_map.302 = (bf16[49,32,2048]{2,1,0:T(8,128)(2,1)}, f32[8,2048]{1,0:T(8,128)}, f32[2,8,2048]{2,1,0:T(8,128)}) custom-call(bf16[49,32,1024]{2,1,0:T(8,128)(2,1)} %bitcast.323, f32[32,256]{1,0:T(8,128)} %broadcast_in_dim.37.m_ref.refs_4_.refs_5_.refs_7_, bf16[32,400,512]{2,1,0:T(8,128)(2,1)} %bitcast.280), custom_call_target="tpu_custom_call" | custom-call | flops 6576668672 | bytes 16056320 | tf_op jit(solution)/shard_map/pallas_call | solution.py:75
  144.0 10.6 %shard_map.301 = (bf16[49,32,512]{2,1,0:T(8,128)(2,1)}, bf16[49,32,2048]{2,1,0:T(8,128)(2,1)}, f32[8,2048]{1,0:T(8,128)}, f32[2,8,2048]{2,1,0:T(8,128)}) custom-call(f32[49,32,512]{2,1,0:T(8,128)} %bitcast.298, f32[2,512]{1,0:T(2,128)} %pad_maximum_fusion.18.s_ref, f32[32,256]{1,0:T(8,128)} %broadcast_in_dim.37.m_ref.refs_4_.refs_5_.refs_7_, ...), custom_call_target="tpu_custom_call" | custom-call | flops 3288334336 | bytes 17661952 | tf_op jit(solution)/shard_map/pallas_call | solution.py:75
  157.2 20.2 %all_to_all.117 = f32[16,1,4096]{2,1,0:T(1,128)S(1)} all-to-all(f32[16,1,4096]{2,1,0:T(1,128)S(1)} %broadcast_in_dim.40), channel_id=1, replica_groups={{0,2,4,6,8,10,12,14,16,18,20,22,24,26,28,30},{1,3,5,7,9,11,13,15,17,19,..., dimensions={0} | all-to-all | bytes 524288 | tf_op jit(solution)/shard_map/all_to_all | solution.py:1313
  180.8 13.3 %shard_map.303 = (bf16[49,32,2048]{2,1,0:T(8,128)(2,1)}, f32[49,32,512]{2,1,0:T(8,128)}, f32[32,1,1024]{2,1,0:T(1,128)}) custom-call(bf16[49,32,2048]{2,1,0:T(8,128)(2,1)} %get-tuple-element.108.c_ref, bf16[49,32,2048]{2,1,0:T(8,128)(2,1)} %get-tuple-element.109.p_ref, f32[8,2048]{1,0:T(8,128)} %stack.288.s_ref, ...), custom_call_target="tpu_custom_call" | custom-call | flops 3288334336 | bytes 32112640 | tf_op jit(solution)/shard_map/pallas_call | solution.py:75
  194.0 3.4 all-to-all-start.5
  200.1 5.5 all-to-all-done.5
  206.3 4.7 shard_map.304
  220.4 6.3 all-to-all-done.6
  230.2 4.3 shard_map.305
  238.2 6.2 all-to-all-done.7
  245.1 3.7 shard_map.306
  252.4 6.2 all-to-all-done.8
  259.4 3.7 shard_map.307
  263.1 9.8 %all_to_all.118 = f32[32,1,256]{2,1,0:T(1,128)S(1)} all-to-all(f32[32,1,256]{2,1,0:T(1,128)} %get-tuple-element.127), channel_id=1, replica_groups=mesh['dp'=4,'fsdp'=8] {'dp','fsdp'}, dimensions={0} | all-to-all | bytes 65536 | tf_op jit(solution)/shard_map/all_to_all | solution.py:1320
  273.7 10.3 %shard_map.308 = (bf16[49,32,512]{2,1,0:T(8,128)(2,1)}, bf16[49,32,2048]{2,1,0:T(8,128)(2,1)}, f32[8,2048]{1,0:T(8,128)}, f32[2,8,2048]{2,1,0:T(8,128)}) custom-call(bf16[49,32,512]{2,1,0:T(8,128)(2,1)} %get-tuple-element.119.refs_0_.x_ref.refs_5_, bf16[49,32,128]{2,1,0:T(8,128)(2,1)} %get-tuple-element.122.o1.refs_8_, ...), custom_call_target="tpu_custom_call" | custom-call | flops 3288334336 | bytes 16056320 | tf_op jit(solution)/shard_map/pallas_call | solution.py:75
  286.3 10.8 %all_to_all.119 = f32[16,1,2048]{2,1,0:T(1,128)S(1)} all-to-all(f32[16,1,2048]{2,1,0:T(1,128)S(1)} %broadcast_in_dim.44), channel_id=1, replica_groups={{0,2,4,6,8,10,12,14,16,18,20,22,24,26,28,30},{1,3,5,7,9,11,13,15,17,19,..., dimensions={0} | all-to-all | bytes 262144 | tf_op jit(solution)/shard_map/all_to_all | solution.py:1313
  299.2 16.4 %shard_map.309 = (bf16[4,7,7,8,2048]{4,3,2,1,0:T(8,128)(2,1)}, bf16[49,32,2048]{2,1,0:T(8,128)(2,1)}, f32[2,8,2048]{2,1,0:T(8,128)}) custom-call(bf16[49,32,2048]{2,1,0:T(8,128)(2,1)} %get-tuple-element.128.e_ref, bf16[49,32,2048]{2,1,0:T(8,128)(2,1)} %get-tuple-element.129.o_ref.refs_0_, bf16[4,7,7,8,2048]{4,3,2,1,0:T(8,128)(2,1)} %bitcast.315, ...), custom_call_target="tpu_custom_call" | custom-call | flops 64225280 | bytes 44957696 | tf_op jit(solution)/shard_map/pallas_call | solution.py:75
  318.6 3.5 all-to-all-start.11
  325.7 4.6 all-to-all-done.11
  332.3 14.4 %shard_map.310 = (bf16[49,32,2048]{2,1,0:T(8,128)(2,1)}, f32[49,32,512]{2,1,0:T(8,128)}, f32[49,32,128]{2,1,0:T(8,128)}, f32[32,1,256]{2,1,0:T(1,128)}) custom-call(bf16[49,32,2048]{2,1,0:T(8,128)(2,1)} %get-tuple-element.133.g_ref.t_ref, bf16[49,32,2048]{2,1,0:T(8,128)(2,1)} %get-tuple-element.128.e_ref, f32[4,2048]{1,0:T(4,128)} %pad_maximum_fusion.6.s_ref, ...), custom_call_target="tpu_custom_call" | custom-call | flops 3288334336 | bytes 32112640 | tf_op jit(solution)/shard_map/pallas_call | solution.py:75
  349.9 6.7 all-to-all-done.12
  357.7 5.4 shard_map.311
  365.7 7.9 %shard_map.314 = bf16[8,4,64,512]{3,2,1,0:T(8,128)(2,1)} custom-call(bf16[49,32,512]{2,1,0:T(8,128)(2,1)} %get-tuple-element.147.refs_0_, bf16[49,32,2048]{2,1,0:T(8,128)(2,1)} %get-tuple-element.148.refs_1_), custom_call_target="tpu_custom_call" | custom-call | flops 3288334336 | bytes 10125312 | tf_op jit(solution)/shard_map/pallas_call | solution.py:991
  374.9 5.5 shard_map.312
  380.4 6.2 all-to-all-start.14
  386.6 3.2 shard_map.317
  395.1 5.5 shard_map.313
  402.6 5.1 all-to-all-start.15
  407.8 3.2 shard_map.315
  413.1 3.6 fusion.2
  422.7 9.5 %shard_map.318 = (f32[49,32,512]{2,1,0:T(8,128)}, bf16[49,32,32]{2,1,0:T(8,128)(2,1)}, f32[32,1,1024]{2,1,0:T(1,128)}) custom-call(f32[49,32,512]{2,1,0:T(8,128)} %get-tuple-element.135.refs_6_.j_ref, f32[49,32,128]{2,1,0:T(8,128)} %get-tuple-element.144.p1, f32[49,32,128]{2,1,0:T(8,128)} %get-tuple-element.142.refs_8_.p2, ...), custom_call_target="tpu_custom_call" | custom-call | flops 51380224 | bytes 9633792 | tf_op jit(solution)/shard_map/pallas_call | solution.py:75
  432.1 6.0 all-to-all-start.16
  438.4 8.0 %all-to-all-done.16 = f32[32,1,1024]{2,1,0:T(1,128)S(1)} async-done(((f32[32,1,1024]{2,1,0:T(1,128)}), f32[32,1,1024]{2,1,0:T(1,128)S(1)}, u32[]{:S(2)}, u32[]{:S(2)}) %all-to-all-start.16) | async-done | bytes 131104 | tf_op jit(solution)/shard_map/all_to_all | solution.py:1320
  447.7 19.1 %shard_map.319 = (bf16[49,32,512]{2,1,0:T(8,128)(2,1)}, bf16[49,32,2048]{2,1,0:T(8,128)(2,1)}, f32[3,8,2048]{2,1,0:T(8,128)}) custom-call(f32[49,32,512]{2,1,0:T(8,128)} %get-tuple-element.156.n_ref, f32[49,32,512]{2,1,0:T(8,128)} %get-tuple-element.114.d_ref, f32[4,512]{1,0:T(4,128)} %pad_maximum_fusion.14.sd_ref, bf16[32,400,512]{2,1,0:T(8,128)(2,1)} %bitcast.283, ...), custom_call_target="tpu_custom_call" | custom-call | flops 3288334336 | bytes 51380224 | tf_op jit(solution)/shard_map/pallas_call | solution.py:75
  470.2 3.7 all-to-all-start.17
  474.6 9.3 %all-to-all-done.17 = f32[16,1,3840]{2,1,0:T(1,128)S(1)} async-done(((f32[16,1,3840]{2,1,0:T(1,128)}), f32[16,1,3840]{2,1,0:T(1,128)S(1)}, u32[]{:S(2)}, u32[]{:S(2)}) %all-to-all-start.17) | async-done | bytes 245792 | tf_op jit(solution)/shard_map/all_to_all | solution.py:1313
  484.1 8.6 %shard_map.320 = bf16[8,4,64,512]{3,2,1,0:T(8,128)(2,1)} custom-call(bf16[49,32,2048]{2,1,0:T(8,128)(2,1)} %get-tuple-element.129.o_ref.refs_0_, bf16[49,32,512]{2,1,0:T(8,128)(2,1)} %get-tuple-element.165.refs_1_), custom_call_target="tpu_custom_call" | custom-call | flops 3288334336 | bytes 10125312 | tf_op jit(solution)/shard_map/pallas_call | solution.py:991
  494.2 20.0 %shard_map.321 = (bf16[49,32,2048]{2,1,0:T(8,128)(2,1)}, bf16[49,32,2048]{2,1,0:T(8,128)(2,1)}, f32[49,32,512]{2,1,0:T(8,128)}, f32[32,1,1024]{2,1,0:T(1,128)}) custom-call(bf16[49,32,2048]{2,1,0:T(8,128)(2,1)} %get-tuple-element.158.g_ref, bf16[49,32,2048]{2,1,0:T(8,128)(2,1)} %get-tuple-element.108.c_ref, bf16[49,32,2048]{2,1,0:T(8,128)(2,1)} %get-tuple-element.109.p_ref, ...), custom_call_target="tpu_custom_call" | custom-call | flops 3288334336 | bytes 51380224 | tf_op jit(solution)/shard_map/pallas_call | solution.py:75
  517.1 8.1 %shard_map.322.refs_2_ = bf16[8,4,192,512]{3,2,1,0:T(8,128)(2,1)} custom-call(bf16[49,32,512]{2,1,0:T(8,128)(2,1)} %get-tuple-element.170.refs_0_, bf16[49,32,2048]{2,1,0:T(8,128)(2,1)} %get-tuple-element.171.refs_1_), custom_call_target="tpu_custom_call" | custom-call | flops 3288334336 | bytes 10125312 | tf_op jit(solution)/shard_map/pallas_call | solution.py:991
  525.2 11.9 %shard_map.323 = bf16[8,4,192,512]{3,2,1,0:T(8,128)(2,1)} custom-call(bf16[49,32,1024]{2,1,0:T(8,128)(2,1)} %bitcast.324, bf16[49,32,2048]{2,1,0:T(8,128)(2,1)} %get-tuple-element.169.refs_1_.s_ref, bf16[8,4,192,512]{3,2,1,0:T(8,128)(2,1)} %shard_map.322.refs_2_), custom_call_target="tpu_custom_call", output_to_operand_aliasing={{}: (2, {})} | custom-call | flops 6576668672 | bytes 13828096 | tf_op jit(solution)/shard_map/pallas_call | solution.py:991
  537.2 4.2 reduce-scatter.10.cloned.1.call-done
  543.4 4.0 multiply_convert_fusion
  547.4 15.9 %shard_map.324 = bf16[2,4,4,144,512]{4,3,2,1,0:T(8,128)(2,1)} custom-call(bf16[7,2,7,2,32,512]{5,4,3,2,1,0:T(8,128)(2,1)} %bitcast.300, bf16[1568,512]{1,0:T(8,128)(2,1)} %bitcast.305), custom_call_target="tpu_custom_call" | custom-call | flops 7398752256 | bytes 12746752 | tf_op jit(solution)/shard_map/pallas_call | solution.py:75
  563.3 3.3 dynamic-slice_bitcast_fusion
  567.3 4.1 collective-permute-done.9
  575.3 19.4 %shard_map.325 = (bf16[7,2,7,2,32,512]{5,4,3,2,1,0:T(8,128)(2,1)}, f32[32,1,1024]{2,1,0:T(1,128)}) custom-call(bf16[7,7,32,512]{3,2,1,0:T(8,128)(2,1)} %bitcast.306, bf16[7,7,32,512]{3,2,1,0:T(8,128)(2,1)} %bitcast.307, bf16[7,2,7,2,32,512]{5,4,3,2,1,0:T(8,128)(2,1)} %bitcast.296, f32[4,512]{1,0:T(4,128)} %fusion.46.s_ref, ...), custom_call_target="tpu_custom_call" | custom-call | flops 7398752256 | bytes 30408704 | tf_op jit(solution)/shard_map/pallas_call | solution.py:75
  594.7 4.3 all-to-all-start.19
  602.1 5.1 all-to-all-done.19
  611.6 15.8 %shard_map.326 = (bf16[4,1568,512]{2,1,0:T(8,128)(2,1)}, bf16[1024,512]{1,0:T(8,128)(2,1)}) custom-call(bf16[14,14,32,512]{3,2,1,0:T(8,128)(2,1)} %bitcast.316, bf16[14,14,32,512]{3,2,1,0:T(8,128)(2,1)} %get-tuple-element.103.a_ref, bf16[4,1568,1024]{2,1,0:T(8,128)(2,1)} %bitcast.304, f32[4,512]{1,0:T(4,128)} %fusion.48.s_ref, ...), custom_call_target="tpu_custom_call" | custom-call | flops 6576668672 | bytes 32112640 | tf_op jit(solution)/shard_map/pallas_call | solution.py:75
  627.5 11.4 %collective-permute-done.11 = bf16[1,4,144,512]{3,2,1,0:T(8,128)(2,1)S(1)} collective-permute-done((bf16[1,4,144,512]{3,2,1,0:T(8,128)(2,1)S(1)}, bf16[1,4,144,512]{3,2,1,0:T(8,128)(2,1)S(1)}, u32[]{:S(2)}, u32[]{:S(2)}) %collective-permute-start.11) | collective-permute-done | bytes 589856 | tf_op jit(solution)/shard_map/ppermute | solution.py:1373
  647.3 3.5 all-to-all-start.20
  650.8 12.1 %shard_map.327.refs_0_ = bf16[4,1568,1024]{2,1,0:T(8,128)(2,1)} custom-call(bf16[4,1568,512]{2,1,0:T(8,128)(2,1)} %get-tuple-element.182.g_ref, bf16[1024,512]{1,0:T(8,128)(2,1)} %bitcast.312, bf16[49,32,2048]{2,1,0:T(8,128)(2,1)} %get-tuple-element.169.refs_1_.s_ref, bf16[32,400,512]{2,1,0:T(8,128)(2,1)} %bitcast.294), custom_call_target="tpu_custom_call" | custom-call | flops 6576668672 | bytes 12845056 | tf_op jit(solution)/shard_map/pallas_call | solution.py:494
  662.9 12.1 %shard_map.328 = bf16[4,1568,1024]{2,1,0:T(8,128)(2,1)} custom-call(bf16[4,1568,512]{2,1,0:T(8,128)(2,1)} %get-tuple-element.182.g_ref, bf16[1024,512]{1,0:T(8,128)(2,1)} %bitcast.313, bf16[49,32,2048]{2,1,0:T(8,128)(2,1)} %get-tuple-element.169.refs_1_.s_ref, bf16[32,400,512]{2,1,0:T(8,128)(2,1)} %bitcast.295, ...), custom_call_target="tpu_custom_call", output_to_operand_aliasing={{}: (4, {})} | custom-call | flops 6576668672 | bytes 12845056 | tf_op jit(solution)/shard_map/pallas_call | solution.py:494
  676.0 3.3 all-to-all-start.21
  (426 shorter events, 136.2 us)
Async XLA Ops:
  7.2 11.8 %copy-start.45 = (bf16[16,32]{1,0:T(8,128)(2,1)S(1)}, bf16[16,32]{1,0:T(8,128)(2,1)}, u32[]{:S(2)}) copy-start(bf16[16,32]{1,0:T(8,128)(2,1)} %param.28) | copy-start | bytes 3076
  7.2 11.9 %copy-start.18 = (bf16[27,512]{1,0:T(8,128)(2,1)S(1)}, bf16[27,512]{1,0:T(8,128)(2,1)}, u32[]{:S(2)}) copy-start(bf16[27,512]{1,0:T(8,128)(2,1)} %param.30) | copy-start | bytes 82948
  7.2 12.1 %copy-start.11 = (bf16[16,2048]{1,0:T(8,128)(2,1)S(1)}, bf16[16,2048]{1,0:T(8,128)(2,1)}, u32[]{:S(2)}) copy-start(bf16[16,2048]{1,0:T(8,128)(2,1)} %param.31) | copy-start | bytes 196612
  7.2 105.9 %all-gather.6.cloned.1.call-start = ((), (), s32[]{:S(2)}) async-start(), calls=%async_computation.32 | async-start | bytes 13516800 | tf_op jit(solution)/shard_map/all_gather | solution.py:1454
  9.2 21.8 %copy-start.56 = (s32[4,8]{1,0:T(4,128)S(1)}, s32[4,8]{1,0:T(4,128)}, u32[]{:S(2)}) copy-start(s32[4,8]{1,0:T(4,128)} %param.21) | copy-start | bytes 388
  9.2 21.8 %copy-start.59 = (s32[4]{0:T(128)S(1)}, s32[4]{0:T(128)}, u32[]{:S(2)}) copy-start(s32[4]{0:T(128)} %param.20) | copy-start | bytes 52
  12.6 12.4 %all-to-all-start = ((bf16[4,32,512]{2,1,0:T(8,128)(2,1)}), bf16[4,32,512]{2,1,0:T(8,128)(2,1)S(1)}, u32[]{:S(2)}, u32[]{:S(2)}) async-start(bf16[4,32,512]{2,1,0:T(8,128)(2,1)} %broadcast_in_dim.34), calls=%async_computation | async-start | bytes 262144 | tf_op jit(solution)/shard_map/all_to_all | solution.py:1346
  25.8 10.3 %all-to-all-start.1 = ((bf16[4,4,32,512]{3,2,1,0:T(8,128)(2,1)}), bf16[4,4,32,512]{3,2,1,0:T(8,128)(2,1)S(1)}, u32[]{:S(2)}, u32[]{:S(2)}) async-start(bf16[4,4,32,512]{3,2,1,0:T(8,128)(2,1)} %broadcast_in_dim.35), calls=%async_computation.1 | async-start | bytes 1048576 | tf_op jit(solution)/shard_map/all_to_all | solution.py:1347
  29.5 167.9 %all-gather.8.cloned.1.call-start = ((), (), s32[]{:S(2)}) async-start(), calls=%async_computation.33 | async-start | bytes 3244032 | tf_op jit(solution)/shard_map/all_gather | solution.py:1454
  31.0 370.5 %copy-start.57 = (f32[4,8]{1,0:T(4,128)}, f32[4,8]{1,0:T(4,128)S(1)}, u32[]{:S(2)}) copy-start(f32[4,8]{1,0:T(4,128)S(1)} %get-tuple-element.239) | copy-start | bytes 388
  36.2 1.9 collective-permute-start
  59.5 12.4 %all-to-all-start.2 = ((f32[32,1,1280]{2,1,0:T(1,128)}), f32[32,1,1280]{2,1,0:T(1,128)S(1)}, u32[]{:S(2)}, u32[]{:S(2)}) async-start(f32[32,1,1280]{2,1,0:T(1,128)} %broadcast_in_dim.39), calls=%async_computation.2 | async-start | bytes 327680 | tf_op jit(solution)/shard_map/all_to_all | solution.py:1306
  126.5 16.8 %all-to-all-start.3 = ((f32[32,1,1024]{2,1,0:T(1,128)}), f32[32,1,1024]{2,1,0:T(1,128)S(1)}, u32[]{:S(2)}, u32[]{:S(2)}) async-start(f32[32,1,1024]{2,1,0:T(1,128)} %get-tuple-element.107), calls=%async_computation.3 | async-start | bytes 262144 | tf_op jit(solution)/shard_map/all_to_all | solution.py:1320
  144.0 33.6 %copy-start.42 = (f32[3,3,128]{2,1,0:T(4,128)S(1)}, f32[3,3,128]{2,1,0:T(4,128)}, u32[]{:S(2)}) copy-start(f32[3,3,128]{2,1,0:T(4,128)} %param.35) | copy-start | bytes 13828
  155.7 1.2 collective-permute-start.1
  177.5 2.4 collective-permute-start.2
  194.0 11.6 %all-to-all-start.5 = ((f32[32,1,1024]{2,1,0:T(1,128)}), f32[32,1,1024]{2,1,0:T(1,128)S(1)}, u32[]{:S(2)}, u32[]{:S(2)}) async-start(f32[32,1,1024]{2,1,0:T(1,128)} %get-tuple-element.115), calls=%async_computation.5 | async-start | bytes 262144 | tf_op jit(solution)/shard_map/all_to_all | solution.py:1320
  197.4 204.2 %copy-start.41 = (f32[4,8]{1,0:T(4,128)}, f32[4,8]{1,0:T(4,128)S(1)}, u32[]{:S(2)}) copy-start(f32[4,8]{1,0:T(4,128)S(1)} %get-tuple-element.330) | copy-start | bytes 388
  197.4 223.7 %copy-start.55 = (f32[4,8]{1,0:T(4,128)}, f32[4,8]{1,0:T(4,128)S(1)}, u32[]{:S(2)}) copy-start(f32[4,8]{1,0:T(4,128)S(1)} %get-tuple-element.329) | copy-start | bytes 388
  199.2 13.4 %copy-start.19 = (f32[9,32]{1,0:T(8,128)S(1)}, f32[9,32]{1,0:T(8,128)}, u32[]{:S(2)}) copy-start(f32[9,32]{1,0:T(8,128)} %param.34) | copy-start | bytes 3460
  200.1 18.1 %copy-start.12 = (f32[7,7,9]{1,2,0:T(8,128)S(1)}, f32[7,7,9]{1,2,0:T(8,128)}, u32[]{:S(2)}) copy-start(f32[7,7,9]{1,2,0:T(8,128)} %constant.124.clone) | copy-start | bytes 5296
  214.4 187.2 %copy-start.28 = (f32[4,8,32]{2,1,0:T(8,128)}, f32[4,8,32]{2,1,0:T(8,128)S(1)}, u32[]{:S(2)}) copy-start(f32[4,8,32]{2,1,0:T(8,128)S(1)} %get-tuple-element.248) | copy-start | bytes 12292
  215.6 11.2 %all-to-all-start.6 = ((f32[32,1,1280]{2,1,0:T(1,128)}), f32[32,1,1280]{2,1,0:T(1,128)S(1)}, u32[]{:S(2)}, u32[]{:S(2)}) async-start(f32[32,1,1280]{2,1,0:T(1,128)} %broadcast_in_dim.43), calls=%async_computation.6 | async-start | bytes 327680 | tf_op jit(solution)/shard_map/all_to_all | solution.py:1306
  218.4 183.2 %copy-start.46 = (f32[32]{0:T(128)}, f32[32]{0:T(128)S(1)}, u32[]{:S(2)}) copy-start(f32[32]{0:T(128)S(1)} %get-tuple-element.196) | copy-start | bytes 388
  227.8 190.9 %copy-start.43 = (f32[32]{0:T(128)}, f32[32]{0:T(128)S(1)}, u32[]{:S(2)}) copy-start(f32[32]{0:T(128)S(1)} %get-tuple-element.245) | copy-start | bytes 388
  227.8 210.3 %copy-start.29 = (f32[32]{0:T(128)}, f32[32]{0:T(128)S(1)}, u32[]{:S(2)}) copy-start(f32[32]{0:T(128)S(1)} %get-tuple-element.246) | copy-start | bytes 388
  229.2 191.9 %copy-start.33 = (f32[512]{0:T(512)}, f32[512]{0:T(512)S(1)}, u32[]{:S(2)}) copy-start(f32[512]{0:T(512)S(1)} %get-tuple-element.243) | copy-start | bytes 6148
  229.2 191.9 %copy-start.34 = (f32[512]{0:T(512)}, f32[512]{0:T(512)S(1)}, u32[]{:S(2)}) copy-start(f32[512]{0:T(512)S(1)} %get-tuple-element.244) | copy-start | bytes 6148
  234.5 9.8 %all-to-all-start.7 = ((f32[32,1,256]{2,1,0:T(1,128)}), f32[32,1,256]{2,1,0:T(1,128)S(1)}, u32[]{:S(2)}, u32[]{:S(2)}) async-start(f32[32,1,256]{2,1,0:T(1,128)} %get-tuple-element.121), calls=%async_computation.7 | async-start | bytes 65536 | tf_op jit(solution)/shard_map/all_to_all | solution.py:1320
  248.8 9.8 %all-to-all-start.8 = ((f32[32,1,256]{2,1,0:T(1,128)}), f32[32,1,256]{2,1,0:T(1,128)S(1)}, u32[]{:S(2)}, u32[]{:S(2)}) async-start(f32[32,1,256]{2,1,0:T(1,128)} %get-tuple-element.124), calls=%async_computation.8 | async-start | bytes 65536 | tf_op jit(solution)/shard_map/all_to_all | solution.py:1320
  285.0 1.2 collective-permute-start.3
  297.2 1.2 collective-permute-start.4
  316.6 1.3 collective-permute-start.5
  318.6 11.7 %all-to-all-start.11 = ((f32[16,1,2048]{2,1,0:T(1,128)}), f32[16,1,2048]{2,1,0:T(1,128)S(1)}, u32[]{:S(2)}, u32[]{:S(2)}) async-start(f32[16,1,2048]{2,1,0:T(1,128)} %broadcast_in_dim.45), calls=%async_computation.11 | async-start | bytes 262144 | tf_op jit(solution)/shard_map/all_to_all | solution.py:1313
  330.4 1.2 collective-permute-start.6
  346.7 9.8 %all-to-all-start.12 = ((f32[32,1,256]{2,1,0:T(1,128)}), f32[32,1,256]{2,1,0:T(1,128)S(1)}, u32[]{:S(2)}, u32[]{:S(2)}) async-start(f32[32,1,256]{2,1,0:T(1,128)} %get-tuple-element.137), calls=%async_computation.12 | async-start | bytes 65536 | tf_op jit(solution)/shard_map/all_to_all | solution.py:1320
  363.1 10.5 %all-to-all-start.13 = ((f32[32,1,256]{2,1,0:T(1,128)}), f32[32,1,256]{2,1,0:T(1,128)S(1)}, u32[]{:S(2)}, u32[]{:S(2)}) async-start(f32[32,1,256]{2,1,0:T(1,128)} %get-tuple-element.139), calls=%async_computation.13 | async-start | bytes 65536 | tf_op jit(solution)/shard_map/all_to_all | solution.py:1320
  380.4 13.5 %all-to-all-start.14 = ((f32[32,1,256]{2,1,0:T(1,128)}), f32[32,1,256]{2,1,0:T(1,128)S(1)}, u32[]{:S(2)}, u32[]{:S(2)}) async-start(f32[32,1,256]{2,1,0:T(1,128)} %get-tuple-element.141), calls=%async_computation.14 | async-start | bytes 65536 | tf_op jit(solution)/shard_map/all_to_all | solution.py:1320
  402.6 14.0 %all-to-all-start.15 = ((f32[32,1,1280]{2,1,0:T(1,128)}), f32[32,1,1280]{2,1,0:T(1,128)S(1)}, u32[]{:S(2)}, u32[]{:S(2)}) async-start(f32[32,1,1280]{2,1,0:T(1,128)} %broadcast_in_dim.47), calls=%async_computation.15 | async-start | bytes 327680 | tf_op jit(solution)/shard_map/all_to_all | solution.py:1306
  407.7 59.1 %reduce-scatter.6.cloned.1.call-start = ((), (), s32[]{:S(2)}) async-start(), calls=%async_computation.27 | async-start | bytes 3538944 | tf_op jit(solution)/shard_map/reduce_scatter | solution.py:1742
  422.7 15.5 %copy-start.5 = (f32[9,32,32]{2,1,0:T(8,128)S(1)}, f32[9,32,32]{2,1,0:T(8,128)}, u32[]{:S(2)}) copy-start(f32[9,32,32]{2,1,0:T(8,128)} %get-tuple-element.117) | copy-start | bytes 110596
  422.7 15.6 %copy-start.30 = (f32[3,8,128]{2,1,0:T(8,128)S(1)}, f32[3,8,128]{2,1,0:T(8,128)}, u32[]{:S(2)}) copy-start(f32[3,8,128]{2,1,0:T(8,128)} %get-tuple-element.164) | copy-start | bytes 36868
  422.7 15.6 %copy-start.31 = (f32[3,8,128]{2,1,0:T(8,128)S(1)}, f32[3,8,128]{2,1,0:T(8,128)}, u32[]{:S(2)}) copy-start(f32[3,8,128]{2,1,0:T(8,128)} %get-tuple-element.163) | copy-start | bytes 36868
  422.7 15.6 %copy-start.32 = (f32[3,8,128]{2,1,0:T(8,128)S(1)}, f32[3,8,128]{2,1,0:T(8,128)}, u32[]{:S(2)}) copy-start(f32[3,8,128]{2,1,0:T(8,128)} %get-tuple-element.162) | copy-start | bytes 36868
  432.1 14.3 %all-to-all-start.16 = ((f32[32,1,1024]{2,1,0:T(1,128)}), f32[32,1,1024]{2,1,0:T(1,128)S(1)}, u32[]{:S(2)}, u32[]{:S(2)}) async-start(f32[32,1,1024]{2,1,0:T(1,128)} %get-tuple-element.157), calls=%async_computation.16 | async-start | bytes 262144 | tf_op jit(solution)/shard_map/all_to_all | solution.py:1320
  468.2 1.2 collective-permute-start.7
  470.2 13.7 %all-to-all-start.17 = ((f32[16,1,3840]{2,1,0:T(1,128)}), f32[16,1,3840]{2,1,0:T(1,128)S(1)}, u32[]{:S(2)}, u32[]{:S(2)}) async-start(f32[16,1,3840]{2,1,0:T(1,128)} %broadcast_in_dim.50), calls=%async_computation.18 | async-start | bytes 491520 | tf_op jit(solution)/shard_map/all_to_all | solution.py:1313
  474.0 63.3 %reduce-scatter.8.cloned.1.call-start = ((), (), s32[]{:S(2)}) async-start(), calls=%async_computation.28 | async-start | bytes 491520 | tf_op jit(solution)/shard_map/reduce_scatter | solution.py:1805
  474.5 66.9 %reduce-scatter.10.cloned.1.call-start = ((), (), s32[]{:S(2)}) async-start(), calls=%async_computation.29 | async-start | bytes 2359296 | tf_op jit(solution)/shard_map/reduce_scatter | solution.py:1822
  484.0 8.7 %collective-permute-start.8 = (f32[3840]{0:T(1024)S(1)}, f32[3840]{0:T(1024)S(1)}, u32[]{:S(2)}, u32[]{:S(2)}) collective-permute-start(f32[3840]{0:T(1024)S(1)} %reduce_sum.468), channel_id=1, source_target_pairs={{0,1},{1,0},{2,3},{3,2},{4,5},{5,4},{6,7},{7,6},{8,9},{9,8},{10,11... | collective-permute-start | bytes 46088 | tf_op jit(solution)/shard_map/ppermute | solution.py:1314
  514.1 22.9 %all-to-all-start.18 = ((f32[32,1,1024]{2,1,0:T(1,128)}), f32[32,1,1024]{2,1,0:T(1,128)S(1)}, u32[]{:S(2)}, u32[]{:S(2)}) async-start(f32[32,1,1024]{2,1,0:T(1,128)} %get-tuple-element.168), calls=%async_computation.19 | async-start | bytes 262144 | tf_op jit(solution)/shard_map/all_to_all | solution.py:1320
  516.8 93.8 %reduce-scatter.12.cloned.1.call-start = ((), (), s32[]{:S(2)}) async-start(), calls=%async_computation.30 | async-start | bytes 7077888 | tf_op jit(solution)/shard_map/reduce_scatter | solution.py:1863
  566.6 4.7 collective-permute-start.9
  573.9 34.8 %collective-permute-start.10 = (bf16[2,4,144,512]{3,2,1,0:T(8,128)(2,1)S(1)}, bf16[2,4,144,512]{3,2,1,0:T(8,128)(2,1)}, u32[]{:S(2)}, u32[]{:S(2)}) collective-permute-start(bf16[2,4,144,512]{3,2,1,0:T(8,128)(2,1)S(1)} %dynamic-slice_bitcast_fusion.1), channel_id=1, source_target_pairs={{0,8},{8,0},{16,24},{24,16},{1,9},{9,1},{17,25},{25,17},{2,10},{10... | collective-permute-start | bytes 3538952 | tf_op jit(solution)/shard_map/ppermute | solution.py:1373
  575.3 24.0 %copy-start.1 = (bf16[49,32,512]{2,1,0:T(8,128)(2,1)S(1)}, bf16[49,32,512]{2,1,0:T(8,128)(2,1)}, u32[]{:S(2)}) copy-start(bf16[49,32,512]{2,1,0:T(8,128)(2,1)} %get-tuple-element.116.refs_0_.refs_10_) | copy-start | bytes 4816900
  575.3 24.0 %copy-start.6 = (bf16[49,32,32]{2,1,0:T(8,128)(2,1)S(1)}, bf16[49,32,32]{2,1,0:T(8,128)(2,1)}, u32[]{:S(2)}) copy-start(bf16[49,32,32]{2,1,0:T(8,128)(2,1)} %get-tuple-element.186) | copy-start | bytes 301060
  594.7 12.6 %all-to-all-start.19 = ((f32[32,1,1024]{2,1,0:T(1,128)}), f32[32,1,1024]{2,1,0:T(1,128)S(1)}, u32[]{:S(2)}, u32[]{:S(2)}) async-start(f32[32,1,1024]{2,1,0:T(1,128)} %get-tuple-element.178), calls=%async_computation.22 | async-start | bytes 262144 | tf_op jit(solution)/shard_map/all_to_all | solution.py:1320
  599.0 81.1 %reduce-scatter.14.cloned.1.call-start = ((), (), s32[]{:S(2)}) async-start(), calls=%async_computation.31 | async-start | bytes 1310720 | tf_op jit(solution)/shard_map/reduce_scatter | solution.py:1890
  610.7 28.1 %collective-permute-start.11 = (bf16[1,4,144,512]{3,2,1,0:T(8,128)(2,1)S(1)}, bf16[1,4,144,512]{3,2,1,0:T(8,128)(2,1)S(1)}, u32[]{:S(2)}, u32[]{:S(2)}) collective-permute-start(bf16[1,4,144,512]{3,2,1,0:T(8,128)(2,1)S(1)} %constant_dynamic-slice_fusion), channel_id=1, source_target_pairs={{0,16},{8,24},{16,0},{24,8},{1,17},{9,25},{17,1},{25,9},{2,18},{10... | collective-permute-start | bytes 1769480 | tf_op jit(solution)/shard_map/ppermute | solution.py:1373
  627.4 12.9 %copy-start.4 = (bf16[768,512]{1,0:T(8,128)(2,1)S(1)}, bf16[768,512]{1,0:T(8,128)(2,1)}, u32[]{:S(2)}) copy-start(bf16[768,512]{1,0:T(8,128)(2,1)} %reduce-scatter.12.cloned.1.call-done) | copy-start | bytes 2359300
  627.4 12.9 %copy-start.10 = (bf16[256,512]{1,0:T(8,128)(2,1)S(1)}, bf16[256,512]{1,0:T(8,128)(2,1)}, u32[]{:S(2)}) copy-start(bf16[256,512]{1,0:T(8,128)(2,1)} %reduce-scatter.10.cloned.1.call-done) | copy-start | bytes 786436
  640.3 5.5 collective-permute-start.12
  647.3 27.7 %all-to-all-start.20 = ((bf16[4,280,512]{2,1,0:T(8,128)(2,1)}), bf16[4,280,512]{2,1,0:T(8,128)(2,1)S(1)}, u32[]{:S(2)}, u32[]{:S(2)}) async-start(bf16[4,280,512]{2,1,0:T(8,128)(2,1)} %pad_maximum_fusion), calls=%async_computation.24 | async-start | bytes 2293760 | tf_op jit(solution)/shard_map/all_to_all | solution.py:1379
  676.0 10.5 %all-to-all-start.21 = ((bf16[4,34,512]{2,1,0:T(8,128)(2,1)}), bf16[4,34,512]{2,1,0:T(8,128)(2,1)S(1)}, u32[]{:S(2)}, u32[]{:S(2)}) async-start(bf16[4,34,512]{2,1,0:T(8,128)(2,1)} %reshape.608), calls=%async_computation.25 | async-start | bytes 327680 | tf_op jit(solution)/shard_map/all_to_all | solution.py:1384
  (36 other events, 181.9 us)
Sparse Core Ops, SparseCore 0:
  12.0 101.0 all-gather.5
  116.5 61.6 all-gather.7
  417.0 47.9 reduce-scatter.5
  476.9 21.8 reduce-scatter.7
  501.9 39.4 reduce-scatter.9
  545.1 63.0 reduce-scatter.11
  641.6 25.3 reduce-scatter.13

commit v3 on v2

--- a/solution.py
+++ b/solution.py
@@ -242,15 +242,29 @@
     )
 
 
-def kernel_conv_down_weights(act_a, grad, dp, fsdp):
+def kernel_conv_down_weights(act_a, grad, raw_b, stats, mask, dp, fsdp):
     height, _, batch, middle = act_a.shape
     half = height // 2
     split = act_a.reshape(half, 2, half, 2, batch, middle)
     own = middle // (dp * fsdp)
     aligned = own % 16 == 0
 
-    def body(a_ref, g_ref, out_ref, cols):
+    def body(a_ref, n_ref, b_ref, s_ref, m_ref, out_ref, g_ref, cols):
         step = pl.program_id(0)
+
+        @pl.when(step == 0)
+        def _():
+            for c in chunks(middle):
+                scale, mean, shift, spread = (s_ref[n : n + 1, c] for n in range(4))
+                m = m_ref[:, : c.stop - c.start]
+
+                @pl.loop(0, half)
+                def _(i):
+                    for j in range(half):
+                        p = i * half + j
+                        value = scale * n_ref[p, :, c] - m * (shift + (b_ref[p, :, c] - mean) * spread)
+                        g_ref[p, :, c] = value.astype(BF)
+
         for r in range(3):
             for c in range(3):
                 top, left = int(r == 0), int(c == 0)
@@ -265,7 +279,7 @@
                         : half - top, int(r != 1), : half - left, int(c != 1)
                     ]
 
-        value = tn(cols[...].reshape(half * half * batch, middle), g_ref[...]).astype(BF)
+        value = tn(cols[...].reshape(half * half * batch, middle), g_ref[...].reshape(-1, middle)).astype(BF)
         if not aligned:
             out_ref[0] = value
             return
@@ -281,21 +295,21 @@
     else:
         out = ((9, middle, middle), BF)
         out_block = (1, middle, middle), lambda t: (t, 0, 0)
-    value = call(
+    value, strided_grad = call(
         body,
         (9,),
-        (split, grad.reshape(-1, middle)),
-        (whole(split.shape), whole((half * half * batch, middle))),
-        (out,),
-        (out_block,),
+        (split, grad, raw_b, stats, mask),
+        (whole(split.shape), whole(grad.shape), whole(raw_b.shape), whole(stats.shape), whole(mask.shape)),
+        (out, (grad.shape, BF)),
+        (out_block, whole(grad.shape)),
         scratch=[pltpu.VMEM((half, half, batch, middle), BF)],
         flops=2 * half * half * batch * 9 * middle * middle,
-        moved=act_a.size * 2 + grad.size * 2 + 18 * middle * middle,
-    )[0]
+        moved=act_a.size * 2 + grad.size * 10 + 18 * middle * middle,
+    )
     if not aligned:
         value = value.reshape(9, dp, fsdp // 2, 2, own, middle).transpose(3, 1, 2, 0, 4, 5)
         value = value.reshape(2, dp, fsdp // 2, 9 * own, middle)[:, jnp.array(by_low_bit(dp))]
-    return value
+    return value, strided_grad
 
 
 def kernel_conv_down_back(grad, taps, raw_a, stats, mask):
@@ -610,39 +624,45 @@
     )
 
 
-def kernel_project(sampled, mask, weight, half):
+def kernel_project(sampled, mask, weight):
     pixels, batch, c_in = sampled.shape
     middle = weight.array.shape[2]
     wide = weight.count * middle
 
     def body(x_ref, m_ref, w_ref, raw_ref, off_ref, sum_ref):
-        zero_first(sum_ref)
-
-        @pl.when(pl.program_id(0) == 0)
-        def _():
-            for k in range(weight.count):
-                few = nn(x_ref[half // 2], weight.of(w_ref, k))
-                off_ref[0:1, k * middle : (k + 1) * middle] = mean_of(few, m_ref[:, :1])
-
         m = m_ref[:, :1]
-        left = x_ref[...].reshape(half * batch, c_in)
-        for k in range(weight.count):
-            raw = nn(left, weight.of(w_ref, k)).reshape(half, batch, middle)
-            span = slice(k * middle, (k + 1) * middle)
-            offset = off_ref[0:1, span]
-            raw_ref[:, :, span] = (raw - offset).astype(BF)
-            sum_ref[0, :, span] += fold(jnp.sum(raw, axis=0) * m)
-            sum_ref[1, :, span] += fold(jnp.sum(raw * raw, axis=0) * m)
-
+        w = w_ref[...].reshape(c_in, middle)
+        offset = mean_of(nn(x_ref[pixels // 2], w), m)
+        off_ref[...] = jnp.broadcast_to(offset, off_ref.shape)
+        part = 7
+        first = second = None
+        for p in range(0, pixels, part):
+            raw = nn(x_ref[p : p + part].reshape(part * batch, c_in), w).reshape(part, batch, middle)
+            raw_ref[p : p + part] = (raw - offset).astype(BF)
+            one, two = jnp.sum(raw, axis=0), jnp.sum(raw * raw, axis=0)
+            first = one if first is None else first + one
+            second = two if second is None else second + two
+        sum_ref[0] = fold(first * m)
+        sum_ref[1] = fold(second * m)
+
+    groups = weight.array.shape[0]
     return call(
         body,
-        (half,),
+        (weight.count,),
         (sampled, mask, weight.array),
-        (row_block(half, batch, c_in), whole(mask.shape), weight.block()),
+        (
+            whole(sampled.shape),
+            whole(mask.shape),
+            ((groups, weight.rows, middle), lambda k: (0, weight.first + k, 0)),
+        ),
         (((pixels, batch, wide), BF), ((8, wide), F32), ((2, 8, wide), F32)),
-        (row_block(half, batch, wide), whole((8, wide)), whole((2, 8, wide))),
+        (
+            ((pixels, batch, middle), lambda k: (0, 0, k)),
+            ((8, middle), lambda k: (0, k)),
+            ((2, 8, middle), lambda k: (0, 0, k)),
+        ),
         flops=2 * sampled.size * wide,
-        moved=sampled.size * 2 + pixels * batch * wide * 4,
+        moved=sampled.size * 2 + pixels * batch * wide * 2,
     )
 
 
@@ -1534,7 +1554,7 @@
         .transpose(2, 3, 0, 1, 4)
         .reshape(area, batch, c_in)
     )
-    raw_p, off_p, sums_p = kernel_project(sampled, mask_rows, project1, half)
+    raw_p, off_p, sums_p = kernel_project(sampled, mask_rows, project1)
 
     def moments(raw):
         return total_over(raw * mask), total_over(raw * raw * mask)
@@ -1643,10 +1663,6 @@
 
     shifts = [None] * 11
     spreads = [None] * 11
-
-    def grad_raw(index, grad, raw, mean, inv, weight, number):
-        unit = (raw - mean) * inv
-        return gain[index] * inv * (grad - weight * (shifts[index] + unit * spreads[index]) / number)
 
     result, grad_total, sums_e = kernel_result(
         raw_e,
@@ -1861,11 +1877,11 @@
     own_kernels = mine_a[blocks * rowse :].reshape(-1)[:size_s]
     mine_b = packed_b.reshape(-1, middle)
     mine_b = lax.psum_scatter(mine_b, "fsdp", scatter_dimension=0, tiled=True)
-    strided_grad = grad_raw(
-        1, grad_strided, raw_b, mean_b, inv_b, mask_rows[:, :1], count
-    ).astype(BF)
+    grad_spatial1, strided_grad = kernel_conv_down_weights(
+        act_a, grad_strided, raw_b, jnp.stack(back_stats(1, mean_b, inv_b)), mask_rows, dp, fsdp
+    )
     strided_grad = strided_grad.reshape(half, half, batch, middle)
-    sum_c1 = scatter_cores(dp, fsdp, kernel_conv_down_weights(act_a, strided_grad, dp, fsdp))
+    sum_c1 = scatter_cores(dp, fsdp, grad_spatial1)
     strided_grad, sum_c1 = lax.optimization_barrier((strided_grad, sum_c1))
     sum_c = scatter_halves(dp, sum_c1.reshape((2, -1) + sum_c1.shape[1:]), 0)
     grad_first, sums_first = kernel_conv_down_back(
@@ -1907,16 +1923,18 @@
     sum_d = sum_d.reshape((dp, fsdp // 2, 2) + sum_d.shape[1:]).transpose(2, 1, 0, 3, 4)
     sum_d = scatter_cores(dp, fsdp, sum_d).reshape(fsdp // 2, -1, middle)
     both = scatter_fsdp(fsdp, jnp.concatenate([sum_d, sum_c], axis=1))
+    grad_features = None
+    for pair in range(slots // 2):
+        grad_features = kernel_grad_features(
+            first_grad, full_reduce1, shortcut_grad, project1, height, frames, pair, grad_features
+        )
+        if pair == 0:
+            grad_features, both = lax.optimization_barrier((grad_features, both))
     own_spatial1 = both[dp * rows_d :]
     sum_d = scatter_dp(both[: dp * rows_d].astype(BF).reshape(dp, rows_d, middle))
     rows_first = c_in // devices
     own_reduce1 = sum_d[:rows_first]
     own_motion = sum_d[rows_first:].reshape(-1)[: 2 * size_m].reshape(2, own, narrow)
-    grad_features = None
-    for pair in range(slots // 2):
-        grad_features = kernel_grad_features(
-            first_grad, full_reduce1, shortcut_grad, project1, height, frames, pair, grad_features
-        )
     grad_features = grad_features.reshape(slots, height, height, frames, c_in)
     return (
         result.transpose(0, 3, 1, 2, 4),

time: 708 us -> 705 us (level)
  transfers between devices with their start and end apart: 39 -> 39, of which waited for: 25 -> 25; matrix products, arithmetic and copies ran while one was open for 11% -> 11% of each run, Pallas kernels for 35% -> 36%
where the time goes in v3:
time: 705 us; the launch traced here: 693 us
  Pallas kernels  321 us (46%)
  waiting for transfers between devices  129 us (18%)
  starting transfers between devices  76.3 us (11%)
  local copies, waits for them, and re-layouts  52.2 us (7%)
  other arithmetic  49.2 us (7%)
  blocking collectives  41.9 us (6%)
  between operations  18.1 us (3%)
    pallas_call x25, Pallas kernels, call(): pl.pallas_call(body, grid=grid, in_specs=[spec(b) for b in in_blocks], ou...  261 us
    all_to_all x10, waiting for transfers between devices, ready(): total = jnp.sum(lax.all_to_all(copies, AXES, 0, 0, tiled=True), axis=(0, 1))  38.6 us
    pallas_call x4, Pallas kernels, kernel_weight_grad(): pl.pallas_call(body, grid=(columns // middle,), in_specs=in_specs, out_sp...  36.6 us
    all_to_all x10, starting transfers between devices, ready(): total = jnp.sum(lax.all_to_all(copies, AXES, 0, 0, tiled=True), axis=(0, 1))  35.1 us
    all_to_all x2, blocking collectives, flat(): lax.all_to_all(copies, AXES, 0, 0, axis_index_groups=self.groups)  32 us
    all_gather x2, waiting for transfers between devices, gather(): return lax.all_gather(value, AXES, axis=0, tiled=False)  29.5 us
    pallas_call x2, Pallas kernels, kernel_grad_features(): pl.pallas_call(body, grid=(parts,), in_specs=in_specs, out_specs=pl.Block...  24.1 us
  transfers between devices with their start and end apart: 39, of which 25 were waited for; matrix products, arithmetic and copies ran while one was open for 11% of the time, Pallas kernels for 36%

profile of v3, /device:TPU:0, one launch (start us, length us, event | category | flops | bytes accessed | tf_op | source)
XLA Modules:
  0.0 692.6 jit_solution(4104697642529548497)
XLA Ops:
  12.6 6.3 all-to-all-start
  19.4 5.6 all-to-all-done
  25.8 3.7 all-to-all-start.1
  31.1 5.1 all-to-all-done.1
  40.0 16.6 %shard_map.298 = (bf16[14,14,32,512]{3,2,1,0:T(8,128)(2,1)}, f32[8,512]{1,0:T(8,128)}, f32[2,8,512]{2,1,0:T(8,128)}) custom-call(bf16[4,1568,1024]{2,1,0:T(8,128)(2,1)} %bitcast.300, bf16[1024,512]{1,0:T(8,128)(2,1)} %bitcast.309, f32[32,256]{1,0:T(8,128)} %broadcast_in_dim.37.m_ref.refs_4_.refs_5_.refs_7_), custom_call_target="tpu_custom_call" | custom-call | flops 6576668672 | bytes 19267584 | tf_op jit(solution)/shard_map/pallas_call | solution.py:75
  59.5 3.8 all-to-all-start.2
  68.4 3.4 all-to-all-done.2
  74.5 9.1 %shard_map.299.a_ref = bf16[14,14,32,512]{3,2,1,0:T(8,128)(2,1)} custom-call(bf16[14,14,32,512]{3,2,1,0:T(8,128)(2,1)} %get-tuple-element.107.a_ref, f32[2,512]{1,0:T(2,128)} %pad_maximum_fusion.18.s_ref, f32[32,256]{1,0:T(8,128)} %broadcast_in_dim.37.m_ref.refs_4_.refs_5_.refs_7_), custom_call_target="tpu_custom_call" | custom-call | flops 32112640 | bytes 19267584 | tf_op jit(solution)/shard_map/pallas_call | solution.py:75
  83.6 29.5 %all-gather.6.cloned.1.call-done = bf16[12800,512]{1,0:T(8,128)(2,1)} async-done(((bf16[400,512]{1,0:T(8,128)(2,1)}), bf16[12800,512]{1,0:T(8,128)(2,1)}) %all-gather.6.cloned.1.call-update) | async-done | bytes 13107216 | tf_op jit(solution)/shard_map/all_gather | solution.py:1474
  113.1 13.5 %shard_map.300 = (f32[7,7,32,512]{3,2,1,0:T(8,128)}, f32[32,1,1024]{2,1,0:T(1,128)}) custom-call(bf16[14,14,32,512]{3,2,1,0:T(8,128)(2,1)} %shard_map.299.a_ref, f32[32,256]{1,0:T(8,128)} %broadcast_in_dim.37.m_ref.refs_4_.refs_5_.refs_7_, bf16[32,400,512]{2,1,0:T(8,128)(2,1)} %bitcast.271, bf16[32,400,512]{2,1,0:T(8,128)(2,1)} %bitcast.272, ...), custom_call_target="tpu_custom_call" | custom-call | flops 7398752256 | bytes 11141120 | tf_op jit(solution)/shard_map/pallas_call | solution.py:75
  129.3 11.9 %shard_map.302 = (bf16[49,32,2048]{2,1,0:T(8,128)(2,1)}, f32[8,2048]{1,0:T(8,128)}, f32[2,8,2048]{2,1,0:T(8,128)}) custom-call(bf16[49,32,1024]{2,1,0:T(8,128)(2,1)} %bitcast.323, f32[32,256]{1,0:T(8,128)} %broadcast_in_dim.37.m_ref.refs_4_.refs_5_.refs_7_, bf16[32,400,512]{2,1,0:T(8,128)(2,1)} %bitcast.280), custom_call_target="tpu_custom_call" | custom-call | flops 6576668672 | bytes 9633792 | tf_op jit(solution)/shard_map/pallas_call | solution.py:75
  143.0 10.6 %shard_map.301 = (bf16[49,32,512]{2,1,0:T(8,128)(2,1)}, bf16[49,32,2048]{2,1,0:T(8,128)(2,1)}, f32[8,2048]{1,0:T(8,128)}, f32[2,8,2048]{2,1,0:T(8,128)}) custom-call(f32[49,32,512]{2,1,0:T(8,128)} %bitcast.303, f32[2,512]{1,0:T(2,128)} %pad_maximum_fusion.19.s_ref, f32[32,256]{1,0:T(8,128)} %broadcast_in_dim.37.m_ref.refs_4_.refs_5_.refs_7_, ...), custom_call_target="tpu_custom_call" | custom-call | flops 3288334336 | bytes 17661952 | tf_op jit(solution)/shard_map/pallas_call | solution.py:75
  156.1 21.0 %all_to_all.117 = f32[16,1,4096]{2,1,0:T(1,128)S(1)} all-to-all(f32[16,1,4096]{2,1,0:T(1,128)S(1)} %broadcast_in_dim.40), channel_id=1, replica_groups={{0,2,4,6,8,10,12,14,16,18,20,22,24,26,28,30},{1,3,5,7,9,11,13,15,17,19,..., dimensions={0} | all-to-all | bytes 524288 | tf_op jit(solution)/shard_map/all_to_all | solution.py:1333
  180.5 13.3 %shard_map.303 = (bf16[49,32,2048]{2,1,0:T(8,128)(2,1)}, f32[49,32,512]{2,1,0:T(8,128)}, f32[32,1,1024]{2,1,0:T(1,128)}) custom-call(bf16[49,32,2048]{2,1,0:T(8,128)(2,1)} %get-tuple-element.112.c_ref, bf16[49,32,2048]{2,1,0:T(8,128)(2,1)} %get-tuple-element.113.p_ref, f32[8,2048]{1,0:T(8,128)} %stack.299.s_ref, ...), custom_call_target="tpu_custom_call" | custom-call | flops 3288334336 | bytes 32112640 | tf_op jit(solution)/shard_map/pallas_call | solution.py:75
  193.8 3.1 all-to-all-start.5
  199.6 5.5 all-to-all-done.5
  205.8 4.6 shard_map.304
  220.0 6.3 all-to-all-done.6
  229.6 4.3 shard_map.305
  237.6 6.2 all-to-all-done.7
  244.5 3.7 shard_map.306
  251.9 6.2 all-to-all-done.8
  258.9 3.7 shard_map.307
  262.5 9.8 %all_to_all.118 = f32[32,1,256]{2,1,0:T(1,128)S(1)} all-to-all(f32[32,1,256]{2,1,0:T(1,128)} %get-tuple-element.131), channel_id=1, replica_groups=mesh['dp'=4,'fsdp'=8] {'dp','fsdp'}, dimensions={0} | all-to-all | bytes 65536 | tf_op jit(solution)/shard_map/all_to_all | solution.py:1340
  273.1 10.3 %shard_map.308 = (bf16[49,32,512]{2,1,0:T(8,128)(2,1)}, bf16[49,32,2048]{2,1,0:T(8,128)(2,1)}, f32[8,2048]{1,0:T(8,128)}, f32[2,8,2048]{2,1,0:T(8,128)}) custom-call(bf16[49,32,512]{2,1,0:T(8,128)(2,1)} %get-tuple-element.123.refs_0_.x_ref.refs_5_, bf16[49,32,128]{2,1,0:T(8,128)(2,1)} %get-tuple-element.126.o1.refs_8_, ...), custom_call_target="tpu_custom_call" | custom-call | flops 3288334336 | bytes 16056320 | tf_op jit(solution)/shard_map/pallas_call | solution.py:75
  285.8 11.0 %all_to_all.119 = f32[16,1,2048]{2,1,0:T(1,128)S(1)} all-to-all(f32[16,1,2048]{2,1,0:T(1,128)S(1)} %broadcast_in_dim.44), channel_id=1, replica_groups={{0,2,4,6,8,10,12,14,16,18,20,22,24,26,28,30},{1,3,5,7,9,11,13,15,17,19,..., dimensions={0} | all-to-all | bytes 262144 | tf_op jit(solution)/shard_map/all_to_all | solution.py:1333
  298.8 16.4 %shard_map.309 = (bf16[4,7,7,8,2048]{4,3,2,1,0:T(8,128)(2,1)}, bf16[49,32,2048]{2,1,0:T(8,128)(2,1)}, f32[2,8,2048]{2,1,0:T(8,128)}) custom-call(bf16[49,32,2048]{2,1,0:T(8,128)(2,1)} %get-tuple-element.132.e_ref, bf16[49,32,2048]{2,1,0:T(8,128)(2,1)} %get-tuple-element.133.o_ref.refs_0_, bf16[4,7,7,8,2048]{4,3,2,1,0:T(8,128)(2,1)} %bitcast.315, ...), custom_call_target="tpu_custom_call" | custom-call | flops 64225280 | bytes 44957696 | tf_op jit(solution)/shard_map/pallas_call | solution.py:75
  318.2 3.5 all-to-all-start.11
  325.3 4.7 all-to-all-done.11
  332.0 14.4 %shard_map.310 = (bf16[49,32,2048]{2,1,0:T(8,128)(2,1)}, f32[49,32,512]{2,1,0:T(8,128)}, f32[49,32,128]{2,1,0:T(8,128)}, f32[32,1,256]{2,1,0:T(1,128)}) custom-call(bf16[49,32,2048]{2,1,0:T(8,128)(2,1)} %get-tuple-element.137.g_ref.t_ref, bf16[49,32,2048]{2,1,0:T(8,128)(2,1)} %get-tuple-element.132.e_ref, f32[4,2048]{1,0:T(4,128)} %pad_maximum_fusion.6.s_ref, ...), custom_call_target="tpu_custom_call" | custom-call | flops 3288334336 | bytes 32112640 | tf_op jit(solution)/shard_map/pallas_call | solution.py:75
  349.5 6.7 all-to-all-done.12
  357.4 5.4 shard_map.311
  365.4 7.9 %shard_map.314 = bf16[8,4,64,512]{3,2,1,0:T(8,128)(2,1)} custom-call(bf16[49,32,512]{2,1,0:T(8,128)(2,1)} %get-tuple-element.151.refs_0_, bf16[49,32,2048]{2,1,0:T(8,128)(2,1)} %get-tuple-element.152.refs_1_), custom_call_target="tpu_custom_call" | custom-call | flops 3288334336 | bytes 10125312 | tf_op jit(solution)/shard_map/pallas_call | solution.py:1011
  374.5 5.5 shard_map.312
  380.0 6.0 all-to-all-start.14
  386.0 3.2 shard_map.317
  389.2 3.2 shard_map.316
  394.5 5.5 shard_map.313
  402.1 5.1 all-to-all-start.15
  407.2 3.2 shard_map.315
  412.5 3.6 fusion.2
  421.8 9.5 %shard_map.318 = (f32[49,32,512]{2,1,0:T(8,128)}, bf16[49,32,32]{2,1,0:T(8,128)(2,1)}, f32[32,1,1024]{2,1,0:T(1,128)}) custom-call(f32[49,32,512]{2,1,0:T(8,128)} %get-tuple-element.139.refs_6_.j_ref, f32[49,32,128]{2,1,0:T(8,128)} %get-tuple-element.148.p1, f32[49,32,128]{2,1,0:T(8,128)} %get-tuple-element.146.refs_8_.p2, ...), custom_call_target="tpu_custom_call" | custom-call | flops 51380224 | bytes 9633792 | tf_op jit(solution)/shard_map/pallas_call | solution.py:75
  431.3 6.1 all-to-all-start.16
  437.7 8.0 %all-to-all-done.16 = f32[32,1,1024]{2,1,0:T(1,128)S(1)} async-done(((f32[32,1,1024]{2,1,0:T(1,128)}), f32[32,1,1024]{2,1,0:T(1,128)S(1)}, u32[]{:S(2)}, u32[]{:S(2)}) %all-to-all-start.16) | async-done | bytes 131104 | tf_op jit(solution)/shard_map/all_to_all | solution.py:1340
  447.0 19.1 %shard_map.319 = (bf16[49,32,512]{2,1,0:T(8,128)(2,1)}, bf16[49,32,2048]{2,1,0:T(8,128)(2,1)}, f32[3,8,2048]{2,1,0:T(8,128)}) custom-call(f32[49,32,512]{2,1,0:T(8,128)} %get-tuple-element.160.n_ref, f32[49,32,512]{2,1,0:T(8,128)} %get-tuple-element.118.d_ref, f32[4,512]{1,0:T(4,128)} %pad_maximum_fusion.16.sd_ref, bf16[32,400,512]{2,1,0:T(8,128)(2,1)} %bitcast.283, ...), custom_call_target="tpu_custom_call" | custom-call | flops 3288334336 | bytes 51380224 | tf_op jit(solution)/shard_map/pallas_call | solution.py:75
  469.5 3.7 all-to-all-start.17
  473.8 9.3 %all-to-all-done.17 = f32[16,1,3840]{2,1,0:T(1,128)S(1)} async-done(((f32[16,1,3840]{2,1,0:T(1,128)}), f32[16,1,3840]{2,1,0:T(1,128)S(1)}, u32[]{:S(2)}, u32[]{:S(2)}) %all-to-all-start.17) | async-done | bytes 245792 | tf_op jit(solution)/shard_map/all_to_all | solution.py:1333
  483.4 8.6 %shard_map.320 = bf16[8,4,64,512]{3,2,1,0:T(8,128)(2,1)} custom-call(bf16[49,32,2048]{2,1,0:T(8,128)(2,1)} %get-tuple-element.133.o_ref.refs_0_, bf16[49,32,512]{2,1,0:T(8,128)(2,1)} %get-tuple-element.169.refs_1_), custom_call_target="tpu_custom_call" | custom-call | flops 3288334336 | bytes 10125312 | tf_op jit(solution)/shard_map/pallas_call | solution.py:1011
  493.4 20.0 %shard_map.321 = (bf16[49,32,2048]{2,1,0:T(8,128)(2,1)}, bf16[49,32,2048]{2,1,0:T(8,128)(2,1)}, f32[49,32,512]{2,1,0:T(8,128)}, f32[32,1,1024]{2,1,0:T(1,128)}) custom-call(bf16[49,32,2048]{2,1,0:T(8,128)(2,1)} %get-tuple-element.162.g_ref, bf16[49,32,2048]{2,1,0:T(8,128)(2,1)} %get-tuple-element.112.c_ref, bf16[49,32,2048]{2,1,0:T(8,128)(2,1)} %get-tuple-element.113.p_ref, ...), custom_call_target="tpu_custom_call" | custom-call | flops 3288334336 | bytes 51380224 | tf_op jit(solution)/shard_map/pallas_call | solution.py:75
  516.3 8.1 %shard_map.322.refs_2_ = bf16[8,4,192,512]{3,2,1,0:T(8,128)(2,1)} custom-call(bf16[49,32,512]{2,1,0:T(8,128)(2,1)} %get-tuple-element.174.refs_0_, bf16[49,32,2048]{2,1,0:T(8,128)(2,1)} %get-tuple-element.175.refs_1_), custom_call_target="tpu_custom_call" | custom-call | flops 3288334336 | bytes 10125312 | tf_op jit(solution)/shard_map/pallas_call | solution.py:1011
  524.5 11.9 %shard_map.323 = bf16[8,4,192,512]{3,2,1,0:T(8,128)(2,1)} custom-call(bf16[49,32,1024]{2,1,0:T(8,128)(2,1)} %bitcast.324, bf16[49,32,2048]{2,1,0:T(8,128)(2,1)} %get-tuple-element.173.refs_1_.s_ref, bf16[8,4,192,512]{3,2,1,0:T(8,128)(2,1)} %shard_map.322.refs_2_), custom_call_target="tpu_custom_call", output_to_operand_aliasing={{}: (2, {})} | custom-call | flops 6576668672 | bytes 13828096 | tf_op jit(solution)/shard_map/pallas_call | solution.py:1011
  536.5 4.1 reduce-scatter.10.cloned.1.call-done
  541.3 18.6 %shard_map.324 = (bf16[2,4,4,144,512]{4,3,2,1,0:T(8,128)(2,1)}, bf16[49,32,512]{2,1,0:T(8,128)(2,1)}) custom-call(bf16[7,2,7,2,32,512]{5,4,3,2,1,0:T(8,128)(2,1)} %bitcast.298, f32[49,32,512]{2,1,0:T(8,128)} %get-tuple-element.171.n_ref, f32[49,32,512]{2,1,0:T(8,128)} %bitcast.305, f32[4,512]{1,0:T(4,128)} %fusion.52.s_ref, ...), custom_call_target="tpu_custom_call" | custom-call | flops 7398752256 | bytes 19169280 | tf_op jit(solution)/shard_map/pallas_call | solution.py:75
  559.9 3.3 dynamic-slice_bitcast_fusion
  563.8 4.1 collective-permute-done.9
  572.8 19.3 %shard_map.325 = (bf16[7,2,7,2,32,512]{5,4,3,2,1,0:T(8,128)(2,1)}, f32[32,1,1024]{2,1,0:T(1,128)}) custom-call(bf16[7,7,32,512]{3,2,1,0:T(8,128)(2,1)} %bitcast.313, bf16[7,7,32,512]{3,2,1,0:T(8,128)(2,1)} %bitcast.314, bf16[7,2,7,2,32,512]{5,4,3,2,1,0:T(8,128)(2,1)} %bitcast.296, f32[4,512]{1,0:T(4,128)} %fusion.46.s_ref, ...), custom_call_target="tpu_custom_call" | custom-call | flops 7398752256 | bytes 30408704 | tf_op jit(solution)/shard_map/pallas_call | solution.py:75
  592.0 4.3 all-to-all-start.19
  599.4 5.3 all-to-all-done.19
  610.0 15.8 %shard_map.326 = (bf16[4,1568,512]{2,1,0:T(8,128)(2,1)}, bf16[1024,512]{1,0:T(8,128)(2,1)}) custom-call(bf16[14,14,32,512]{3,2,1,0:T(8,128)(2,1)} %bitcast.316, bf16[14,14,32,512]{3,2,1,0:T(8,128)(2,1)} %get-tuple-element.107.a_ref, bf16[4,1568,1024]{2,1,0:T(8,128)(2,1)} %bitcast.302, f32[4,512]{1,0:T(4,128)} %fusion.48.s_ref, ...), custom_call_target="tpu_custom_call" | custom-call | flops 6576668672 | bytes 32112640 | tf_op jit(solution)/shard_map/pallas_call | solution.py:75
  625.8 11.2 %collective-permute-done.11 = bf16[1,4,144,512]{3,2,1,0:T(8,128)(2,1)S(1)} collective-permute-done((bf16[1,4,144,512]{3,2,1,0:T(8,128)(2,1)S(1)}, bf16[1,4,144,512]{3,2,1,0:T(8,128)(2,1)S(1)}, u32[]{:S(2)}, u32[]{:S(2)}) %collective-permute-start.11) | collective-permute-done | bytes 589856 | tf_op jit(solution)/shard_map/ppermute | solution.py:1393
  642.0 3.6 all-to-all-start.20
  649.9 12.1 %shard_map.327.refs_0_ = bf16[4,1568,1024]{2,1,0:T(8,128)(2,1)} custom-call(bf16[4,1568,512]{2,1,0:T(8,128)(2,1)} %get-tuple-element.188.g_ref, bf16[1024,512]{1,0:T(8,128)(2,1)} %bitcast.310, bf16[49,32,2048]{2,1,0:T(8,128)(2,1)} %get-tuple-element.173.refs_1_.s_ref, bf16[32,400,512]{2,1,0:T(8,128)(2,1)} %bitcast.294), custom_call_target="tpu_custom_call" | custom-call | flops 6576668672 | bytes 12845056 | tf_op jit(solution)/shard_map/pallas_call | solution.py:508
  662.9 3.6 all-to-all-start.21
  667.4 12.0 %shard_map.328 = bf16[4,1568,1024]{2,1,0:T(8,128)(2,1)} custom-call(bf16[4,1568,512]{2,1,0:T(8,128)(2,1)} %get-tuple-element.188.g_ref, bf16[1024,512]{1,0:T(8,128)(2,1)} %bitcast.311, bf16[49,32,2048]{2,1,0:T(8,128)(2,1)} %get-tuple-element.173.refs_1_.s_ref, bf16[32,400,512]{2,1,0:T(8,128)(2,1)} %bitcast.295, ...), custom_call_target="tpu_custom_call", output_to_operand_aliasing={{}: (4, {})} | custom-call | flops 6576668672 | bytes 12845056 | tf_op jit(solution)/shard_map/pallas_call | solution.py:508
  (413 shorter events, 130.7 us)
Async XLA Ops:
  7.2 12.1 %copy-start.10 = (bf16[16,2048]{1,0:T(8,128)(2,1)S(1)}, bf16[16,2048]{1,0:T(8,128)(2,1)}, u32[]{:S(2)}) copy-start(bf16[16,2048]{1,0:T(8,128)(2,1)} %param.31) | copy-start | bytes 196612
  7.2 105.9 %all-gather.6.cloned.1.call-start = ((), (), s32[]{:S(2)}) async-start(), calls=%async_computation.32 | async-start | bytes 13516800 | tf_op jit(solution)/shard_map/all_gather | solution.py:1474
  9.2 21.8 %copy-start.49 = (s32[4,8]{1,0:T(4,128)S(1)}, s32[4,8]{1,0:T(4,128)}, u32[]{:S(2)}) copy-start(s32[4,8]{1,0:T(4,128)} %param.21) | copy-start | bytes 388
  9.2 21.8 %copy-start.52 = (s32[4]{0:T(128)S(1)}, s32[4]{0:T(128)}, u32[]{:S(2)}) copy-start(s32[4]{0:T(128)} %param.20) | copy-start | bytes 52
  12.6 12.4 %all-to-all-start = ((bf16[4,32,512]{2,1,0:T(8,128)(2,1)}), bf16[4,32,512]{2,1,0:T(8,128)(2,1)S(1)}, u32[]{:S(2)}, u32[]{:S(2)}) async-start(bf16[4,32,512]{2,1,0:T(8,128)(2,1)} %broadcast_in_dim.34), calls=%async_computation | async-start | bytes 262144 | tf_op jit(solution)/shard_map/all_to_all | solution.py:1366
  25.8 10.3 %all-to-all-start.1 = ((bf16[4,4,32,512]{3,2,1,0:T(8,128)(2,1)}), bf16[4,4,32,512]{3,2,1,0:T(8,128)(2,1)S(1)}, u32[]{:S(2)}, u32[]{:S(2)}) async-start(bf16[4,4,32,512]{3,2,1,0:T(8,128)(2,1)} %broadcast_in_dim.35), calls=%async_computation.1 | async-start | bytes 1048576 | tf_op jit(solution)/shard_map/all_to_all | solution.py:1367
  29.5 167.4 %all-gather.8.cloned.1.call-start = ((), (), s32[]{:S(2)}) async-start(), calls=%async_computation.33 | async-start | bytes 3244032 | tf_op jit(solution)/shard_map/all_gather | solution.py:1474
  31.0 369.9 %copy-start.50 = (f32[4,8]{1,0:T(4,128)}, f32[4,8]{1,0:T(4,128)S(1)}, u32[]{:S(2)}) copy-start(f32[4,8]{1,0:T(4,128)S(1)} %get-tuple-element.247) | copy-start | bytes 388
  36.2 1.9 collective-permute-start
  59.5 12.3 %all-to-all-start.2 = ((f32[32,1,1280]{2,1,0:T(1,128)}), f32[32,1,1280]{2,1,0:T(1,128)S(1)}, u32[]{:S(2)}, u32[]{:S(2)}) async-start(f32[32,1,1280]{2,1,0:T(1,128)} %broadcast_in_dim.39), calls=%async_computation.2 | async-start | bytes 327680 | tf_op jit(solution)/shard_map/all_to_all | solution.py:1326
  73.9 489.3 %copy-start.19 = (f32[512]{0:T(512)}, f32[512]{0:T(512)S(1)}, u32[]{:S(2)}) copy-start(f32[512]{0:T(512)S(1)} %get-tuple-element.274) | copy-start | bytes 6148
  73.9 489.3 %copy-start.20 = (f32[512]{0:T(512)}, f32[512]{0:T(512)S(1)}, u32[]{:S(2)}) copy-start(f32[512]{0:T(512)S(1)} %get-tuple-element.275) | copy-start | bytes 6148
  126.5 15.7 %all-to-all-start.3 = ((f32[32,1,1024]{2,1,0:T(1,128)}), f32[32,1,1024]{2,1,0:T(1,128)S(1)}, u32[]{:S(2)}, u32[]{:S(2)}) async-start(f32[32,1,1024]{2,1,0:T(1,128)} %get-tuple-element.111), calls=%async_computation.3 | async-start | bytes 262144 | tf_op jit(solution)/shard_map/all_to_all | solution.py:1340
  143.0 34.4 %copy-start.35 = (f32[3,3,128]{2,1,0:T(4,128)S(1)}, f32[3,3,128]{2,1,0:T(4,128)}, u32[]{:S(2)}) copy-start(f32[3,3,128]{2,1,0:T(4,128)} %param.35) | copy-start | bytes 13828
  154.7 1.2 collective-permute-start.1
  177.3 2.4 collective-permute-start.2
  193.8 11.3 %all-to-all-start.5 = ((f32[32,1,1024]{2,1,0:T(1,128)}), f32[32,1,1024]{2,1,0:T(1,128)S(1)}, u32[]{:S(2)}, u32[]{:S(2)}) async-start(f32[32,1,1024]{2,1,0:T(1,128)} %get-tuple-element.119), calls=%async_computation.5 | async-start | bytes 262144 | tf_op jit(solution)/shard_map/all_to_all | solution.py:1340
  196.9 204.1 %copy-start.34 = (f32[4,8]{1,0:T(4,128)}, f32[4,8]{1,0:T(4,128)S(1)}, u32[]{:S(2)}) copy-start(f32[4,8]{1,0:T(4,128)S(1)} %get-tuple-element.340) | copy-start | bytes 388
  196.9 223.4 %copy-start.48 = (f32[4,8]{1,0:T(4,128)}, f32[4,8]{1,0:T(4,128)S(1)}, u32[]{:S(2)}) copy-start(f32[4,8]{1,0:T(4,128)S(1)} %get-tuple-element.339) | copy-start | bytes 388
  198.7 13.3 %copy-start.16 = (f32[9,32]{1,0:T(8,128)S(1)}, f32[9,32]{1,0:T(8,128)}, u32[]{:S(2)}) copy-start(f32[9,32]{1,0:T(8,128)} %param.34) | copy-start | bytes 3460
  199.6 18.1 %copy-start.11 = (f32[7,7,9]{1,2,0:T(8,128)S(1)}, f32[7,7,9]{1,2,0:T(8,128)}, u32[]{:S(2)}) copy-start(f32[7,7,9]{1,2,0:T(8,128)} %constant.124.clone) | copy-start | bytes 5296
  213.9 187.1 %copy-start.21 = (f32[4,8,32]{2,1,0:T(8,128)}, f32[4,8,32]{2,1,0:T(8,128)S(1)}, u32[]{:S(2)}) copy-start(f32[4,8,32]{2,1,0:T(8,128)S(1)} %get-tuple-element.256) | copy-start | bytes 12292
  215.1 11.2 %all-to-all-start.6 = ((f32[32,1,1280]{2,1,0:T(1,128)}), f32[32,1,1280]{2,1,0:T(1,128)S(1)}, u32[]{:S(2)}, u32[]{:S(2)}) async-start(f32[32,1,1280]{2,1,0:T(1,128)} %broadcast_in_dim.43), calls=%async_computation.6 | async-start | bytes 327680 | tf_op jit(solution)/shard_map/all_to_all | solution.py:1326
  217.9 183.1 %copy-start.39 = (f32[32]{0:T(128)}, f32[32]{0:T(128)S(1)}, u32[]{:S(2)}) copy-start(f32[32]{0:T(128)S(1)} %get-tuple-element.204) | copy-start | bytes 388
  227.3 190.7 %copy-start.36 = (f32[32]{0:T(128)}, f32[32]{0:T(128)S(1)}, u32[]{:S(2)}) copy-start(f32[32]{0:T(128)S(1)} %get-tuple-element.253) | copy-start | bytes 388
  227.3 210.0 %copy-start.22 = (f32[32]{0:T(128)}, f32[32]{0:T(128)S(1)}, u32[]{:S(2)}) copy-start(f32[32]{0:T(128)S(1)} %get-tuple-element.254) | copy-start | bytes 388
  228.7 191.7 %copy-start.26 = (f32[512]{0:T(512)}, f32[512]{0:T(512)S(1)}, u32[]{:S(2)}) copy-start(f32[512]{0:T(512)S(1)} %get-tuple-element.251) | copy-start | bytes 6148
  228.7 191.7 %copy-start.27 = (f32[512]{0:T(512)}, f32[512]{0:T(512)S(1)}, u32[]{:S(2)}) copy-start(f32[512]{0:T(512)S(1)} %get-tuple-element.252) | copy-start | bytes 6148
  233.9 9.8 %all-to-all-start.7 = ((f32[32,1,256]{2,1,0:T(1,128)}), f32[32,1,256]{2,1,0:T(1,128)S(1)}, u32[]{:S(2)}, u32[]{:S(2)}) async-start(f32[32,1,256]{2,1,0:T(1,128)} %get-tuple-element.125), calls=%async_computation.7 | async-start | bytes 65536 | tf_op jit(solution)/shard_map/all_to_all | solution.py:1340
  248.3 9.8 %all-to-all-start.8 = ((f32[32,1,256]{2,1,0:T(1,128)}), f32[32,1,256]{2,1,0:T(1,128)S(1)}, u32[]{:S(2)}, u32[]{:S(2)}) async-start(f32[32,1,256]{2,1,0:T(1,128)} %get-tuple-element.128), calls=%async_computation.8 | async-start | bytes 65536 | tf_op jit(solution)/shard_map/all_to_all | solution.py:1340
  284.4 1.2 collective-permute-start.3
  296.9 1.2 collective-permute-start.4
  316.3 1.3 collective-permute-start.5
  318.2 11.7 %all-to-all-start.11 = ((f32[16,1,2048]{2,1,0:T(1,128)}), f32[16,1,2048]{2,1,0:T(1,128)S(1)}, u32[]{:S(2)}, u32[]{:S(2)}) async-start(f32[16,1,2048]{2,1,0:T(1,128)} %broadcast_in_dim.45), calls=%async_computation.11 | async-start | bytes 262144 | tf_op jit(solution)/shard_map/all_to_all | solution.py:1333
  330.1 1.2 collective-permute-start.6
  346.3 9.8 %all-to-all-start.12 = ((f32[32,1,256]{2,1,0:T(1,128)}), f32[32,1,256]{2,1,0:T(1,128)S(1)}, u32[]{:S(2)}, u32[]{:S(2)}) async-start(f32[32,1,256]{2,1,0:T(1,128)} %get-tuple-element.141), calls=%async_computation.12 | async-start | bytes 65536 | tf_op jit(solution)/shard_map/all_to_all | solution.py:1340
  362.8 10.5 %all-to-all-start.13 = ((f32[32,1,256]{2,1,0:T(1,128)}), f32[32,1,256]{2,1,0:T(1,128)S(1)}, u32[]{:S(2)}, u32[]{:S(2)}) async-start(f32[32,1,256]{2,1,0:T(1,128)} %get-tuple-element.143), calls=%async_computation.13 | async-start | bytes 65536 | tf_op jit(solution)/shard_map/all_to_all | solution.py:1340
  380.0 13.3 %all-to-all-start.14 = ((f32[32,1,256]{2,1,0:T(1,128)}), f32[32,1,256]{2,1,0:T(1,128)S(1)}, u32[]{:S(2)}, u32[]{:S(2)}) async-start(f32[32,1,256]{2,1,0:T(1,128)} %get-tuple-element.145), calls=%async_computation.14 | async-start | bytes 65536 | tf_op jit(solution)/shard_map/all_to_all | solution.py:1340
  402.1 14.0 %all-to-all-start.15 = ((f32[32,1,1280]{2,1,0:T(1,128)}), f32[32,1,1280]{2,1,0:T(1,128)S(1)}, u32[]{:S(2)}, u32[]{:S(2)}) async-start(f32[32,1,1280]{2,1,0:T(1,128)} %broadcast_in_dim.47), calls=%async_computation.15 | async-start | bytes 327680 | tf_op jit(solution)/shard_map/all_to_all | solution.py:1326
  407.2 59.0 %reduce-scatter.6.cloned.1.call-start = ((), (), s32[]{:S(2)}) async-start(), calls=%async_computation.27 | async-start | bytes 3538944 | tf_op jit(solution)/shard_map/reduce_scatter | solution.py:1758
  421.8 15.6 %copy-start.4 = (f32[9,32,32]{2,1,0:T(8,128)S(1)}, f32[9,32,32]{2,1,0:T(8,128)}, u32[]{:S(2)}) copy-start(f32[9,32,32]{2,1,0:T(8,128)} %get-tuple-element.121) | copy-start | bytes 110596
  421.8 15.7 %copy-start.23 = (f32[3,8,128]{2,1,0:T(8,128)S(1)}, f32[3,8,128]{2,1,0:T(8,128)}, u32[]{:S(2)}) copy-start(f32[3,8,128]{2,1,0:T(8,128)} %get-tuple-element.168) | copy-start | bytes 36868
  421.8 15.7 %copy-start.24 = (f32[3,8,128]{2,1,0:T(8,128)S(1)}, f32[3,8,128]{2,1,0:T(8,128)}, u32[]{:S(2)}) copy-start(f32[3,8,128]{2,1,0:T(8,128)} %get-tuple-element.167) | copy-start | bytes 36868
  421.8 15.7 %copy-start.25 = (f32[3,8,128]{2,1,0:T(8,128)S(1)}, f32[3,8,128]{2,1,0:T(8,128)}, u32[]{:S(2)}) copy-start(f32[3,8,128]{2,1,0:T(8,128)} %get-tuple-element.166) | copy-start | bytes 36868
  431.3 14.4 %all-to-all-start.16 = ((f32[32,1,1024]{2,1,0:T(1,128)}), f32[32,1,1024]{2,1,0:T(1,128)S(1)}, u32[]{:S(2)}, u32[]{:S(2)}) async-start(f32[32,1,1024]{2,1,0:T(1,128)} %get-tuple-element.161), calls=%async_computation.16 | async-start | bytes 262144 | tf_op jit(solution)/shard_map/all_to_all | solution.py:1340
  467.4 1.2 collective-permute-start.7
  469.5 13.7 %all-to-all-start.17 = ((f32[16,1,3840]{2,1,0:T(1,128)}), f32[16,1,3840]{2,1,0:T(1,128)S(1)}, u32[]{:S(2)}, u32[]{:S(2)}) async-start(f32[16,1,3840]{2,1,0:T(1,128)} %broadcast_in_dim.50), calls=%async_computation.18 | async-start | bytes 491520 | tf_op jit(solution)/shard_map/all_to_all | solution.py:1333
  473.2 63.3 %reduce-scatter.8.cloned.1.call-start = ((), (), s32[]{:S(2)}) async-start(), calls=%async_computation.28 | async-start | bytes 491520 | tf_op jit(solution)/shard_map/reduce_scatter | solution.py:1821
  473.8 66.9 %reduce-scatter.10.cloned.1.call-start = ((), (), s32[]{:S(2)}) async-start(), calls=%async_computation.29 | async-start | bytes 2359296 | tf_op jit(solution)/shard_map/reduce_scatter | solution.py:1838
  483.3 8.7 %collective-permute-start.8 = (f32[3840]{0:T(1024)S(1)}, f32[3840]{0:T(1024)S(1)}, u32[]{:S(2)}, u32[]{:S(2)}) collective-permute-start(f32[3840]{0:T(1024)S(1)} %reduce_sum.468), channel_id=1, source_target_pairs={{0,1},{1,0},{2,3},{3,2},{4,5},{5,4},{6,7},{7,6},{8,9},{9,8},{10,11... | collective-permute-start | bytes 46088 | tf_op jit(solution)/shard_map/ppermute | solution.py:1334
  513.4 23.0 %all-to-all-start.18 = ((f32[32,1,1024]{2,1,0:T(1,128)}), f32[32,1,1024]{2,1,0:T(1,128)S(1)}, u32[]{:S(2)}, u32[]{:S(2)}) async-start(f32[32,1,1024]{2,1,0:T(1,128)} %get-tuple-element.172), calls=%async_computation.19 | async-start | bytes 262144 | tf_op jit(solution)/shard_map/all_to_all | solution.py:1340
  516.0 92.7 %reduce-scatter.12.cloned.1.call-start = ((), (), s32[]{:S(2)}) async-start(), calls=%async_computation.30 | async-start | bytes 7077888 | tf_op jit(solution)/shard_map/reduce_scatter | solution.py:1879
  563.2 4.7 collective-permute-start.9
  570.9 35.8 %collective-permute-start.10 = (bf16[2,4,144,512]{3,2,1,0:T(8,128)(2,1)S(1)}, bf16[2,4,144,512]{3,2,1,0:T(8,128)(2,1)}, u32[]{:S(2)}, u32[]{:S(2)}) collective-permute-start(bf16[2,4,144,512]{3,2,1,0:T(8,128)(2,1)S(1)} %dynamic-slice_bitcast_fusion.1), channel_id=1, source_target_pairs={{0,8},{8,0},{16,24},{24,16},{1,9},{9,1},{17,25},{25,17},{2,10},{10... | collective-permute-start | bytes 3538952 | tf_op jit(solution)/shard_map/ppermute | solution.py:1393
  572.8 23.9 %copy-start = (bf16[49,32,512]{2,1,0:T(8,128)(2,1)S(1)}, bf16[49,32,512]{2,1,0:T(8,128)(2,1)}, u32[]{:S(2)}) copy-start(bf16[49,32,512]{2,1,0:T(8,128)(2,1)} %get-tuple-element.120.refs_0_.refs_10_) | copy-start | bytes 4816900
  572.8 23.9 %copy-start.5 = (bf16[49,32,32]{2,1,0:T(8,128)(2,1)S(1)}, bf16[49,32,32]{2,1,0:T(8,128)(2,1)}, u32[]{:S(2)}) copy-start(bf16[49,32,32]{2,1,0:T(8,128)(2,1)} %get-tuple-element.192) | copy-start | bytes 301060
  592.0 12.6 %all-to-all-start.19 = ((f32[32,1,1024]{2,1,0:T(1,128)}), f32[32,1,1024]{2,1,0:T(1,128)S(1)}, u32[]{:S(2)}, u32[]{:S(2)}) async-start(f32[32,1,1024]{2,1,0:T(1,128)} %get-tuple-element.184), calls=%async_computation.22 | async-start | bytes 262144 | tf_op jit(solution)/shard_map/all_to_all | solution.py:1340
  596.3 83.1 %reduce-scatter.14.cloned.1.call-start = ((), (), s32[]{:S(2)}) async-start(), calls=%async_computation.31 | async-start | bytes 1310720 | tf_op jit(solution)/shard_map/reduce_scatter | solution.py:1906
  608.8 28.3 %collective-permute-start.11 = (bf16[1,4,144,512]{3,2,1,0:T(8,128)(2,1)S(1)}, bf16[1,4,144,512]{3,2,1,0:T(8,128)(2,1)S(1)}, u32[]{:S(2)}, u32[]{:S(2)}) collective-permute-start(bf16[1,4,144,512]{3,2,1,0:T(8,128)(2,1)S(1)} %constant_dynamic-slice_fusion), channel_id=1, source_target_pairs={{0,16},{8,24},{16,0},{24,8},{1,17},{9,25},{17,1},{25,9},{2,18},{10... | collective-permute-start | bytes 1769480 | tf_op jit(solution)/shard_map/ppermute | solution.py:1393
  625.8 12.6 %copy-start.3 = (bf16[768,512]{1,0:T(8,128)(2,1)S(1)}, bf16[768,512]{1,0:T(8,128)(2,1)}, u32[]{:S(2)}) copy-start(bf16[768,512]{1,0:T(8,128)(2,1)} %reduce-scatter.12.cloned.1.call-done) | copy-start | bytes 2359300
  625.8 12.6 %copy-start.9 = (bf16[256,512]{1,0:T(8,128)(2,1)S(1)}, bf16[256,512]{1,0:T(8,128)(2,1)}, u32[]{:S(2)}) copy-start(bf16[256,512]{1,0:T(8,128)(2,1)} %reduce-scatter.10.cloned.1.call-done) | copy-start | bytes 786436
  638.4 2.0 collective-permute-start.12
  642.0 19.9 %all-to-all-start.20 = ((bf16[4,280,512]{2,1,0:T(8,128)(2,1)}), bf16[4,280,512]{2,1,0:T(8,128)(2,1)S(1)}, u32[]{:S(2)}, u32[]{:S(2)}) async-start(bf16[4,280,512]{2,1,0:T(8,128)(2,1)} %pad_maximum_fusion), calls=%async_computation.24 | async-start | bytes 2293760 | tf_op jit(solution)/shard_map/all_to_all | solution.py:1399
  662.9 20.4 %all-to-all-start.21 = ((bf16[4,34,512]{2,1,0:T(8,128)(2,1)}), bf16[4,34,512]{2,1,0:T(8,128)(2,1)S(1)}, u32[]{:S(2)}, u32[]{:S(2)}) async-start(bf16[4,34,512]{2,1,0:T(8,128)(2,1)} %reshape.592), calls=%async_computation.25 | async-start | bytes 327680 | tf_op jit(solution)/shard_map/all_to_all | solution.py:1404
  (29 other events, 218.0 us)
Sparse Core Ops, SparseCore 0:
  12.0 101.0 all-gather.5
  116.5 61.1 all-gather.7
  416.3 47.8 reduce-scatter.5
  476.1 21.8 reduce-scatter.7
  501.2 39.4 reduce-scatter.9
  544.2 63.1 reduce-scatter.11
  639.6 26.3 reduce-scatter.13

commit v4 on v3

--- a/solution.py
+++ b/solution.py
@@ -1499,10 +1499,9 @@
         array = value if aligned else jnp.concatenate(flat)[None]
         return [Packed(array, *place) for place in places]
 
-    project1, expand1, reduce2, spatial1 = gather_packed(
+    project1, expand1, spatial1 = gather_packed(
         (columns_of(w_project1), rowsp, blocks),
         (columns_of(w_expand1), rows1, blocks),
-        (w_reduce2, rows2, 1),
         (w_spatial1.reshape(-1, middle), own, 1),
     )
     taps1 = [Packed(spatial1.array, spatial1.rows, spatial1.first + t, 1) for t in range(9)]
@@ -1510,10 +1509,12 @@
         [w_spatial2.reshape(1, -1), w_motion_in.reshape(1, -1), w_motion_out.reshape(1, -1)], axis=1
     )
     rowse = w_expand2.shape[0]
-    late_rows = columns_of(w_expand2).shape[0]
+    late_rows = rows2 + columns_of(w_expand2).shape[0]
     smalls = rows_of(smalls)[0]
-    expand2, tail = gather_packed(
-        (columns_of(w_expand2), rowse, blocks), (smalls, 1, smalls.shape[0])
+    reduce2, expand2, tail = gather_packed(
+        (w_reduce2, rows2, 1),
+        (columns_of(w_expand2), rowse, blocks),
+        (smalls, 1, smalls.shape[0]),
     )
     if aligned:
         flat_small = tail.array[:, late_rows:].reshape(devices, -1)
@@ -1865,9 +1866,10 @@
             axis=2,
         )
     shifts[1], spreads[1] = sums.ready(sums_strided, 2)
-    shifts[1], spreads[1], packed_b, mine_a, mine_r = lax.optimization_barrier(
-        (shifts[1], spreads[1], packed_b, mine_a, mine_r)
-    )
+    shifts[1], spreads[1], packed_b, mine_a = lax.optimization_barrier(
+        (shifts[1], spreads[1], packed_b, mine_a)
+    )
+    packed_b, mine_r = lax.optimization_barrier((packed_b, mine_r))
 
     def columns_back(value, rows):
         return value.reshape(blocks, rows, middle).swapaxes(0, 1).reshape(rows, wide)

time: 705 us -> 702 us (level)
  blocking collectives: 41.9 us -> 54.2 us
  waiting for transfers between devices: 129 us -> 117 us
    all_to_all x0 -> x1, blocking collectives: none -> 12.3 us  [quick_gather(): lax.all_to_all(jnp.broadcast_to(value[None], (dp,) + value.shape), 'dp',...]
    all_gather x2, waiting for transfers between devices: 29.5 us -> 19.6 us  [gather(): return lax.all_gather(value, AXES, axis=0, tiled=False)]
  transfers between devices with their start and end apart: 39 -> 38, of which waited for: 25 -> 25; matrix products, arithmetic and copies ran while one was open for 11% -> 11% of each run, Pallas kernels for 36% -> 34%
where the time goes in v4:
time: 702 us; the launch traced here: 690 us
  Pallas kernels  321 us (46%)
  waiting for transfers between devices  117 us (17%)
  starting transfers between devices  71.5 us (10%)
  blocking collectives  54.2 us (8%)
  local copies, waits for them, and re-layouts  52.9 us (8%)
  other arithmetic  49.7 us (7%)
  between operations  17.9 us (3%)
    pallas_call x25, Pallas kernels, call(): pl.pallas_call(body, grid=grid, in_specs=[spec(b) for b in in_blocks], ou...  261 us
    all_to_all x10, waiting for transfers between devices, ready(): total = jnp.sum(lax.all_to_all(copies, AXES, 0, 0, tiled=True), axis=(0, 1))  39.7 us
    all_to_all x10, starting transfers between devices, ready(): total = jnp.sum(lax.all_to_all(copies, AXES, 0, 0, tiled=True), axis=(0, 1))  36.7 us
    pallas_call x4, Pallas kernels, kernel_weight_grad(): pl.pallas_call(body, grid=(columns // middle,), in_specs=in_specs, out_sp...  36.6 us
    all_to_all x2, blocking collectives, flat(): lax.all_to_all(copies, AXES, 0, 0, axis_index_groups=self.groups)  32.2 us
    pallas_call x2, Pallas kernels, kernel_grad_features(): pl.pallas_call(body, grid=(parts,), in_specs=in_specs, out_specs=pl.Block...  24.1 us
    all_gather x2, waiting for transfers between devices, gather(): return lax.all_gather(value, AXES, axis=0, tiled=False)  19.6 us
  transfers between devices with their start and end apart: 38, of which 25 were waited for; matrix products, arithmetic and copies ran while one was open for 11% of the time, Pallas kernels for 34%

profile of v4, /device:TPU:0, one launch (start us, length us, event | category | flops | bytes accessed | tf_op | source)
XLA Modules:
  0.0 690.2 jit_solution(736082050965622286)
XLA Ops:
  14.4 12.3 %all_to_all.117 = bf16[4,32,512]{2,1,0:T(8,128)(2,1)S(1)} all-to-all(bf16[4,32,512]{2,1,0:T(8,128)(2,1)S(1)} %broadcast_in_dim.34), channel_id=1, replica_groups=mesh['dp'=4,'fsdp'=8] {'dp'}, dimensions={0} | all-to-all | bytes 262144 | tf_op jit(solution)/shard_map/all_to_all | solution.py:1366
  27.5 3.7 all-to-all-start.1
  32.0 5.8 all-to-all-done.1
  41.7 16.6 %shard_map.298 = (bf16[14,14,32,512]{3,2,1,0:T(8,128)(2,1)}, f32[8,512]{1,0:T(8,128)}, f32[2,8,512]{2,1,0:T(8,128)}) custom-call(bf16[4,1568,1024]{2,1,0:T(8,128)(2,1)} %bitcast.304, bf16[1024,512]{1,0:T(8,128)(2,1)} %bitcast.313, f32[32,256]{1,0:T(8,128)} %broadcast_in_dim.37.m_ref.refs_4_.refs_5_.refs_7_), custom_call_target="tpu_custom_call" | custom-call | flops 6576668672 | bytes 19267584 | tf_op jit(solution)/shard_map/pallas_call | solution.py:75
  61.2 3.5 all-to-all-start.2
  70.2 6.1 all-to-all-done.2
  79.4 9.1 %shard_map.299.a_ref = bf16[14,14,32,512]{3,2,1,0:T(8,128)(2,1)} custom-call(bf16[14,14,32,512]{3,2,1,0:T(8,128)(2,1)} %get-tuple-element.108.a_ref, f32[2,512]{1,0:T(2,128)} %pad_maximum_fusion.18.s_ref, f32[32,256]{1,0:T(8,128)} %broadcast_in_dim.37.m_ref.refs_4_.refs_5_.refs_7_), custom_call_target="tpu_custom_call" | custom-call | flops 32112640 | bytes 19267584 | tf_op jit(solution)/shard_map/pallas_call | solution.py:75
  88.5 16.4 %all-gather.6.cloned.1.call-done = bf16[10752,512]{1,0:T(8,128)(2,1)} async-done(((bf16[336,512]{1,0:T(8,128)(2,1)}), bf16[10752,512]{1,0:T(8,128)(2,1)}) %all-gather.6.cloned.1.call-update) | async-done | bytes 11010064 | tf_op jit(solution)/shard_map/all_gather | solution.py:1474
  104.9 13.5 %shard_map.300 = (f32[7,7,32,512]{3,2,1,0:T(8,128)}, f32[32,1,1024]{2,1,0:T(1,128)}) custom-call(bf16[14,14,32,512]{3,2,1,0:T(8,128)(2,1)} %shard_map.299.a_ref, f32[32,256]{1,0:T(8,128)} %broadcast_in_dim.37.m_ref.refs_4_.refs_5_.refs_7_, bf16[32,336,512]{2,1,0:T(8,128)(2,1)} %bitcast.276, bf16[32,336,512]{2,1,0:T(8,128)(2,1)} %bitcast.277, ...), custom_call_target="tpu_custom_call" | custom-call | flops 7398752256 | bytes 11141120 | tf_op jit(solution)/shard_map/pallas_call | solution.py:75
  121.3 11.9 %shard_map.302 = (bf16[49,32,2048]{2,1,0:T(8,128)(2,1)}, f32[8,2048]{1,0:T(8,128)}, f32[2,8,2048]{2,1,0:T(8,128)}) custom-call(bf16[49,32,1024]{2,1,0:T(8,128)(2,1)} %bitcast.326, f32[32,256]{1,0:T(8,128)} %broadcast_in_dim.37.m_ref.refs_4_.refs_5_.refs_7_, bf16[32,336,512]{2,1,0:T(8,128)(2,1)} %bitcast.285), custom_call_target="tpu_custom_call" | custom-call | flops 6576668672 | bytes 9633792 | tf_op jit(solution)/shard_map/pallas_call | solution.py:75
  135.5 10.6 %shard_map.301 = (bf16[49,32,512]{2,1,0:T(8,128)(2,1)}, bf16[49,32,2048]{2,1,0:T(8,128)(2,1)}, f32[8,2048]{1,0:T(8,128)}, f32[2,8,2048]{2,1,0:T(8,128)}) custom-call(f32[49,32,512]{2,1,0:T(8,128)} %bitcast.307, f32[2,512]{1,0:T(2,128)} %pad_maximum_fusion.19.s_ref, f32[32,256]{1,0:T(8,128)} %broadcast_in_dim.37.m_ref.refs_4_.refs_5_.refs_7_, ...), custom_call_target="tpu_custom_call" | custom-call | flops 3288334336 | bytes 17661952 | tf_op jit(solution)/shard_map/pallas_call | solution.py:75
  148.7 21.1 %all_to_all.118 = f32[16,1,4096]{2,1,0:T(1,128)S(1)} all-to-all(f32[16,1,4096]{2,1,0:T(1,128)S(1)} %broadcast_in_dim.40), channel_id=1, replica_groups={{0,2,4,6,8,10,12,14,16,18,20,22,24,26,28,30},{1,3,5,7,9,11,13,15,17,19,..., dimensions={0} | all-to-all | bytes 524288 | tf_op jit(solution)/shard_map/all_to_all | solution.py:1333
  173.1 3.2 all-gather.8.cloned.1.call-done.w_ref
  176.3 13.2 %shard_map.303 = (bf16[49,32,2048]{2,1,0:T(8,128)(2,1)}, f32[49,32,512]{2,1,0:T(8,128)}, f32[32,1,1024]{2,1,0:T(1,128)}) custom-call(bf16[49,32,2048]{2,1,0:T(8,128)(2,1)} %get-tuple-element.113.c_ref, bf16[49,32,2048]{2,1,0:T(8,128)(2,1)} %get-tuple-element.114.p_ref, f32[8,2048]{1,0:T(8,128)} %stack.299.s_ref, ...), custom_call_target="tpu_custom_call" | custom-call | flops 3288334336 | bytes 32112640 | tf_op jit(solution)/shard_map/pallas_call | solution.py:75
  189.5 3.9 all-to-all-start.5
  195.0 6.7 all-to-all-done.5
  203.0 4.6 shard_map.304
  217.1 6.3 all-to-all-done.6
  226.8 4.3 shard_map.305
  234.8 6.2 all-to-all-done.7
  241.7 3.7 shard_map.306
  249.1 6.2 all-to-all-done.8
  256.0 3.7 shard_map.307
  259.7 9.8 %all_to_all.119 = f32[32,1,256]{2,1,0:T(1,128)S(1)} all-to-all(f32[32,1,256]{2,1,0:T(1,128)} %get-tuple-element.132), channel_id=1, replica_groups=mesh['dp'=4,'fsdp'=8] {'dp','fsdp'}, dimensions={0} | all-to-all | bytes 65536 | tf_op jit(solution)/shard_map/all_to_all | solution.py:1340
  270.3 10.3 %shard_map.308 = (bf16[49,32,512]{2,1,0:T(8,128)(2,1)}, bf16[49,32,2048]{2,1,0:T(8,128)(2,1)}, f32[8,2048]{1,0:T(8,128)}, f32[2,8,2048]{2,1,0:T(8,128)}) custom-call(bf16[49,32,512]{2,1,0:T(8,128)(2,1)} %get-tuple-element.124.refs_0_.x_ref.refs_5_, bf16[49,32,128]{2,1,0:T(8,128)(2,1)} %get-tuple-element.127.o1.refs_8_, ...), custom_call_target="tpu_custom_call" | custom-call | flops 3288334336 | bytes 16056320 | tf_op jit(solution)/shard_map/pallas_call | solution.py:75
  282.9 11.1 %all_to_all.120 = f32[16,1,2048]{2,1,0:T(1,128)S(1)} all-to-all(f32[16,1,2048]{2,1,0:T(1,128)S(1)} %broadcast_in_dim.44), channel_id=1, replica_groups={{0,2,4,6,8,10,12,14,16,18,20,22,24,26,28,30},{1,3,5,7,9,11,13,15,17,19,..., dimensions={0} | all-to-all | bytes 262144 | tf_op jit(solution)/shard_map/all_to_all | solution.py:1333
  296.0 16.4 %shard_map.309 = (bf16[4,7,7,8,2048]{4,3,2,1,0:T(8,128)(2,1)}, bf16[49,32,2048]{2,1,0:T(8,128)(2,1)}, f32[2,8,2048]{2,1,0:T(8,128)}) custom-call(bf16[49,32,2048]{2,1,0:T(8,128)(2,1)} %get-tuple-element.133.e_ref, bf16[49,32,2048]{2,1,0:T(8,128)(2,1)} %get-tuple-element.134.o_ref.refs_0_, bf16[4,7,7,8,2048]{4,3,2,1,0:T(8,128)(2,1)} %bitcast.317, ...), custom_call_target="tpu_custom_call" | custom-call | flops 64225280 | bytes 44957696 | tf_op jit(solution)/shard_map/pallas_call | solution.py:75
  315.5 3.5 all-to-all-start.11
  322.5 4.7 all-to-all-done.11
  329.8 14.4 %shard_map.310 = (bf16[49,32,2048]{2,1,0:T(8,128)(2,1)}, f32[49,32,512]{2,1,0:T(8,128)}, f32[49,32,128]{2,1,0:T(8,128)}, f32[32,1,256]{2,1,0:T(1,128)}) custom-call(bf16[49,32,2048]{2,1,0:T(8,128)(2,1)} %get-tuple-element.138.g_ref.t_ref, bf16[49,32,2048]{2,1,0:T(8,128)(2,1)} %get-tuple-element.133.e_ref, f32[4,2048]{1,0:T(4,128)} %pad_maximum_fusion.6.s_ref, ...), custom_call_target="tpu_custom_call" | custom-call | flops 3288334336 | bytes 32112640 | tf_op jit(solution)/shard_map/pallas_call | solution.py:75
  347.3 6.7 all-to-all-done.12
  355.2 5.4 shard_map.311
  363.2 7.9 %shard_map.314 = bf16[8,4,64,512]{3,2,1,0:T(8,128)(2,1)} custom-call(bf16[49,32,512]{2,1,0:T(8,128)(2,1)} %get-tuple-element.152.refs_0_, bf16[49,32,2048]{2,1,0:T(8,128)(2,1)} %get-tuple-element.153.refs_1_), custom_call_target="tpu_custom_call" | custom-call | flops 3288334336 | bytes 10125312 | tf_op jit(solution)/shard_map/pallas_call | solution.py:1011
  372.3 5.4 shard_map.312
  377.7 6.0 all-to-all-start.14
  383.8 3.2 shard_map.317
  386.9 3.2 shard_map.316
  392.2 5.5 shard_map.313
  399.8 5.1 all-to-all-start.15
  405.0 3.2 shard_map.315
  410.3 3.6 fusion.2
  419.7 9.5 %shard_map.318 = (f32[49,32,512]{2,1,0:T(8,128)}, bf16[49,32,32]{2,1,0:T(8,128)(2,1)}, f32[32,1,1024]{2,1,0:T(1,128)}) custom-call(f32[49,32,512]{2,1,0:T(8,128)} %get-tuple-element.140.refs_6_.j_ref, f32[49,32,128]{2,1,0:T(8,128)} %get-tuple-element.149.p1, f32[49,32,128]{2,1,0:T(8,128)} %get-tuple-element.147.refs_8_.p2, ...), custom_call_target="tpu_custom_call" | custom-call | flops 51380224 | bytes 9633792 | tf_op jit(solution)/shard_map/pallas_call | solution.py:75
  429.2 6.0 all-to-all-start.16
  435.6 8.0 %all-to-all-done.16 = f32[32,1,1024]{2,1,0:T(1,128)S(1)} async-done(((f32[32,1,1024]{2,1,0:T(1,128)}), f32[32,1,1024]{2,1,0:T(1,128)S(1)}, u32[]{:S(2)}, u32[]{:S(2)}) %all-to-all-start.16) | async-done | bytes 131104 | tf_op jit(solution)/shard_map/all_to_all | solution.py:1340
  444.9 19.1 %shard_map.319 = (bf16[49,32,512]{2,1,0:T(8,128)(2,1)}, bf16[49,32,2048]{2,1,0:T(8,128)(2,1)}, f32[3,8,2048]{2,1,0:T(8,128)}) custom-call(f32[49,32,512]{2,1,0:T(8,128)} %get-tuple-element.161.n_ref, f32[49,32,512]{2,1,0:T(8,128)} %get-tuple-element.119.d_ref, f32[4,512]{1,0:T(4,128)} %pad_maximum_fusion.16.sd_ref, ...), custom_call_target="tpu_custom_call" | custom-call | flops 3288334336 | bytes 51380224 | tf_op jit(solution)/shard_map/pallas_call | solution.py:75
  467.4 3.7 all-to-all-start.17
  471.7 9.3 %all-to-all-done.17 = f32[16,1,3840]{2,1,0:T(1,128)S(1)} async-done(((f32[16,1,3840]{2,1,0:T(1,128)}), f32[16,1,3840]{2,1,0:T(1,128)S(1)}, u32[]{:S(2)}, u32[]{:S(2)}) %all-to-all-start.17) | async-done | bytes 245792 | tf_op jit(solution)/shard_map/all_to_all | solution.py:1333
  481.3 8.7 %shard_map.320 = bf16[8,4,64,512]{3,2,1,0:T(8,128)(2,1)} custom-call(bf16[49,32,2048]{2,1,0:T(8,128)(2,1)} %get-tuple-element.134.o_ref.refs_0_, bf16[49,32,512]{2,1,0:T(8,128)(2,1)} %get-tuple-element.170.refs_1_), custom_call_target="tpu_custom_call" | custom-call | flops 3288334336 | bytes 10125312 | tf_op jit(solution)/shard_map/pallas_call | solution.py:1011
  491.4 20.0 %shard_map.321 = (bf16[49,32,2048]{2,1,0:T(8,128)(2,1)}, bf16[49,32,2048]{2,1,0:T(8,128)(2,1)}, f32[49,32,512]{2,1,0:T(8,128)}, f32[32,1,1024]{2,1,0:T(1,128)}) custom-call(bf16[49,32,2048]{2,1,0:T(8,128)(2,1)} %get-tuple-element.163.g_ref, bf16[49,32,2048]{2,1,0:T(8,128)(2,1)} %get-tuple-element.113.c_ref, bf16[49,32,2048]{2,1,0:T(8,128)(2,1)} %get-tuple-element.114.p_ref, ...), custom_call_target="tpu_custom_call" | custom-call | flops 3288334336 | bytes 51380224 | tf_op jit(solution)/shard_map/pallas_call | solution.py:75
  514.3 8.1 %shard_map.322.refs_2_ = bf16[8,4,192,512]{3,2,1,0:T(8,128)(2,1)} custom-call(bf16[49,32,512]{2,1,0:T(8,128)(2,1)} %get-tuple-element.175.refs_0_, bf16[49,32,2048]{2,1,0:T(8,128)(2,1)} %get-tuple-element.176.refs_1_), custom_call_target="tpu_custom_call" | custom-call | flops 3288334336 | bytes 10125312 | tf_op jit(solution)/shard_map/pallas_call | solution.py:1011
  522.4 11.9 %shard_map.323 = bf16[8,4,192,512]{3,2,1,0:T(8,128)(2,1)} custom-call(bf16[49,32,1024]{2,1,0:T(8,128)(2,1)} %bitcast.327, bf16[49,32,2048]{2,1,0:T(8,128)(2,1)} %get-tuple-element.174.refs_1_.s_ref, bf16[8,4,192,512]{3,2,1,0:T(8,128)(2,1)} %shard_map.322.refs_2_), custom_call_target="tpu_custom_call", output_to_operand_aliasing={{}: (2, {})} | custom-call | flops 6576668672 | bytes 13828096 | tf_op jit(solution)/shard_map/pallas_call | solution.py:1011
  534.5 4.1 reduce-scatter.10.cloned.1.call-done
  539.2 18.9 %shard_map.324 = (bf16[2,4,4,144,512]{4,3,2,1,0:T(8,128)(2,1)}, bf16[49,32,512]{2,1,0:T(8,128)(2,1)}) custom-call(bf16[7,2,7,2,32,512]{5,4,3,2,1,0:T(8,128)(2,1)} %bitcast.302, f32[49,32,512]{2,1,0:T(8,128)} %get-tuple-element.172.n_ref, f32[49,32,512]{2,1,0:T(8,128)} %bitcast.309, f32[4,512]{1,0:T(4,128)} %fusion.52.s_ref, ...), custom_call_target="tpu_custom_call" | custom-call | flops 7398752256 | bytes 19169280 | tf_op jit(solution)/shard_map/pallas_call | solution.py:75
  558.1 3.4 dynamic-slice_bitcast_fusion
  562.2 4.1 collective-permute-done.9
  570.7 19.2 %shard_map.325 = (bf16[7,2,7,2,32,512]{5,4,3,2,1,0:T(8,128)(2,1)}, f32[32,1,1024]{2,1,0:T(1,128)}) custom-call(bf16[7,7,32,512]{3,2,1,0:T(8,128)(2,1)} %bitcast.319, bf16[7,7,32,512]{3,2,1,0:T(8,128)(2,1)} %bitcast.320, bf16[7,2,7,2,32,512]{5,4,3,2,1,0:T(8,128)(2,1)} %bitcast.299, f32[4,512]{1,0:T(4,128)} %fusion.46.s_ref, ...), custom_call_target="tpu_custom_call" | custom-call | flops 7398752256 | bytes 30408704 | tf_op jit(solution)/shard_map/pallas_call | solution.py:75
  590.0 4.8 all-to-all-start.19
  598.1 5.1 all-to-all-done.19
  607.9 15.9 %shard_map.326 = (bf16[4,1568,512]{2,1,0:T(8,128)(2,1)}, bf16[1024,512]{1,0:T(8,128)(2,1)}) custom-call(bf16[14,14,32,512]{3,2,1,0:T(8,128)(2,1)} %bitcast.318, bf16[14,14,32,512]{3,2,1,0:T(8,128)(2,1)} %get-tuple-element.108.a_ref, bf16[4,1568,1024]{2,1,0:T(8,128)(2,1)} %bitcast.306, f32[4,512]{1,0:T(4,128)} %fusion.48.s_ref, ...), custom_call_target="tpu_custom_call" | custom-call | flops 6576668672 | bytes 32112640 | tf_op jit(solution)/shard_map/pallas_call | solution.py:75
  623.8 11.2 %collective-permute-done.11 = bf16[1,4,144,512]{3,2,1,0:T(8,128)(2,1)S(1)} collective-permute-done((bf16[1,4,144,512]{3,2,1,0:T(8,128)(2,1)S(1)}, bf16[1,4,144,512]{3,2,1,0:T(8,128)(2,1)S(1)}, u32[]{:S(2)}, u32[]{:S(2)}) %collective-permute-start.11) | collective-permute-done | bytes 589856 | tf_op jit(solution)/shard_map/ppermute | solution.py:1393
  639.9 3.5 all-to-all-start.20
  647.7 12.1 %shard_map.327.refs_0_ = bf16[4,1568,1024]{2,1,0:T(8,128)(2,1)} custom-call(bf16[4,1568,512]{2,1,0:T(8,128)(2,1)} %get-tuple-element.190.g_ref, bf16[1024,512]{1,0:T(8,128)(2,1)} %bitcast.314, bf16[49,32,2048]{2,1,0:T(8,128)(2,1)} %get-tuple-element.174.refs_1_.s_ref, bf16[32,336,512]{2,1,0:T(8,128)(2,1)} %bitcast.297), custom_call_target="tpu_custom_call" | custom-call | flops 6576668672 | bytes 12845056 | tf_op jit(solution)/shard_map/pallas_call | solution.py:508
  660.8 3.6 all-to-all-start.21
  665.2 12.0 %shard_map.328 = bf16[4,1568,1024]{2,1,0:T(8,128)(2,1)} custom-call(bf16[4,1568,512]{2,1,0:T(8,128)(2,1)} %get-tuple-element.190.g_ref, bf16[1024,512]{1,0:T(8,128)(2,1)} %bitcast.315, bf16[49,32,2048]{2,1,0:T(8,128)(2,1)} %get-tuple-element.174.refs_1_.s_ref, bf16[32,336,512]{2,1,0:T(8,128)(2,1)} %bitcast.298, ...), custom_call_target="tpu_custom_call", output_to_operand_aliasing={{}: (4, {})} | custom-call | flops 6576668672 | bytes 12845056 | tf_op jit(solution)/shard_map/pallas_call | solution.py:508
  (444 shorter events, 132.3 us)
Async XLA Ops:
  7.2 97.7 %all-gather.6.cloned.1.call-start = ((), (), s32[]{:S(2)}) async-start(), calls=%async_computation.32 | async-start | bytes 11354112 | tf_op jit(solution)/shard_map/all_gather | solution.py:1474
  9.2 22.8 %copy-start.64 = (s32[4,8]{1,0:T(4,128)S(1)}, s32[4,8]{1,0:T(4,128)}, u32[]{:S(2)}) copy-start(s32[4,8]{1,0:T(4,128)} %param.21) | copy-start | bytes 388
  9.2 22.8 %copy-start.68 = (s32[4]{0:T(128)S(1)}, s32[4]{0:T(128)}, u32[]{:S(2)}) copy-start(s32[4]{0:T(128)} %param.20) | copy-start | bytes 52
  11.0 165.3 %all-gather.8.cloned.1.call-start = ((), (), s32[]{:S(2)}) async-start(), calls=%async_computation.33 | async-start | bytes 5406720 | tf_op jit(solution)/shard_map/all_gather | solution.py:1474
  27.5 10.3 %all-to-all-start.1 = ((bf16[4,4,32,512]{3,2,1,0:T(8,128)(2,1)}), bf16[4,4,32,512]{3,2,1,0:T(8,128)(2,1)S(1)}, u32[]{:S(2)}, u32[]{:S(2)}) async-start(bf16[4,4,32,512]{3,2,1,0:T(8,128)(2,1)} %broadcast_in_dim.35), calls=%async_computation.1 | async-start | bytes 1048576 | tf_op jit(solution)/shard_map/all_to_all | solution.py:1367
  32.0 193.8 %copy-start.65 = (f32[4,8]{1,0:T(4,128)}, f32[4,8]{1,0:T(4,128)S(1)}, u32[]{:S(2)}) copy-start(f32[4,8]{1,0:T(4,128)S(1)} %get-tuple-element.249) | copy-start | bytes 388
  37.9 1.9 collective-permute-start
  39.2 170.9 %copy-start.20 = (f32[4,7]{1,0:T(4,128)}, f32[4,7]{1,0:T(4,128)S(1)}, u32[]{:S(2)}) copy-start(f32[4,7]{1,0:T(4,128)S(1)} %get-tuple-element.343) | copy-start | bytes 340
  61.2 15.0 %all-to-all-start.2 = ((f32[32,1,1280]{2,1,0:T(1,128)}), f32[32,1,1280]{2,1,0:T(1,128)S(1)}, u32[]{:S(2)}, u32[]{:S(2)}) async-start(f32[32,1,1280]{2,1,0:T(1,128)} %broadcast_in_dim.39), calls=%async_computation.2 | async-start | bytes 327680 | tf_op jit(solution)/shard_map/all_to_all | solution.py:1326
  118.4 15.8 %all-to-all-start.3 = ((f32[32,1,1024]{2,1,0:T(1,128)}), f32[32,1,1024]{2,1,0:T(1,128)S(1)}, u32[]{:S(2)}, u32[]{:S(2)}) async-start(f32[32,1,1024]{2,1,0:T(1,128)} %get-tuple-element.112), calls=%async_computation.3 | async-start | bytes 262144 | tf_op jit(solution)/shard_map/all_to_all | solution.py:1340
  135.5 34.4 %copy-start.50 = (f32[3,3,128]{2,1,0:T(4,128)S(1)}, f32[3,3,128]{2,1,0:T(4,128)}, u32[]{:S(2)}) copy-start(f32[3,3,128]{2,1,0:T(4,128)} %param.35) | copy-start | bytes 13828
  147.2 1.2 collective-permute-start.1
  169.9 2.4 collective-permute-start.2
  189.5 12.1 %all-to-all-start.5 = ((f32[32,1,1024]{2,1,0:T(1,128)}), f32[32,1,1024]{2,1,0:T(1,128)S(1)}, u32[]{:S(2)}, u32[]{:S(2)}) async-start(f32[32,1,1024]{2,1,0:T(1,128)} %get-tuple-element.120), calls=%async_computation.5 | async-start | bytes 262144 | tf_op jit(solution)/shard_map/all_to_all | solution.py:1340
  193.5 32.3 %copy-start.48 = (f32[4,8]{1,0:T(4,128)}, f32[4,8]{1,0:T(4,128)S(1)}, u32[]{:S(2)}) copy-start(f32[4,8]{1,0:T(4,128)S(1)} %get-tuple-element.342) | copy-start | bytes 388
  193.5 32.3 %copy-start.62 = (f32[4,8]{1,0:T(4,128)}, f32[4,8]{1,0:T(4,128)S(1)}, u32[]{:S(2)}) copy-start(f32[4,8]{1,0:T(4,128)S(1)} %get-tuple-element.341) | copy-start | bytes 388
  194.1 15.2 %copy-start.17 = (f32[9,32]{1,0:T(8,128)S(1)}, f32[9,32]{1,0:T(8,128)}, u32[]{:S(2)}) copy-start(f32[9,32]{1,0:T(8,128)} %param.34) | copy-start | bytes 3460
  195.0 19.9 %copy-start.12 = (f32[7,7,9]{1,2,0:T(8,128)S(1)}, f32[7,7,9]{1,2,0:T(8,128)}, u32[]{:S(2)}) copy-start(f32[7,7,9]{1,2,0:T(8,128)} %constant.124.clone) | copy-start | bytes 5296
  211.1 14.8 %copy-start.33 = (f32[4,8,32]{2,1,0:T(8,128)}, f32[4,8,32]{2,1,0:T(8,128)S(1)}, u32[]{:S(2)}) copy-start(f32[4,8,32]{2,1,0:T(8,128)S(1)} %get-tuple-element.258) | copy-start | bytes 12292
  212.3 11.2 %all-to-all-start.6 = ((f32[32,1,1280]{2,1,0:T(1,128)}), f32[32,1,1280]{2,1,0:T(1,128)S(1)}, u32[]{:S(2)}, u32[]{:S(2)}) async-start(f32[32,1,1280]{2,1,0:T(1,128)} %broadcast_in_dim.43), calls=%async_computation.6 | async-start | bytes 327680 | tf_op jit(solution)/shard_map/all_to_all | solution.py:1326
  224.4 191.4 %copy-start.51 = (f32[32]{0:T(128)}, f32[32]{0:T(128)S(1)}, u32[]{:S(2)}) copy-start(f32[32]{0:T(128)S(1)} %get-tuple-element.255) | copy-start | bytes 388
  224.4 210.8 %copy-start.35 = (f32[32]{0:T(128)}, f32[32]{0:T(128)S(1)}, u32[]{:S(2)}) copy-start(f32[32]{0:T(128)S(1)} %get-tuple-element.256) | copy-start | bytes 388
  225.8 192.4 %copy-start.18 = (f32[512]{0:T(512)}, f32[512]{0:T(512)S(1)}, u32[]{:S(2)}) copy-start(f32[512]{0:T(512)S(1)} %get-tuple-element.252) | copy-start | bytes 6148
  225.8 192.4 %copy-start.39 = (f32[512]{0:T(512)}, f32[512]{0:T(512)S(1)}, u32[]{:S(2)}) copy-start(f32[512]{0:T(512)S(1)} %get-tuple-element.253) | copy-start | bytes 6148
  225.8 192.4 %copy-start.40 = (f32[512]{0:T(512)}, f32[512]{0:T(512)S(1)}, u32[]{:S(2)}) copy-start(f32[512]{0:T(512)S(1)} %get-tuple-element.254) | copy-start | bytes 6148
  231.1 9.8 %all-to-all-start.7 = ((f32[32,1,256]{2,1,0:T(1,128)}), f32[32,1,256]{2,1,0:T(1,128)S(1)}, u32[]{:S(2)}, u32[]{:S(2)}) async-start(f32[32,1,256]{2,1,0:T(1,128)} %get-tuple-element.126), calls=%async_computation.7 | async-start | bytes 65536 | tf_op jit(solution)/shard_map/all_to_all | solution.py:1340
  245.4 9.8 %all-to-all-start.8 = ((f32[32,1,256]{2,1,0:T(1,128)}), f32[32,1,256]{2,1,0:T(1,128)S(1)}, u32[]{:S(2)}, u32[]{:S(2)}) async-start(f32[32,1,256]{2,1,0:T(1,128)} %get-tuple-element.129), calls=%async_computation.8 | async-start | bytes 65536 | tf_op jit(solution)/shard_map/all_to_all | solution.py:1340
  281.6 1.2 collective-permute-start.3
  294.1 1.2 collective-permute-start.4
  313.5 1.3 collective-permute-start.5
  315.5 11.7 %all-to-all-start.11 = ((f32[16,1,2048]{2,1,0:T(1,128)}), f32[16,1,2048]{2,1,0:T(1,128)S(1)}, u32[]{:S(2)}, u32[]{:S(2)}) async-start(f32[16,1,2048]{2,1,0:T(1,128)} %broadcast_in_dim.45), calls=%async_computation.11 | async-start | bytes 262144 | tf_op jit(solution)/shard_map/all_to_all | solution.py:1333
  327.3 1.2 collective-permute-start.6
  344.2 9.8 %all-to-all-start.12 = ((f32[32,1,256]{2,1,0:T(1,128)}), f32[32,1,256]{2,1,0:T(1,128)S(1)}, u32[]{:S(2)}, u32[]{:S(2)}) async-start(f32[32,1,256]{2,1,0:T(1,128)} %get-tuple-element.142), calls=%async_computation.12 | async-start | bytes 65536 | tf_op jit(solution)/shard_map/all_to_all | solution.py:1340
  360.6 10.5 %all-to-all-start.13 = ((f32[32,1,256]{2,1,0:T(1,128)}), f32[32,1,256]{2,1,0:T(1,128)S(1)}, u32[]{:S(2)}, u32[]{:S(2)}) async-start(f32[32,1,256]{2,1,0:T(1,128)} %get-tuple-element.144), calls=%async_computation.13 | async-start | bytes 65536 | tf_op jit(solution)/shard_map/all_to_all | solution.py:1340
  377.7 13.3 %all-to-all-start.14 = ((f32[32,1,256]{2,1,0:T(1,128)}), f32[32,1,256]{2,1,0:T(1,128)S(1)}, u32[]{:S(2)}, u32[]{:S(2)}) async-start(f32[32,1,256]{2,1,0:T(1,128)} %get-tuple-element.146), calls=%async_computation.14 | async-start | bytes 65536 | tf_op jit(solution)/shard_map/all_to_all | solution.py:1340
  399.8 14.0 %all-to-all-start.15 = ((f32[32,1,1280]{2,1,0:T(1,128)}), f32[32,1,1280]{2,1,0:T(1,128)S(1)}, u32[]{:S(2)}, u32[]{:S(2)}) async-start(f32[32,1,1280]{2,1,0:T(1,128)} %broadcast_in_dim.47), calls=%async_computation.15 | async-start | bytes 327680 | tf_op jit(solution)/shard_map/all_to_all | solution.py:1326
  404.9 59.1 %reduce-scatter.6.cloned.1.call-start = ((), (), s32[]{:S(2)}) async-start(), calls=%async_computation.27 | async-start | bytes 3538944 | tf_op jit(solution)/shard_map/reduce_scatter | solution.py:1759
  419.7 15.6 %copy-start.4 = (f32[9,32,32]{2,1,0:T(8,128)S(1)}, f32[9,32,32]{2,1,0:T(8,128)}, u32[]{:S(2)}) copy-start(f32[9,32,32]{2,1,0:T(8,128)} %get-tuple-element.122) | copy-start | bytes 110596
  419.7 15.6 %copy-start.21 = (f32[4,7]{1,0:T(4,128)S(1)}, f32[4,7]{1,0:T(4,128)}, u32[]{:S(2)}) copy-start(f32[4,7]{1,0:T(4,128)} %copy-done.20) | copy-start | bytes 340
  419.7 15.7 %copy-start.36 = (f32[3,8,128]{2,1,0:T(8,128)S(1)}, f32[3,8,128]{2,1,0:T(8,128)}, u32[]{:S(2)}) copy-start(f32[3,8,128]{2,1,0:T(8,128)} %get-tuple-element.169) | copy-start | bytes 36868
  419.7 15.7 %copy-start.37 = (f32[3,8,128]{2,1,0:T(8,128)S(1)}, f32[3,8,128]{2,1,0:T(8,128)}, u32[]{:S(2)}) copy-start(f32[3,8,128]{2,1,0:T(8,128)} %get-tuple-element.168) | copy-start | bytes 36868
  419.7 15.7 %copy-start.38 = (f32[3,8,128]{2,1,0:T(8,128)S(1)}, f32[3,8,128]{2,1,0:T(8,128)}, u32[]{:S(2)}) copy-start(f32[3,8,128]{2,1,0:T(8,128)} %get-tuple-element.167) | copy-start | bytes 36868
  419.7 23.9 %copy-start.41 = (f32[512]{0:T(512)S(1)}, f32[512]{0:T(512)}, u32[]{:S(2)}) copy-start(f32[512]{0:T(512)} %get-tuple-element.261) | copy-start | bytes 6148
  429.2 14.4 %all-to-all-start.16 = ((f32[32,1,1024]{2,1,0:T(1,128)}), f32[32,1,1024]{2,1,0:T(1,128)S(1)}, u32[]{:S(2)}, u32[]{:S(2)}) async-start(f32[32,1,1024]{2,1,0:T(1,128)} %get-tuple-element.162), calls=%async_computation.16 | async-start | bytes 262144 | tf_op jit(solution)/shard_map/all_to_all | solution.py:1340
  465.3 1.2 collective-permute-start.7
  467.4 13.7 %all-to-all-start.17 = ((f32[16,1,3840]{2,1,0:T(1,128)}), f32[16,1,3840]{2,1,0:T(1,128)S(1)}, u32[]{:S(2)}, u32[]{:S(2)}) async-start(f32[16,1,3840]{2,1,0:T(1,128)} %broadcast_in_dim.50), calls=%async_computation.18 | async-start | bytes 491520 | tf_op jit(solution)/shard_map/all_to_all | solution.py:1333
  471.1 63.4 %reduce-scatter.8.cloned.1.call-start = ((), (), s32[]{:S(2)}) async-start(), calls=%async_computation.28 | async-start | bytes 491520 | tf_op jit(solution)/shard_map/reduce_scatter | solution.py:1822
  471.7 66.9 %reduce-scatter.10.cloned.1.call-start = ((), (), s32[]{:S(2)}) async-start(), calls=%async_computation.29 | async-start | bytes 2359296 | tf_op jit(solution)/shard_map/reduce_scatter | solution.py:1839
  481.2 8.7 %collective-permute-start.8 = (f32[3840]{0:T(1024)S(1)}, f32[3840]{0:T(1024)S(1)}, u32[]{:S(2)}, u32[]{:S(2)}) collective-permute-start(f32[3840]{0:T(1024)S(1)} %reduce_sum.468), channel_id=1, source_target_pairs={{0,1},{1,0},{2,3},{3,2},{4,5},{5,4},{6,7},{7,6},{8,9},{9,8},{10,11... | collective-permute-start | bytes 46088 | tf_op jit(solution)/shard_map/ppermute | solution.py:1334
  511.3 23.0 %all-to-all-start.18 = ((f32[32,1,1024]{2,1,0:T(1,128)}), f32[32,1,1024]{2,1,0:T(1,128)S(1)}, u32[]{:S(2)}, u32[]{:S(2)}) async-start(f32[32,1,1024]{2,1,0:T(1,128)} %get-tuple-element.173), calls=%async_computation.19 | async-start | bytes 262144 | tf_op jit(solution)/shard_map/all_to_all | solution.py:1340
  514.0 92.6 %reduce-scatter.12.cloned.1.call-start = ((), (), s32[]{:S(2)}) async-start(), calls=%async_computation.30 | async-start | bytes 7077888 | tf_op jit(solution)/shard_map/reduce_scatter | solution.py:1881
  561.5 4.7 collective-permute-start.9
  568.9 35.6 %collective-permute-start.10 = (bf16[2,4,144,512]{3,2,1,0:T(8,128)(2,1)S(1)}, bf16[2,4,144,512]{3,2,1,0:T(8,128)(2,1)}, u32[]{:S(2)}, u32[]{:S(2)}) collective-permute-start(bf16[2,4,144,512]{3,2,1,0:T(8,128)(2,1)S(1)} %dynamic-slice_bitcast_fusion.1), channel_id=1, source_target_pairs={{0,8},{8,0},{16,24},{24,16},{1,9},{9,1},{17,25},{25,17},{2,10},{10... | collective-permute-start | bytes 3538952 | tf_op jit(solution)/shard_map/ppermute | solution.py:1393
  570.7 24.6 %copy-start = (bf16[49,32,512]{2,1,0:T(8,128)(2,1)S(1)}, bf16[49,32,512]{2,1,0:T(8,128)(2,1)}, u32[]{:S(2)}) copy-start(bf16[49,32,512]{2,1,0:T(8,128)(2,1)} %get-tuple-element.121.refs_0_.refs_10_) | copy-start | bytes 4816900
  570.7 24.6 %copy-start.5 = (bf16[49,32,32]{2,1,0:T(8,128)(2,1)S(1)}, bf16[49,32,32]{2,1,0:T(8,128)(2,1)}, u32[]{:S(2)}) copy-start(bf16[49,32,32]{2,1,0:T(8,128)(2,1)} %get-tuple-element.194) | copy-start | bytes 301060
  590.0 13.2 %all-to-all-start.19 = ((f32[32,1,1024]{2,1,0:T(1,128)}), f32[32,1,1024]{2,1,0:T(1,128)S(1)}, u32[]{:S(2)}, u32[]{:S(2)}) async-start(f32[32,1,1024]{2,1,0:T(1,128)} %get-tuple-element.184), calls=%async_computation.21 | async-start | bytes 262144 | tf_op jit(solution)/shard_map/all_to_all | solution.py:1340
  594.8 82.5 %reduce-scatter.14.cloned.1.call-start = ((), (), s32[]{:S(2)}) async-start(), calls=%async_computation.31 | async-start | bytes 1310720 | tf_op jit(solution)/shard_map/reduce_scatter | solution.py:1908
  606.6 28.4 %collective-permute-start.11 = (bf16[1,4,144,512]{3,2,1,0:T(8,128)(2,1)S(1)}, bf16[1,4,144,512]{3,2,1,0:T(8,128)(2,1)S(1)}, u32[]{:S(2)}, u32[]{:S(2)}) collective-permute-start(bf16[1,4,144,512]{3,2,1,0:T(8,128)(2,1)S(1)} %constant_dynamic-slice_fusion), channel_id=1, source_target_pairs={{0,16},{8,24},{16,0},{24,8},{1,17},{9,25},{17,1},{25,9},{2,18},{10... | collective-permute-start | bytes 1769480 | tf_op jit(solution)/shard_map/ppermute | solution.py:1393
  623.8 11.4 %copy-start.2 = (bf16[1024,512]{1,0:T(8,128)(2,1)S(1)}, bf16[1024,512]{1,0:T(8,128)(2,1)}, u32[]{:S(2)}) copy-start(bf16[1024,512]{1,0:T(8,128)(2,1)} %get-tuple-element.193) | copy-start | bytes 3145732
  623.8 12.6 %copy-start.3 = (bf16[768,512]{1,0:T(8,128)(2,1)S(1)}, bf16[768,512]{1,0:T(8,128)(2,1)}, u32[]{:S(2)}) copy-start(bf16[768,512]{1,0:T(8,128)(2,1)} %reduce-scatter.12.cloned.1.call-done) | copy-start | bytes 2359300
  623.8 12.6 %copy-start.9 = (bf16[256,512]{1,0:T(8,128)(2,1)S(1)}, bf16[256,512]{1,0:T(8,128)(2,1)}, u32[]{:S(2)}) copy-start(bf16[256,512]{1,0:T(8,128)(2,1)} %reduce-scatter.10.cloned.1.call-done) | copy-start | bytes 786436
  636.2 2.0 collective-permute-start.12
  639.9 19.9 %all-to-all-start.20 = ((bf16[4,280,512]{2,1,0:T(8,128)(2,1)}), bf16[4,280,512]{2,1,0:T(8,128)(2,1)S(1)}, u32[]{:S(2)}, u32[]{:S(2)}) async-start(bf16[4,280,512]{2,1,0:T(8,128)(2,1)} %pad_maximum_fusion), calls=%async_computation.24 | async-start | bytes 2293760 | tf_op jit(solution)/shard_map/all_to_all | solution.py:1399
  660.8 20.4 %all-to-all-start.21 = ((bf16[4,34,512]{2,1,0:T(8,128)(2,1)}), bf16[4,34,512]{2,1,0:T(8,128)(2,1)S(1)}, u32[]{:S(2)}, u32[]{:S(2)}) async-start(bf16[4,34,512]{2,1,0:T(8,128)(2,1)} %reshape.592), calls=%async_computation.25 | async-start | bytes 327680 | tf_op jit(solution)/shard_map/all_to_all | solution.py:1404
  (44 other events, 283.1 us)
Sparse Core Ops, SparseCore 0:
  11.5 93.3 all-gather.5
  107.8 68.4 all-gather.7
  414.2 47.9 reduce-scatter.5
  474.0 21.8 reduce-scatter.7
  499.1 39.4 reduce-scatter.9
  542.1 63.1 reduce-scatter.11
  637.6 26.2 reduce-scatter.13
